TPU v7x, 256 devices: a whole 4x4x8 slice. The times are simulated.
256 devices in a mesh: slab: 64 (over y, z, core), band: 4 (over x).
Axes of the slice: x: 4, y: 4, z: 8, core: 2. Of those that a mesh axis runs over, the one named last changes fastest.
Arguments:
- wavefunctions: bfloat16 [8, 2, 256, 256, 256], P('band', None, 'slab'), may hold values from -6 to 6
- potential: float32 [256, 256, 256], P('slab', 'band'), may hold values from -0.6 to 0.6
- atom_box: int32 [3, 2048], P(None, 'slab'), may hold values from 0 to 255, as said below
- atom_count: int32 [64], P('slab'), may hold values from 8 to 32, as said below
- projectors: bfloat16 [2048, 8, 1728], P('slab'), may hold values from -0.59765625 to 0.59765625
- coupling: float32 [8, 8], replicated, may hold values from -2 to 2
Outputs:
- applied: bfloat16 [8, 2, 256, 256, 256], P('band', None, 'slab')
Inputs may be any that keep to these rules, and one draw needn't show every extreme that they name: `atom_box`: atoms are laid out by owner slab, 32 slots each; row 0 of an atom's column lies among the 4 z planes of its owner slab; rows 1 and 2 are any y and x cells; boxes wrap around the periodic grid. `atom_count`: slots at and beyond the count are not live; the slabs around one defect position are full.
All inputs are finite; a program needn't handle non-finite values.
Results may differ from a plain program's by a relative error of at most 0.011.
Values may be sent and summed in bfloat16 or wider, within the bound.
No kernel may reach another device: no remote copies, remote signals or barrier semaphores. Data moves between devices by JAX's collectives and lax.ppermute only.
A program may use at most 256 MiB of HBM per device.

v0:
```python
import math

import jax
import jax.numpy as jnp
from jax import lax
from jax.sharding import PartitionSpec as P

BOX = 12


def from_behind(block, axis, distance):
    devices = range(lax.axis_size(axis))
    route = [((i - distance) % len(devices), i) for i in devices]
    return lax.ppermute(block, axis, route)


def dft_table(length, sign):
    counter = jnp.arange(length, dtype=jnp.int32)
    product = counter[:, None] * counter[None, :] % length
    angle = product.astype(jnp.float32) * (2.0 * math.pi / length)
    cosine = jnp.cos(angle) / math.sqrt(length)
    sine = sign * jnp.sin(angle) / math.sqrt(length)
    return jnp.stack([jnp.stack([cosine, sine]), jnp.stack([-sine, cosine])]).astype(jnp.bfloat16)


def frequency_square(counter, length):
    signed = jnp.where(counter < length // 2, counter, counter - length)
    return (signed * signed).astype(jnp.float32)


def wrap_pad(field, edge):
    field = jnp.concatenate([field, field[:, :, :, : edge - 1]], axis=3)
    return jnp.concatenate([field, field[:, :, :, :, : edge - 1]], axis=4)


def fold_wrap(total, length, edge):
    spill = total[:, :, :, length:]
    total = total[:, :, :, :length] + jnp.pad(
        spill, ((0, 0), (0, 0), (0, 0), (0, length - edge + 1), (0, 0))
    )
    spill = total[:, :, :, :, length:]
    return total[:, :, :, :, :length] + jnp.pad(
        spill, ((0, 0), (0, 0), (0, 0), (0, 0), (0, length - edge + 1))
    )


def pick_boxes(padded, starts, edge):
    band_count = padded.shape[0]
    parts = padded.shape[1]

    def one_box(start):
        return lax.dynamic_slice(
            padded, (0, 0, start[0], start[1], start[2]), (band_count, parts, edge, edge, edge)
        )

    taken = jax.vmap(one_box)(starts)
    return taken.reshape(starts.shape[0], band_count, parts, edge * edge * edge)


def add_boxes(total, weights, coefficients, starts, edge):
    contrib = jnp.einsum("apn,apbc->abcn", weights, coefficients, precision=lax.Precision.HIGHEST)
    contrib = contrib.reshape(
        contrib.shape[0], contrib.shape[1], contrib.shape[2], edge, edge, edge
    )
    numbers = lax.ScatterDimensionNumbers(
        update_window_dims=(1, 2, 3, 4, 5),
        inserted_window_dims=(),
        scatter_dims_to_operand_dims=(2, 3, 4),
    )
    return lax.scatter_add(total, starts, contrib, numbers)


def shards(wavefunctions, potential, atom_box, atom_count, projectors, coupling):
    highest = lax.Precision.HIGHEST
    band_count = wavefunctions.shape[0]
    plane_count = wavefunctions.shape[2]
    length = wavefunctions.shape[3]
    slot_count = projectors.shape[0]
    forward = dft_table(length, 1.0)
    inverse = dft_table(length, -1.0)
    potential_full = lax.all_gather(
        potential.astype(jnp.bfloat16), "band", axis=1, tiled=True
    ).astype(potential.dtype)
    along_x = jnp.einsum(
        "ackn,bczyn->bazyk", forward, wavefunctions, preferred_element_type=jnp.float32
    ).astype(jnp.bfloat16)
    along_xy = jnp.einsum(
        "ackn,bczns->bazks", forward, along_x, preferred_element_type=jnp.float32
    ).astype(jnp.bfloat16)
    counter = jnp.arange(length, dtype=jnp.int32)
    inverse_norm = 1.0 / (3.0 * (length // 2) ** 2)
    row_count = length // lax.axis_size("slab")
    row_global = lax.axis_index("slab") * row_count + jnp.arange(row_count, dtype=jnp.int32)
    factor = (
        frequency_square(counter, length)[:, None, None]
        + frequency_square(row_global, length)[None, :, None]
        + frequency_square(counter, length)[None, None, :]
    ) * inverse_norm
    spectral = jnp.einsum(
        "ackn,bcnys->bakys",
        forward,
        lax.all_to_all(along_xy, "slab", split_axis=3, concat_axis=2, tiled=True),
        preferred_element_type=jnp.float32,
    )
    spectral = (spectral * factor).astype(jnp.bfloat16)
    back_z = lax.all_to_all(
        jnp.einsum(
            "ackn,bcnys->bakys", inverse, spectral, preferred_element_type=jnp.float32
        ).astype(jnp.bfloat16),
        "slab",
        split_axis=2,
        concat_axis=3,
        tiled=True,
    )
    back_zy = jnp.einsum(
        "ackn,bczns->bazks", inverse, back_z, preferred_element_type=jnp.float32
    ).astype(jnp.bfloat16)
    kinetic = jnp.einsum("ackn,bczyn->bazyk", inverse, back_zy, preferred_element_type=jnp.float32)
    slab_anchor = lax.axis_index("slab") * plane_count
    reach = (plane_count + BOX - 2) // plane_count
    extended = plane_count + BOX - 1
    padded_length = length + BOX - 1
    live = (jnp.arange(slot_count, dtype=jnp.int32) < atom_count[0]).astype(jnp.float32)
    symmetric = (coupling + coupling.T) * 0.5
    pieces = [wavefunctions]
    for distance in range(1, reach + 1):
        taken = min(plane_count, extended - distance * plane_count)
        pieces.append(from_behind(wavefunctions[:, :, :taken], "slab", -distance))
    wave_extended = wrap_pad(jnp.concatenate(pieces, axis=2), BOX)
    starts = jnp.stack([atom_box[0] - slab_anchor, atom_box[1], atom_box[2]], axis=1)
    boxes = pick_boxes(wave_extended, starts, BOX)
    projections = jnp.einsum(
        "apn,abcn->apbc", projectors, boxes, preferred_element_type=jnp.float32
    )
    coefficients = live[:, None, None, None] * jnp.einsum(
        "pq,aqbc->apbc", symmetric, projections, precision=highest
    )
    total = jnp.zeros((band_count, 2, extended, padded_length, padded_length), jnp.float32)
    total = add_boxes(total, projectors.astype(jnp.float32), coefficients, starts, BOX)
    total = fold_wrap(total, length, BOX)
    local_part = total[:, :, :plane_count]
    for distance in range(1, reach + 1):
        taken = min(plane_count, extended - distance * plane_count)
        lower = distance * plane_count
        arrived = from_behind(total[:, :, lower : lower + taken], "slab", distance)
        local_part = local_part + jnp.pad(
            arrived, ((0, 0), (0, 0), (0, plane_count - taken), (0, 0), (0, 0))
        )
    applied = kinetic + potential_full[None, None] * wavefunctions.astype(jnp.float32) + local_part
    return applied.astype(jnp.bfloat16)


def solution(mesh):
    placed = (
        P("band", None, "slab", None, None),
        P("slab", "band", None),
        P(None, "slab"),
        P("slab"),
        P("slab", None, None),
        P(),
    )
    return jax.shard_map(
        shards,
        mesh=mesh,
        in_specs=placed,
        out_specs=P("band", None, "slab", None, None),
        check_vma=False,
    )
```

profile of v0, /device:TPU:38, one launch (start us, length us, event | category | flops | bytes accessed | tf_op | source)
XLA Modules:
  0.0 1523.5 jit_solution(5861208143456452930)
XLA Ops:
  0.0 7.8 collective-permute-start.1
  15.4 5.0 fusion.12
  20.4 6.3 copy.25
  26.7 5.9 all-to-all-start
  37.6 8.7 collective-permute-done
  48.1 54.7 %collective-permute-done.1 = bf16[2,2,4,256,256]{4,3,2,1,0:T(8,128)(2,1)} collective-permute-done((bf16[2,2,4,256,256]{4,3,2,1,0:T(8,128)(2,1)}, bf16[2,2,4,256,256]{4,3,2,1,0:T(8,128)(2,1)}, u32[]{:S(2)}, u32[]{:S(2)}) %collective-permute-start.1) | collective-permute-done | bytes 2097184 | tf_op jit(solution)/shard_map/ppermute | solution.py:14
  104.6 22.4 %collective-permute-done.2 = bf16[2,2,3,256,256]{4,3,2,1,0:T(8,128)(2,1)} collective-permute-done((bf16[2,2,3,256,256]{4,3,2,1,0:T(8,128)(2,1)}, bf16[2,2,3,256,256]{4,3,2,1,0:T(8,128)(2,1)}, u32[]{:S(2)}, u32[]{:S(2)}) %collective-permute-start.2) | collective-permute-done | bytes 1572896 | tf_op jit(solution)/shard_map/ppermute | solution.py:14
  128.6 5.4 fusion
  134.0 144.0 %while.2 = (s32[]{:T(128)}, bf16[2,2,15,267,267]{4,3,2,1,0:T(8,128)(2,1)}, s32[32,5]{0,1:T(8,128)S(1)}, bf16[32,2,2,12,12,12]{5,4,3,2,1,0:T(8,128)(2,1)}, s32[]{:T(128)}) while((s32[]{:T(128)}, bf16[2,2,15,267,267]{4,3,2,1,0:T(8,128)(2,1)}, s32[32,5]{0,1:T(8,128)S(1)}, bf16[32,2,2,12,12,12]{5,4,3,2,1,0:T(8,128)(2,1)}, s32[]{:T(128)}) %tuple.48), condition=%wide.while_cond, body=%wide.while_body.sunk | while | flops 2 | bytes 395393 | solution.py:52
  278.1 10.8 copy.35
  295.5 4.1 copy.40
  299.6 14.1 copy.41
  313.8 11.2 broadcast_in_dim.2.clone
  325.0 812.1 %while.3 = (s32[]{:T(128)}, f32[2,2,15,267,267]{4,3,1,2,0:T(8,128)}, s32[32,3]{0,1:T(4,128)S(1)}, f32[32,2,2,12,12,12]{5,4,3,2,1,0:T(8,128)}, s32[]{:T(128)}, /*index=5*/s32[5]{0:T(128)S(1)}, s32[1]{0:T(128)}, s32[]{:T(128)}) while((s32[]{:T(128)}, f32[2,2,15,267,267]{4,3,1,2,0:T(8,128)}, s32[32,3]{0,1:T(4,128)S(1)}, ...), condition=%wide.while_cond.1, body=%wide.while_body.1.sunk | while | flops 13845 | bytes 927454 | solution.py:70
  328.1 4.0 add_select_fusion.3
  332.1 18.2 %dynamic-update-slice.16 = f32[2,2,15,267,267]{4,3,1,2,0:T(8,128)} dynamic-update-slice(f32[2,2,15,267,267]{4,3,1,2,0:T(8,128)} %get-tuple-element.155, f32[2,2,12,12,12]{4,3,1,2,0:T(8,128)S(1)} %copy.100, s32[]{:T(128)} %constant.20.clone.1..sunk, s32[]{:T(128)} %constant.20.clone.1..sunk, s32[]{:T(128)} %bitcast.180, s32[]{:T(128)} %bitcast.181, s32[]{:T(128)} %bitcast.182) | dynamic-update-slice | bytes 55300 | tf_op jit(solution)/shard_map/scatter-add
  353.5 4.0 add_select_fusion.3
  357.6 18.2 %dynamic-update-slice.16 = f32[2,2,15,267,267]{4,3,1,2,0:T(8,128)} dynamic-update-slice(f32[2,2,15,267,267]{4,3,1,2,0:T(8,128)} %get-tuple-element.155, f32[2,2,12,12,12]{4,3,1,2,0:T(8,128)S(1)} %copy.100, s32[]{:T(128)} %constant.20.clone.1..sunk, s32[]{:T(128)} %constant.20.clone.1..sunk, s32[]{:T(128)} %bitcast.180, s32[]{:T(128)} %bitcast.181, s32[]{:T(128)} %bitcast.182) | dynamic-update-slice | bytes 55300 | tf_op jit(solution)/shard_map/scatter-add
  378.9 4.0 add_select_fusion.3
  383.0 18.2 %dynamic-update-slice.16 = f32[2,2,15,267,267]{4,3,1,2,0:T(8,128)} dynamic-update-slice(f32[2,2,15,267,267]{4,3,1,2,0:T(8,128)} %get-tuple-element.155, f32[2,2,12,12,12]{4,3,1,2,0:T(8,128)S(1)} %copy.100, s32[]{:T(128)} %constant.20.clone.1..sunk, s32[]{:T(128)} %constant.20.clone.1..sunk, s32[]{:T(128)} %bitcast.180, s32[]{:T(128)} %bitcast.181, s32[]{:T(128)} %bitcast.182) | dynamic-update-slice | bytes 55300 | tf_op jit(solution)/shard_map/scatter-add
  404.3 4.0 add_select_fusion.3
  408.3 18.2 %dynamic-update-slice.16 = f32[2,2,15,267,267]{4,3,1,2,0:T(8,128)} dynamic-update-slice(f32[2,2,15,267,267]{4,3,1,2,0:T(8,128)} %get-tuple-element.155, f32[2,2,12,12,12]{4,3,1,2,0:T(8,128)S(1)} %copy.100, s32[]{:T(128)} %constant.20.clone.1..sunk, s32[]{:T(128)} %constant.20.clone.1..sunk, s32[]{:T(128)} %bitcast.180, s32[]{:T(128)} %bitcast.181, s32[]{:T(128)} %bitcast.182) | dynamic-update-slice | bytes 55300 | tf_op jit(solution)/shard_map/scatter-add
  433.7 18.2 %dynamic-update-slice.16 = f32[2,2,15,267,267]{4,3,1,2,0:T(8,128)} dynamic-update-slice(f32[2,2,15,267,267]{4,3,1,2,0:T(8,128)} %get-tuple-element.155, f32[2,2,12,12,12]{4,3,1,2,0:T(8,128)S(1)} %copy.100, s32[]{:T(128)} %constant.20.clone.1..sunk, s32[]{:T(128)} %constant.20.clone.1..sunk, s32[]{:T(128)} %bitcast.180, s32[]{:T(128)} %bitcast.181, s32[]{:T(128)} %bitcast.182) | dynamic-update-slice | bytes 55300 | tf_op jit(solution)/shard_map/scatter-add
  459.1 18.2 %dynamic-update-slice.16 = f32[2,2,15,267,267]{4,3,1,2,0:T(8,128)} dynamic-update-slice(f32[2,2,15,267,267]{4,3,1,2,0:T(8,128)} %get-tuple-element.155, f32[2,2,12,12,12]{4,3,1,2,0:T(8,128)S(1)} %copy.100, s32[]{:T(128)} %constant.20.clone.1..sunk, s32[]{:T(128)} %constant.20.clone.1..sunk, s32[]{:T(128)} %bitcast.180, s32[]{:T(128)} %bitcast.181, s32[]{:T(128)} %bitcast.182) | dynamic-update-slice | bytes 55300 | tf_op jit(solution)/shard_map/scatter-add
  480.5 4.0 add_select_fusion.3
  484.5 18.2 %dynamic-update-slice.16 = f32[2,2,15,267,267]{4,3,1,2,0:T(8,128)} dynamic-update-slice(f32[2,2,15,267,267]{4,3,1,2,0:T(8,128)} %get-tuple-element.155, f32[2,2,12,12,12]{4,3,1,2,0:T(8,128)S(1)} %copy.100, s32[]{:T(128)} %constant.20.clone.1..sunk, s32[]{:T(128)} %constant.20.clone.1..sunk, s32[]{:T(128)} %bitcast.180, s32[]{:T(128)} %bitcast.181, s32[]{:T(128)} %bitcast.182) | dynamic-update-slice | bytes 55300 | tf_op jit(solution)/shard_map/scatter-add
  509.9 18.2 %dynamic-update-slice.16 = f32[2,2,15,267,267]{4,3,1,2,0:T(8,128)} dynamic-update-slice(f32[2,2,15,267,267]{4,3,1,2,0:T(8,128)} %get-tuple-element.155, f32[2,2,12,12,12]{4,3,1,2,0:T(8,128)S(1)} %copy.100, s32[]{:T(128)} %constant.20.clone.1..sunk, s32[]{:T(128)} %constant.20.clone.1..sunk, s32[]{:T(128)} %bitcast.180, s32[]{:T(128)} %bitcast.181, s32[]{:T(128)} %bitcast.182) | dynamic-update-slice | bytes 55300 | tf_op jit(solution)/shard_map/scatter-add
  531.2 4.0 add_select_fusion.3
  535.3 18.2 %dynamic-update-slice.16 = f32[2,2,15,267,267]{4,3,1,2,0:T(8,128)} dynamic-update-slice(f32[2,2,15,267,267]{4,3,1,2,0:T(8,128)} %get-tuple-element.155, f32[2,2,12,12,12]{4,3,1,2,0:T(8,128)S(1)} %copy.100, s32[]{:T(128)} %constant.20.clone.1..sunk, s32[]{:T(128)} %constant.20.clone.1..sunk, s32[]{:T(128)} %bitcast.180, s32[]{:T(128)} %bitcast.181, s32[]{:T(128)} %bitcast.182) | dynamic-update-slice | bytes 55300 | tf_op jit(solution)/shard_map/scatter-add
  560.7 18.2 %dynamic-update-slice.16 = f32[2,2,15,267,267]{4,3,1,2,0:T(8,128)} dynamic-update-slice(f32[2,2,15,267,267]{4,3,1,2,0:T(8,128)} %get-tuple-element.155, f32[2,2,12,12,12]{4,3,1,2,0:T(8,128)S(1)} %copy.100, s32[]{:T(128)} %constant.20.clone.1..sunk, s32[]{:T(128)} %constant.20.clone.1..sunk, s32[]{:T(128)} %bitcast.180, s32[]{:T(128)} %bitcast.181, s32[]{:T(128)} %bitcast.182) | dynamic-update-slice | bytes 55300 | tf_op jit(solution)/shard_map/scatter-add
  582.0 4.0 add_select_fusion.3
  586.0 18.2 %dynamic-update-slice.16 = f32[2,2,15,267,267]{4,3,1,2,0:T(8,128)} dynamic-update-slice(f32[2,2,15,267,267]{4,3,1,2,0:T(8,128)} %get-tuple-element.155, f32[2,2,12,12,12]{4,3,1,2,0:T(8,128)S(1)} %copy.100, s32[]{:T(128)} %constant.20.clone.1..sunk, s32[]{:T(128)} %constant.20.clone.1..sunk, s32[]{:T(128)} %bitcast.180, s32[]{:T(128)} %bitcast.181, s32[]{:T(128)} %bitcast.182) | dynamic-update-slice | bytes 55300 | tf_op jit(solution)/shard_map/scatter-add
  611.4 18.2 %dynamic-update-slice.16 = f32[2,2,15,267,267]{4,3,1,2,0:T(8,128)} dynamic-update-slice(f32[2,2,15,267,267]{4,3,1,2,0:T(8,128)} %get-tuple-element.155, f32[2,2,12,12,12]{4,3,1,2,0:T(8,128)S(1)} %copy.100, s32[]{:T(128)} %constant.20.clone.1..sunk, s32[]{:T(128)} %constant.20.clone.1..sunk, s32[]{:T(128)} %bitcast.180, s32[]{:T(128)} %bitcast.181, s32[]{:T(128)} %bitcast.182) | dynamic-update-slice | bytes 55300 | tf_op jit(solution)/shard_map/scatter-add
  636.8 18.2 %dynamic-update-slice.16 = f32[2,2,15,267,267]{4,3,1,2,0:T(8,128)} dynamic-update-slice(f32[2,2,15,267,267]{4,3,1,2,0:T(8,128)} %get-tuple-element.155, f32[2,2,12,12,12]{4,3,1,2,0:T(8,128)S(1)} %copy.100, s32[]{:T(128)} %constant.20.clone.1..sunk, s32[]{:T(128)} %constant.20.clone.1..sunk, s32[]{:T(128)} %bitcast.180, s32[]{:T(128)} %bitcast.181, s32[]{:T(128)} %bitcast.182) | dynamic-update-slice | bytes 55300 | tf_op jit(solution)/shard_map/scatter-add
  662.2 18.2 %dynamic-update-slice.16 = f32[2,2,15,267,267]{4,3,1,2,0:T(8,128)} dynamic-update-slice(f32[2,2,15,267,267]{4,3,1,2,0:T(8,128)} %get-tuple-element.155, f32[2,2,12,12,12]{4,3,1,2,0:T(8,128)S(1)} %copy.100, s32[]{:T(128)} %constant.20.clone.1..sunk, s32[]{:T(128)} %constant.20.clone.1..sunk, s32[]{:T(128)} %bitcast.180, s32[]{:T(128)} %bitcast.181, s32[]{:T(128)} %bitcast.182) | dynamic-update-slice | bytes 55300 | tf_op jit(solution)/shard_map/scatter-add
  687.6 18.3 %dynamic-update-slice.16 = f32[2,2,15,267,267]{4,3,1,2,0:T(8,128)} dynamic-update-slice(f32[2,2,15,267,267]{4,3,1,2,0:T(8,128)} %get-tuple-element.155, f32[2,2,12,12,12]{4,3,1,2,0:T(8,128)S(1)} %copy.100, s32[]{:T(128)} %constant.20.clone.1..sunk, s32[]{:T(128)} %constant.20.clone.1..sunk, s32[]{:T(128)} %bitcast.180, s32[]{:T(128)} %bitcast.181, s32[]{:T(128)} %bitcast.182) | dynamic-update-slice | bytes 55300 | tf_op jit(solution)/shard_map/scatter-add
  713.0 18.2 %dynamic-update-slice.16 = f32[2,2,15,267,267]{4,3,1,2,0:T(8,128)} dynamic-update-slice(f32[2,2,15,267,267]{4,3,1,2,0:T(8,128)} %get-tuple-element.155, f32[2,2,12,12,12]{4,3,1,2,0:T(8,128)S(1)} %copy.100, s32[]{:T(128)} %constant.20.clone.1..sunk, s32[]{:T(128)} %constant.20.clone.1..sunk, s32[]{:T(128)} %bitcast.180, s32[]{:T(128)} %bitcast.181, s32[]{:T(128)} %bitcast.182) | dynamic-update-slice | bytes 55300 | tf_op jit(solution)/shard_map/scatter-add
  738.4 18.2 %dynamic-update-slice.16 = f32[2,2,15,267,267]{4,3,1,2,0:T(8,128)} dynamic-update-slice(f32[2,2,15,267,267]{4,3,1,2,0:T(8,128)} %get-tuple-element.155, f32[2,2,12,12,12]{4,3,1,2,0:T(8,128)S(1)} %copy.100, s32[]{:T(128)} %constant.20.clone.1..sunk, s32[]{:T(128)} %constant.20.clone.1..sunk, s32[]{:T(128)} %bitcast.180, s32[]{:T(128)} %bitcast.181, s32[]{:T(128)} %bitcast.182) | dynamic-update-slice | bytes 55300 | tf_op jit(solution)/shard_map/scatter-add
  763.7 18.2 %dynamic-update-slice.16 = f32[2,2,15,267,267]{4,3,1,2,0:T(8,128)} dynamic-update-slice(f32[2,2,15,267,267]{4,3,1,2,0:T(8,128)} %get-tuple-element.155, f32[2,2,12,12,12]{4,3,1,2,0:T(8,128)S(1)} %copy.100, s32[]{:T(128)} %constant.20.clone.1..sunk, s32[]{:T(128)} %constant.20.clone.1..sunk, s32[]{:T(128)} %bitcast.180, s32[]{:T(128)} %bitcast.181, s32[]{:T(128)} %bitcast.182) | dynamic-update-slice | bytes 55300 | tf_op jit(solution)/shard_map/scatter-add
  789.1 18.2 %dynamic-update-slice.16 = f32[2,2,15,267,267]{4,3,1,2,0:T(8,128)} dynamic-update-slice(f32[2,2,15,267,267]{4,3,1,2,0:T(8,128)} %get-tuple-element.155, f32[2,2,12,12,12]{4,3,1,2,0:T(8,128)S(1)} %copy.100, s32[]{:T(128)} %constant.20.clone.1..sunk, s32[]{:T(128)} %constant.20.clone.1..sunk, s32[]{:T(128)} %bitcast.180, s32[]{:T(128)} %bitcast.181, s32[]{:T(128)} %bitcast.182) | dynamic-update-slice | bytes 55300 | tf_op jit(solution)/shard_map/scatter-add
  814.5 18.2 %dynamic-update-slice.16 = f32[2,2,15,267,267]{4,3,1,2,0:T(8,128)} dynamic-update-slice(f32[2,2,15,267,267]{4,3,1,2,0:T(8,128)} %get-tuple-element.155, f32[2,2,12,12,12]{4,3,1,2,0:T(8,128)S(1)} %copy.100, s32[]{:T(128)} %constant.20.clone.1..sunk, s32[]{:T(128)} %constant.20.clone.1..sunk, s32[]{:T(128)} %bitcast.180, s32[]{:T(128)} %bitcast.181, s32[]{:T(128)} %bitcast.182) | dynamic-update-slice | bytes 55300 | tf_op jit(solution)/shard_map/scatter-add
  839.9 18.1 %dynamic-update-slice.16 = f32[2,2,15,267,267]{4,3,1,2,0:T(8,128)} dynamic-update-slice(f32[2,2,15,267,267]{4,3,1,2,0:T(8,128)} %get-tuple-element.155, f32[2,2,12,12,12]{4,3,1,2,0:T(8,128)S(1)} %copy.100, s32[]{:T(128)} %constant.20.clone.1..sunk, s32[]{:T(128)} %constant.20.clone.1..sunk, s32[]{:T(128)} %bitcast.180, s32[]{:T(128)} %bitcast.181, s32[]{:T(128)} %bitcast.182) | dynamic-update-slice | bytes 55300 | tf_op jit(solution)/shard_map/scatter-add
  865.2 18.2 %dynamic-update-slice.16 = f32[2,2,15,267,267]{4,3,1,2,0:T(8,128)} dynamic-update-slice(f32[2,2,15,267,267]{4,3,1,2,0:T(8,128)} %get-tuple-element.155, f32[2,2,12,12,12]{4,3,1,2,0:T(8,128)S(1)} %copy.100, s32[]{:T(128)} %constant.20.clone.1..sunk, s32[]{:T(128)} %constant.20.clone.1..sunk, s32[]{:T(128)} %bitcast.180, s32[]{:T(128)} %bitcast.181, s32[]{:T(128)} %bitcast.182) | dynamic-update-slice | bytes 55300 | tf_op jit(solution)/shard_map/scatter-add
  890.6 18.2 %dynamic-update-slice.16 = f32[2,2,15,267,267]{4,3,1,2,0:T(8,128)} dynamic-update-slice(f32[2,2,15,267,267]{4,3,1,2,0:T(8,128)} %get-tuple-element.155, f32[2,2,12,12,12]{4,3,1,2,0:T(8,128)S(1)} %copy.100, s32[]{:T(128)} %constant.20.clone.1..sunk, s32[]{:T(128)} %constant.20.clone.1..sunk, s32[]{:T(128)} %bitcast.180, s32[]{:T(128)} %bitcast.181, s32[]{:T(128)} %bitcast.182) | dynamic-update-slice | bytes 55300 | tf_op jit(solution)/shard_map/scatter-add
  915.9 18.2 %dynamic-update-slice.16 = f32[2,2,15,267,267]{4,3,1,2,0:T(8,128)} dynamic-update-slice(f32[2,2,15,267,267]{4,3,1,2,0:T(8,128)} %get-tuple-element.155, f32[2,2,12,12,12]{4,3,1,2,0:T(8,128)S(1)} %copy.100, s32[]{:T(128)} %constant.20.clone.1..sunk, s32[]{:T(128)} %constant.20.clone.1..sunk, s32[]{:T(128)} %bitcast.180, s32[]{:T(128)} %bitcast.181, s32[]{:T(128)} %bitcast.182) | dynamic-update-slice | bytes 55300 | tf_op jit(solution)/shard_map/scatter-add
  941.3 18.2 %dynamic-update-slice.16 = f32[2,2,15,267,267]{4,3,1,2,0:T(8,128)} dynamic-update-slice(f32[2,2,15,267,267]{4,3,1,2,0:T(8,128)} %get-tuple-element.155, f32[2,2,12,12,12]{4,3,1,2,0:T(8,128)S(1)} %copy.100, s32[]{:T(128)} %constant.20.clone.1..sunk, s32[]{:T(128)} %constant.20.clone.1..sunk, s32[]{:T(128)} %bitcast.180, s32[]{:T(128)} %bitcast.181, s32[]{:T(128)} %bitcast.182) | dynamic-update-slice | bytes 55300 | tf_op jit(solution)/shard_map/scatter-add
  966.7 18.2 %dynamic-update-slice.16 = f32[2,2,15,267,267]{4,3,1,2,0:T(8,128)} dynamic-update-slice(f32[2,2,15,267,267]{4,3,1,2,0:T(8,128)} %get-tuple-element.155, f32[2,2,12,12,12]{4,3,1,2,0:T(8,128)S(1)} %copy.100, s32[]{:T(128)} %constant.20.clone.1..sunk, s32[]{:T(128)} %constant.20.clone.1..sunk, s32[]{:T(128)} %bitcast.180, s32[]{:T(128)} %bitcast.181, s32[]{:T(128)} %bitcast.182) | dynamic-update-slice | bytes 55300 | tf_op jit(solution)/shard_map/scatter-add
  992.1 18.2 %dynamic-update-slice.16 = f32[2,2,15,267,267]{4,3,1,2,0:T(8,128)} dynamic-update-slice(f32[2,2,15,267,267]{4,3,1,2,0:T(8,128)} %get-tuple-element.155, f32[2,2,12,12,12]{4,3,1,2,0:T(8,128)S(1)} %copy.100, s32[]{:T(128)} %constant.20.clone.1..sunk, s32[]{:T(128)} %constant.20.clone.1..sunk, s32[]{:T(128)} %bitcast.180, s32[]{:T(128)} %bitcast.181, s32[]{:T(128)} %bitcast.182) | dynamic-update-slice | bytes 55300 | tf_op jit(solution)/shard_map/scatter-add
  1017.5 18.2 %dynamic-update-slice.16 = f32[2,2,15,267,267]{4,3,1,2,0:T(8,128)} dynamic-update-slice(f32[2,2,15,267,267]{4,3,1,2,0:T(8,128)} %get-tuple-element.155, f32[2,2,12,12,12]{4,3,1,2,0:T(8,128)S(1)} %copy.100, s32[]{:T(128)} %constant.20.clone.1..sunk, s32[]{:T(128)} %constant.20.clone.1..sunk, s32[]{:T(128)} %bitcast.180, s32[]{:T(128)} %bitcast.181, s32[]{:T(128)} %bitcast.182) | dynamic-update-slice | bytes 55300 | tf_op jit(solution)/shard_map/scatter-add
  1042.9 18.2 %dynamic-update-slice.16 = f32[2,2,15,267,267]{4,3,1,2,0:T(8,128)} dynamic-update-slice(f32[2,2,15,267,267]{4,3,1,2,0:T(8,128)} %get-tuple-element.155, f32[2,2,12,12,12]{4,3,1,2,0:T(8,128)S(1)} %copy.100, s32[]{:T(128)} %constant.20.clone.1..sunk, s32[]{:T(128)} %constant.20.clone.1..sunk, s32[]{:T(128)} %bitcast.180, s32[]{:T(128)} %bitcast.181, s32[]{:T(128)} %bitcast.182) | dynamic-update-slice | bytes 55300 | tf_op jit(solution)/shard_map/scatter-add
  1068.2 18.2 %dynamic-update-slice.16 = f32[2,2,15,267,267]{4,3,1,2,0:T(8,128)} dynamic-update-slice(f32[2,2,15,267,267]{4,3,1,2,0:T(8,128)} %get-tuple-element.155, f32[2,2,12,12,12]{4,3,1,2,0:T(8,128)S(1)} %copy.100, s32[]{:T(128)} %constant.20.clone.1..sunk, s32[]{:T(128)} %constant.20.clone.1..sunk, s32[]{:T(128)} %bitcast.180, s32[]{:T(128)} %bitcast.181, s32[]{:T(128)} %bitcast.182) | dynamic-update-slice | bytes 55300 | tf_op jit(solution)/shard_map/scatter-add
  1093.6 18.2 %dynamic-update-slice.16 = f32[2,2,15,267,267]{4,3,1,2,0:T(8,128)} dynamic-update-slice(f32[2,2,15,267,267]{4,3,1,2,0:T(8,128)} %get-tuple-element.155, f32[2,2,12,12,12]{4,3,1,2,0:T(8,128)S(1)} %copy.100, s32[]{:T(128)} %constant.20.clone.1..sunk, s32[]{:T(128)} %constant.20.clone.1..sunk, s32[]{:T(128)} %bitcast.180, s32[]{:T(128)} %bitcast.181, s32[]{:T(128)} %bitcast.182) | dynamic-update-slice | bytes 55300 | tf_op jit(solution)/shard_map/scatter-add
  1118.9 18.2 %dynamic-update-slice.16 = f32[2,2,15,267,267]{4,3,1,2,0:T(8,128)} dynamic-update-slice(f32[2,2,15,267,267]{4,3,1,2,0:T(8,128)} %get-tuple-element.155, f32[2,2,12,12,12]{4,3,1,2,0:T(8,128)S(1)} %copy.100, s32[]{:T(128)} %constant.20.clone.1..sunk, s32[]{:T(128)} %constant.20.clone.1..sunk, s32[]{:T(128)} %bitcast.180, s32[]{:T(128)} %bitcast.181, s32[]{:T(128)} %bitcast.182) | dynamic-update-slice | bytes 55300 | tf_op jit(solution)/shard_map/scatter-add
  1138.6 9.2 pad_add_fusion
  1151.6 9.5 slice_add_fusion
  1161.1 7.6 fusion.63
  1171.7 24.7 %collective-permute-start.4 = (f32[2,2,4,256,256]{4,3,1,2,0:T(8,128)}, f32[2,2,4,256,256]{4,3,1,2,0:T(8,128)}, u32[]{:S(2)}, u32[]{:S(2)}) collective-permute-start(f32[2,2,4,256,256]{4,3,1,2,0:T(8,128)} %get-tuple-element.54), channel_id=1, source_target_pairs={{248,0},{252,4},{0,8},{4,12},{8,16},{12,20},{16,24},{20,28},{24,32... | collective-permute-start | bytes 12582920 | tf_op jit(solution)/shard_map/ppermute | solution.py:14
  1199.9 5.0 fusion.15
  1204.9 6.2 copy.29
  1211.1 27.5 %all-to-all-start.1 = ((bf16[2,2,256,4,256]{4,1,3,0,2:T(2,128)(2,1)}), bf16[2,2,256,4,256]{4,1,3,0,2:T(2,128)(2,1)}, u32[]{:S(2)}, u32[]{:S(2)}) async-start(bf16[2,2,256,4,256]{4,1,3,0,2:T(2,128)(2,1)} %copy.29), calls=%async_computation.1 | async-start | bytes 4194304 | tf_op jit(solution)/shard_map/all_to_all | solution.py:106
  1243.6 13.5 all_gather.3
  1258.2 199.8 %all-to-all-done.1 = bf16[2,2,256,4,256]{4,1,3,0,2:T(2,128)(2,1)} async-done(((bf16[2,2,256,4,256]{4,1,3,0,2:T(2,128)(2,1)}), bf16[2,2,256,4,256]{4,1,3,0,2:T(2,128)(2,1)}, u32[]{:S(2)}, u32[]{:S(2)}) %all-to-all-start.1) | async-done | bytes 2097184 | tf_op jit(solution)/shard_map/all_to_all | solution.py:106
  1462.7 47.7 %collective-permute-done.5 = f32[2,2,3,256,256]{4,3,1,2,0:T(8,128)} collective-permute-done((f32[2,2,3,256,256]{4,3,1,2,0:T(8,128)}, f32[2,2,3,256,256]{4,3,1,2,0:T(8,128)}, u32[]{:S(2)}, u32[]{:S(2)}) %collective-permute-start.5) | collective-permute-done | bytes 3145760 | tf_op jit(solution)/shard_map/ppermute | solution.py:14
  1510.5 10.0 fusion.4
  (352 shorter events, 394.5 us)
Async XLA Ops:
  0.0 292.1 %copy-start = (bf16[32,8,1728]{2,1,0:T(8,128)(2,1)S(1)}, bf16[32,8,1728]{2,1,0:T(8,128)(2,1)}, u32[]{:S(2)}) copy-start(bf16[32,8,1728]{2,1,0:T(8,128)(2,1)} %param.10) | copy-start | bytes 2654212
  0.0 15.4 %copy-start.2 = (bf16[2,2,4,256,256]{4,3,2,1,0:T(8,128)(2,1)S(1)}, bf16[2,2,4,256,256]{4,3,2,1,0:T(8,128)(2,1)}, u32[]{:S(2)}) copy-start(bf16[2,2,4,256,256]{4,3,2,1,0:T(8,128)(2,1)} %param.6) | copy-start | bytes 6291460
  0.0 46.4 %collective-permute-start = (bf16[2,2,4,256,256]{4,3,2,1,0:T(8,128)(2,1)}, bf16[2,2,4,256,256]{4,3,2,1,0:T(8,128)(2,1)}, u32[]{:S(2)}, u32[]{:S(2)}) collective-permute-start(bf16[2,2,4,256,256]{4,3,2,1,0:T(8,128)(2,1)} %param.6), channel_id=1, source_target_pairs={{4,0},{8,4},{12,8},{16,12},{20,16},{24,20},{28,24},{32,28},{36,32}... | collective-permute-start | bytes 6291464 | tf_op jit(solution)/shard_map/ppermute | solution.py:14
  0.0 102.8 %collective-permute-start.1 = (bf16[2,2,4,256,256]{4,3,2,1,0:T(8,128)(2,1)}, bf16[2,2,4,256,256]{4,3,2,1,0:T(8,128)(2,1)}, u32[]{:S(2)}, u32[]{:S(2)}) collective-permute-start(bf16[2,2,4,256,256]{4,3,2,1,0:T(8,128)(2,1)} %param.6), channel_id=1, source_target_pairs={{8,0},{12,4},{16,8},{20,12},{24,16},{28,20},{32,24},{36,28},{40,32... | collective-permute-start | bytes 6291464 | tf_op jit(solution)/shard_map/ppermute | solution.py:14
  10.6 116.4 %collective-permute-start.2 = (bf16[2,2,3,256,256]{4,3,2,1,0:T(8,128)(2,1)}, bf16[2,2,3,256,256]{4,3,2,1,0:T(8,128)(2,1)}, u32[]{:S(2)}, u32[]{:S(2)}) collective-permute-start(bf16[2,2,3,256,256]{4,3,2,1,0:T(8,128)(2,1)} %slice.45), channel_id=1, source_target_pairs={{12,0},{16,4},{20,8},{24,12},{28,16},{32,20},{36,24},{40,28},{44,3... | collective-permute-start | bytes 4718600 | tf_op jit(solution)/shard_map/ppermute | solution.py:14
  20.4 13.4 copy-start.8
  20.4 15.0 copy-start.7
  26.7 1169.7 %all-to-all-start = ((bf16[2,2,4,256,256]{4,1,2,0,3:T(2,128)(2,1)}), bf16[2,2,4,256,256]{4,1,2,0,3:T(2,128)(2,1)}, u32[]{:S(2)}, u32[]{:S(2)}) async-start(bf16[2,2,4,256,256]{4,1,2,0,3:T(2,128)(2,1)} %copy.25), calls=%async_computation | async-start | bytes 4194304 | tf_op jit(solution)/shard_map/all_to_all | solution.py:102
  35.5 0.8 copy-start.10
  35.5 0.9 copy-start.11
  288.9 4.9 copy-start.9
  313.8 11.2 copy-start.12
  1168.8 341.7 %collective-permute-start.3 = (f32[2,2,4,256,256]{4,3,1,2,0:T(8,128)}, f32[2,2,4,256,256]{4,3,1,2,0:T(8,128)}, u32[]{:S(2)}, u32[]{:S(2)}) collective-permute-start(f32[2,2,4,256,256]{4,3,1,2,0:T(8,128)} %get-tuple-element.53), channel_id=1, source_target_pairs={{252,0},{0,4},{4,8},{8,12},{12,16},{16,20},{20,24},{24,28},{28,32}... | collective-permute-start | bytes 12582920 | tf_op jit(solution)/shard_map/ppermute | solution.py:14
  1171.7 28.2 %copy-start.5 = (bf16[1,2,256,256]{3,2,1,0:T(8,128)(2,1)S(1)}, bf16[1,2,256,256]{3,2,1,0:T(8,128)(2,1)}, u32[]{:S(2)}) copy-start(bf16[1,2,256,256]{3,2,1,0:T(8,128)(2,1)} %get-tuple-element.57) | copy-start | bytes 786436
  1171.7 28.2 %copy-start.6 = (bf16[1,2,256,256]{3,2,1,0:T(8,128)(2,1)S(1)}, bf16[1,2,256,256]{3,2,1,0:T(8,128)(2,1)}, u32[]{:S(2)}) copy-start(bf16[1,2,256,256]{3,2,1,0:T(8,128)(2,1)} %get-tuple-element.58) | copy-start | bytes 786436
  1171.7 338.8 %collective-permute-start.4 = (f32[2,2,4,256,256]{4,3,1,2,0:T(8,128)}, f32[2,2,4,256,256]{4,3,1,2,0:T(8,128)}, u32[]{:S(2)}, u32[]{:S(2)}) collective-permute-start(f32[2,2,4,256,256]{4,3,1,2,0:T(8,128)} %get-tuple-element.54), channel_id=1, source_target_pairs={{248,0},{252,4},{0,8},{4,12},{8,16},{12,20},{16,24},{20,28},{24,32... | collective-permute-start | bytes 12582920 | tf_op jit(solution)/shard_map/ppermute | solution.py:14
  1211.1 246.8 %all-to-all-start.1 = ((bf16[2,2,256,4,256]{4,1,3,0,2:T(2,128)(2,1)}), bf16[2,2,256,4,256]{4,1,3,0,2:T(2,128)(2,1)}, u32[]{:S(2)}, u32[]{:S(2)}) async-start(bf16[2,2,256,4,256]{4,1,3,0,2:T(2,128)(2,1)} %copy.29), calls=%async_computation.1 | async-start | bytes 4194304 | tf_op jit(solution)/shard_map/all_to_all | solution.py:106
  1238.6 5.0 copy-start.4
  1242.4 268.1 %collective-permute-start.5 = (f32[2,2,3,256,256]{4,3,1,2,0:T(8,128)}, f32[2,2,3,256,256]{4,3,1,2,0:T(8,128)}, u32[]{:S(2)}, u32[]{:S(2)}) collective-permute-start(f32[2,2,3,256,256]{4,3,1,2,0:T(8,128)} %slice.109), channel_id=1, source_target_pairs={{244,0},{248,4},{252,8},{0,12},{4,16},{8,20},{12,24},{16,28},{20,3... | collective-permute-start | bytes 9437192 | tf_op jit(solution)/shard_map/ppermute | solution.py:14
  1258.2 252.3 %copy-start.3 = (bf16[2,2,4,256,256]{4,3,2,1,0:T(8,128)(2,1)S(1)}, bf16[2,2,4,256,256]{4,3,2,1,0:T(8,128)(2,1)}, u32[]{:S(2)}) copy-start(bf16[2,2,4,256,256]{4,3,2,1,0:T(8,128)(2,1)} %param.6) | copy-start | bytes 6291460
  1510.5 13.1 copy-start.1
where the time goes:
time: 1530 us; the launch traced here: 1520 us
  local copies, waits for them, and re-layouts  901 us (59%)
  waiting for transfers between devices  333 us (22%)
  other arithmetic  180 us (12%)
  starting transfers between devices  71 us (5%)
  matrix products  23.2 us (2%)
    scatter-add x160, local copies, waits for them, and re-layouts  664 us
    all_to_all x1, waiting for transfers between devices, shards(): lax.all_to_all(jnp.einsum('ackn,bcnys->bakys', inverse, spectral, preferr...  200 us
    scatter-add x64, other arithmetic  148 us
    gather x96, local copies, waits for them, and re-layouts  144 us
    ppermute x6, waiting for transfers between devices, from_behind(): return lax.ppermute(block, axis, route)  134 us
    ppermute x6, starting transfers between devices, from_behind(): return lax.ppermute(block, axis, route)  37.6 us
  transfers between devices with their start and end apart: 8, of which 5 were waited for; matrix products, arithmetic and copies ran while one was open for 72% of the time, Pallas kernels for 0%

commit v1 on v0

v1 whole, which is shorter than its diff:
```python
import numpy as np

import jax
import jax.numpy as jnp
from jax import lax
from jax.experimental import pallas as pl
from jax.experimental.pallas import tpu as pltpu
from jax.sharding import PartitionSpec as P

BOX = 12
PAD = 16
LANES = 128
HEAP = LANES // PAD
F32 = jnp.float32
BF16 = jnp.bfloat16
HIGHEST = lax.Precision.HIGHEST
VMEM_LIMIT = 56 * 1024 * 1024
NT = (((1,), (1,)), ((), ()))
TN = (((0,), (0,)), ((), ()))


def kinetic_table(length):
    counter = np.arange(length)
    signed = np.where(counter < length // 2, counter, counter - length).astype(np.float64)
    angle = 2.0 * np.pi * ((counter[:, None] * counter[None, :]) % length) / length
    spectrum = signed**2 / (3.0 * (length // 2) ** 2)
    row = (np.cos(angle) * spectrum[None, :]).sum(1) / length
    table = row[(counter[:, None] - counter[None, :]) % length]
    high = jnp.asarray(table, F32).astype(BF16)
    low = (jnp.asarray(table, F32) - high.astype(F32)).astype(BF16)
    return high, low


def whole(space=pltpu.VMEM):
    return pl.BlockSpec(memory_space=space)


def dot(a, b, dims=None, precision=None):
    if dims is None:
        dims = (((1,), (0,)), ((), ()))
    return lax.dot_general(a, b, dims, precision=precision, preferred_element_type=F32)


def along_z_kernel(high_ref, low_ref, in_ref, out_ref, wide, result):
    length = high_ref.shape[0]
    stride = in_ref.shape[0] // length
    wide[...] = in_ref[...].astype(F32)

    def step(i, carry):
        left = wide[pl.ds(2 * i, length, stride=stride), :]
        right = wide[pl.ds(2 * i + 1, length, stride=stride), :]
        both = jnp.concatenate([left, right], axis=1).astype(BF16)
        out = dot(high_ref[...], both) + dot(low_ref[...], both)
        result[pl.ds(2 * i, length, stride=stride), :] = out[:, :LANES]
        result[pl.ds(2 * i + 1, length, stride=stride), :] = out[:, LANES:]
        return carry

    lax.fori_loop(0, stride // 2, step, 0)
    out_ref[...] = result[...].astype(BF16)


def along_z(high, low, block):
    rows = block.shape[0]
    return pl.pallas_call(
        along_z_kernel,
        out_shape=jax.ShapeDtypeStruct(block.shape, BF16),
        in_specs=[whole()] * 3,
        out_specs=whole(),
        scratch_shapes=[pltpu.VMEM((rows, LANES), F32), pltpu.VMEM((rows, LANES), F32)],
        compiler_params=pltpu.CompilerParams(vmem_limit_bytes=VMEM_LIMIT),
        cost_estimate=pl.CostEstimate(
            flops=4 * 256 * rows * LANES, bytes_accessed=4 * rows * LANES, transcendentals=0
        ),
        name="along_z",
    )(high, low, block)


def select_matrix(xt_ref, group, length):
    column = lax.broadcasted_iota(jnp.int32, (length, LANES), 0)
    return jnp.where(column == xt_ref[pl.ds(group, 1), :], 1.0, 0.0).astype(BF16)


def heap_matrix():
    lane = lax.broadcasted_iota(jnp.int32, (HEAP, LANES), 1)
    atom = lax.broadcasted_iota(jnp.int32, (HEAP, LANES), 0)
    return jnp.where(lane // PAD == atom, 1.0, 0.0).astype(F32)


def project_kernel(y_ref, xt_ref, wave_ref, weight_ref, out_ref, field, sums):
    reach, heaps, nproj = weight_ref.shape[1], weight_ref.shape[0], weight_ref.shape[2]
    planes, length = wave_ref.shape[0], wave_ref.shape[1]
    rows = weight_ref.shape[3]
    parts = planes * PAD // rows
    for i in range(planes):
        for half in range(2):
            part = wave_ref[i, :, half * LANES : (half + 1) * LANES].astype(F32)
            field[i, half, 0:length, :] = part
            field[i, half, length : length + PAD, :] = part[0:PAD]
    lane = lax.broadcasted_iota(jnp.int32, (planes * PAD, LANES), 1)

    def step(index, carry):
        reach_index = index // heaps
        heap = index % heaps
        select = select_matrix(xt_ref, index, length)
        taken = jnp.zeros((planes * PAD, LANES), F32)
        for a in range(HEAP):
            y0 = y_ref[index * HEAP + a]
            left = field[:, 0, pl.ds(y0, PAD), :].reshape(planes * PAD, LANES)
            right = field[:, 1, pl.ds(y0, PAD), :].reshape(planes * PAD, LANES)
            window = jnp.concatenate([left, right], axis=1).astype(BF16)
            taken = jnp.where(lane // PAD == a, dot(window, select), taken)
        lines = []
        for p in range(nproj):
            weight = weight_ref[heap, reach_index, p].astype(F32)
            for part in range(parts):
                product = weight * taken[part * rows : (part + 1) * rows]
                lines.append(jnp.sum(product, axis=0, keepdims=True))
        sums[pl.ds(pl.multiple_of(index * nproj * parts, 8), nproj * parts), :] = jnp.concatenate(lines, axis=0)
        return carry

    lax.fori_loop(0, reach * heaps, step, 0)
    per_reach = heaps * nproj * parts
    for d in range(reach):
        out_ref[d] = dot(
            heap_matrix(), sums[d * per_reach : (d + 1) * per_reach, :], NT, HIGHEST
        )


def project(y0, xt, wave, weights):
    heaps, reach, nproj, rows, _ = weights.shape
    planes, length, _ = wave.shape
    parts = planes * PAD // rows
    return pl.pallas_call(
        project_kernel,
        out_shape=jax.ShapeDtypeStruct((reach, HEAP, heaps * nproj * parts), F32),
        in_specs=[whole(pltpu.SMEM), whole(), whole(), whole()],
        out_specs=whole(),
        scratch_shapes=[
            pltpu.VMEM((planes, 2, length + PAD, LANES), F32),
            pltpu.VMEM((reach * heaps * nproj * parts, LANES), F32),
        ],
        compiler_params=pltpu.CompilerParams(vmem_limit_bytes=VMEM_LIMIT),
        cost_estimate=pl.CostEstimate(
            flops=10_000_000_000, bytes_accessed=5_000_000, transcendentals=0
        ),
        name="project",
    )(y0, xt, wave, weights)


def local_kernel(
    y_ref, xt_ref, full_ref, live_ref, mix_ref, high_ref, low_ref, potential_ref,
    wave_ref, weight_ref, out_ref, total, spread,
):
    heaps, reach, nproj, rows, _ = weight_ref.shape
    planes, length = wave_ref.shape[0], wave_ref.shape[1]
    slab_planes = potential_ref.shape[0]
    parts = planes // slab_planes
    per_reach = heaps * nproj * parts

    def fill(i, carry):
        wave = wave_ref[i]
        value = dot(wave, high_ref[...]) + dot(wave, low_ref[...])
        value += dot(high_ref[...], wave) + dot(low_ref[...], wave)
        value += potential_ref[lax.rem(i, slab_planes)].astype(F32) * wave.astype(F32)
        for half in range(2):
            total[i, half, 0:length, :] = value[:, half * LANES : (half + 1) * LANES]
            total[i, half, length : length + PAD, :] = jnp.zeros((PAD, LANES), F32)
        return carry

    lax.fori_loop(0, planes, fill, 0)
    for d in range(reach):
        coefficients = dot(full_ref[d] * live_ref[d], mix_ref[...], None, HIGHEST)
        spread[d * per_reach : (d + 1) * per_reach, :] = dot(
            coefficients, heap_matrix(), TN, HIGHEST
        )
    lane = lax.broadcasted_iota(jnp.int32, (planes * PAD, LANES), 1)

    def step(index, carry):
        reach_index = index // heaps
        heap = index % heaps
        select = select_matrix(xt_ref, index, length)
        lines = spread[pl.ds(pl.multiple_of(index * nproj * parts, 8), nproj * parts), :]
        blocks = [jnp.zeros((rows, LANES), F32) for _ in range(parts)]
        for p in range(nproj):
            weight = weight_ref[heap, reach_index, p].astype(F32)
            for part in range(parts):
                at = p * parts + part
                blocks[part] = blocks[part] + weight * lines[at : at + 1, :]
        blocks = jnp.concatenate(blocks, axis=0)
        for a in range(HEAP):
            y0 = y_ref[index * HEAP + a]
            one = jnp.where(lane // PAD == a, blocks, 0.0).astype(BF16)
            placed = dot(one, select, NT)
            for half in range(2):
                part = placed[:, half * LANES : (half + 1) * LANES]
                total[:, half, pl.ds(y0, PAD), :] += part.reshape(planes, PAD, LANES)
        return carry

    lax.fori_loop(0, reach * heaps, step, 0)

    def finish(i, carry):
        for half in range(2):
            at = slice(half * LANES, (half + 1) * LANES)
            out_ref[i, 0:PAD, at] = total[i, half, 0:PAD, :] + total[i, half, length : length + PAD, :]
            out_ref[i, PAD:length, at] = total[i, half, PAD:length, :]
        return carry

    lax.fori_loop(0, planes, finish, 0)


def local_part(y0, xt, full, live, mix, high, low, potential, wave, weights):
    heaps, reach, nproj, rows, _ = weights.shape
    planes, length, _ = wave.shape
    parts = planes * PAD // rows
    return pl.pallas_call(
        local_kernel,
        out_shape=jax.ShapeDtypeStruct(wave.shape, F32),
        in_specs=[whole(pltpu.SMEM)] + [whole()] * 9,
        out_specs=whole(),
        scratch_shapes=[
            pltpu.VMEM((planes, 2, length + PAD, LANES), F32),
            pltpu.VMEM((reach * heaps * nproj * parts, LANES), F32),
        ],
        compiler_params=pltpu.CompilerParams(vmem_limit_bytes=VMEM_LIMIT),
        cost_estimate=pl.CostEstimate(
            flops=10_000_000_000, bytes_accessed=10_000_000, transcendentals=0
        ),
        name="local",
    )(y0, xt, full, live, mix, high, low, potential, wave, weights)


def join_kernel(local_ref, arrived_ref, out_ref):
    bands, rows, columns = arrived_ref.shape[0], arrived_ref.shape[1], arrived_ref.shape[2]
    slab_planes, comps = arrived_ref.shape[3], arrived_ref.shape[4]
    for b in range(bands):
        for c in range(comps):
            for z in range(slab_planes):
                plane = (b * comps + c) * slab_planes + z
                for r in range(rows):
                    for h in range(columns):
                        at = (plane, slice(r * 16, (r + 1) * 16), slice(h * LANES, (h + 1) * LANES))
                        value = local_ref[at] + arrived_ref[b, r, h, z, c].astype(F32)
                        out_ref[at] = value.astype(BF16)


def join(local, arrived):
    bands, row_blocks, halves, slab_planes, comps = arrived.shape[:5]
    planes, length, _ = local.shape
    count = 8
    step_rows = row_blocks // count
    return pl.pallas_call(
        join_kernel,
        out_shape=jax.ShapeDtypeStruct(local.shape, BF16),
        grid=(count,),
        in_specs=[
            pl.BlockSpec((planes, length // count, length), lambda i: (0, i, 0)),
            pl.BlockSpec(
                (bands, step_rows, halves, slab_planes, comps, 16, LANES),
                lambda i: (0, i, 0, 0, 0, 0, 0),
            ),
        ],
        out_specs=pl.BlockSpec((planes, length // count, length), lambda i: (0, i, 0)),
        compiler_params=pltpu.CompilerParams(vmem_limit_bytes=VMEM_LIMIT),
        cost_estimate=pl.CostEstimate(
            flops=2 * local.size, bytes_accessed=8 * local.size, transcendentals=0
        ),
        name="join",
    )(local, arrived)


def ahead(block, distance):
    size = lax.axis_size("slab")
    return lax.ppermute(block, "slab", [(i, (i + distance) % size) for i in range(size)])


def framed_weights(projectors, atom_box, slab_anchor, slab_planes):
    nproj = projectors.shape[1]
    mine = lax.axis_index("band") * HEAP
    share = lax.dynamic_slice_in_dim(projectors, mine, HEAP, 0)
    share = share.reshape(HEAP, nproj, BOX, BOX, BOX).transpose(1, 2, 3, 0, 4)
    share = jnp.pad(share, ((0, 0), (0, 0), (0, PAD - BOX), (0, 0), (0, PAD - BOX)))
    share = share.reshape(nproj, BOX, PAD, LANES)
    offset = lax.dynamic_slice_in_dim(atom_box[0], mine, HEAP, 0) - slab_anchor
    offset = jnp.repeat(offset, PAD)
    frames = BOX + slab_planes
    framed = jnp.zeros((nproj, frames, PAD, LANES), projectors.dtype)
    for o in range(slab_planes):
        moved = jnp.pad(share, ((0, 0), (o, slab_planes - o), (0, 0), (0, 0)))
        framed = jnp.where(offset == o, moved, framed)
    reach = frames // slab_planes
    framed = framed.reshape(nproj, reach, slab_planes * PAD, LANES)
    return framed.transpose(1, 0, 2, 3)


def shards(wavefunctions, potential, atom_box, atom_count, projectors, coupling):
    bands, comps, slab_planes, length, _ = wavefunctions.shape
    parts = bands * comps
    planes = parts * slab_planes
    slabs = lax.axis_size("slab")
    slots, nproj, _ = projectors.shape
    heaps = slots // HEAP
    reach = (BOX + slab_planes) // slab_planes
    high, low = kinetic_table(length)
    slab_anchor = lax.axis_index("slab") * slab_planes

    row_blocks, halves = length // 16, length // LANES
    send = wavefunctions.reshape(bands, comps, slab_planes, row_blocks, 16, halves, LANES)
    send = send.transpose(0, 3, 5, 2, 1, 4, 6).reshape(slabs, slab_planes * comps, 16, LANES)
    columns = lax.all_to_all(send, "slab", split_axis=0, concat_axis=0, tiled=True)

    framed = framed_weights(projectors, atom_box, slab_anchor, slab_planes)
    weights = jnp.stack([framed[0]] + [ahead(framed[d], d) for d in range(1, reach)])
    weights = lax.all_gather(weights, "band", axis=0)
    facts = jnp.concatenate([atom_box[1], atom_box[2], atom_count, jnp.zeros((LANES - 2 * slots - 1,), jnp.int32)])
    facts = jnp.stack([facts] + [ahead(facts, d) for d in range(1, reach)])
    y0 = facts[:, :slots].reshape(-1)
    x0 = facts[:, slots : 2 * slots]
    count = facts[:, 2 * slots]
    k = jnp.arange(PAD, dtype=jnp.int32)
    xt = jnp.where(k < BOX, (x0[:, :, None] + k) % length, -1).reshape(reach * heaps, LANES)

    wave = wavefunctions.reshape(planes, length, length)
    partial = project(y0, xt, wave, weights)
    full = partial
    for o in range(1, reach):
        up = ahead(partial[o:], -o)
        down = ahead(partial[: reach - o], o)
        full = full + jnp.pad(up, ((0, o), (0, 0), (0, 0)))
        full = full + jnp.pad(down, ((o, 0), (0, 0), (0, 0)))

    slot = jnp.arange(heaps)[None, :] * HEAP + jnp.arange(HEAP)[:, None]
    live = (slot[None] < count[:, None, None]).astype(F32)
    live = jnp.repeat(live, nproj * parts, axis=2)
    symmetric = (coupling + coupling.T) * 0.5
    mix = jnp.einsum(
        "gh,pq,bc->gqbhpc", jnp.eye(heaps, dtype=F32), symmetric, jnp.eye(parts, dtype=F32),
        precision=HIGHEST,
    ).reshape(heaps * nproj * parts, heaps * nproj * parts)
    potential_full = lax.all_gather(potential.astype(BF16), "band", axis=1, tiled=True)
    local = local_part(y0, xt, full, live, mix, high, low, potential_full, wave, weights)

    columns = along_z(high, low, columns.reshape(-1, LANES))
    columns = columns.reshape(slabs, slab_planes * comps, 16, LANES)
    back = lax.all_to_all(columns, "slab", split_axis=0, concat_axis=0, tiled=True)
    back = back.reshape(bands, row_blocks, halves, slab_planes, comps, 16, LANES)
    return join(local, back).reshape(wavefunctions.shape)


def solution(mesh):
    placed = (
        P("band", None, "slab", None, None),
        P("slab", "band", None),
        P(None, "slab"),
        P("slab"),
        P("slab", None, None),
        P(),
    )
    return jax.shard_map(
        shards,
        mesh=mesh,
        in_specs=placed,
        out_specs=P("band", None, "slab", None, None),
        check_vma=False,
    )
```

time: 1530 us -> 199 us (0.13)
  the two profiles are of different devices: /device:TPU:38 before, /device:TPU:1 now
where the time goes in v1:
time: 199 us; the launch traced here: 198 us
  Pallas kernels  48.2 us (24%)
  waiting for transfers between devices  45.7 us (23%)
  starting transfers between devices  44.2 us (22%)
  local copies, waits for them, and re-layouts  28.8 us (14%)
  between operations  14.3 us (7%)
  blocking collectives  11.9 us (6%)
  other arithmetic  4.99 us (3%)
    ppermute x12, waiting for transfers between devices, ahead(): lax.ppermute(block, 'slab', [(i, (i + distance) % size) for i in range(si...  45.7 us
    ppermute x12, starting transfers between devices, ahead(): lax.ppermute(block, 'slab', [(i, (i + distance) % size) for i in range(si...  21 us
    pallas_call x1, Pallas kernels, local_part(): pl.pallas_call(local_kernel, out_shape=jax.ShapeDtypeStruct(wave.shape, F...  19.1 us
    all_to_all x1, starting transfers between devices, shards(): lax.all_to_all(send, 'slab', split_axis=0, concat_axis=0, tiled=True)  13.3 us
    all_gather x1, blocking collectives, shards(): lax.all_gather(potential.astype(BF16), 'band', axis=1, tiled=True)  11.9 us
    pallas_call x1, Pallas kernels, project(): pl.pallas_call(project_kernel, out_shape=jax.ShapeDtypeStruct((reach, HEA...  11.7 us
    pallas_call x1, Pallas kernels, along_z(): pl.pallas_call(along_z_kernel, out_shape=jax.ShapeDtypeStruct(block.shape...  10.9 us
    all_to_all x1, starting transfers between devices, shards(): lax.all_to_all(columns, 'slab', split_axis=0, concat_axis=0, tiled=True)  9.86 us
  transfers between devices with their start and end apart: 15, of which 5 were waited for; matrix products, arithmetic and copies ran while one was open for 14% of the time, Pallas kernels for 21%

profile of v1, /device:TPU:1, one launch (start us, length us, event | category | flops | bytes accessed | tf_op | source)
XLA Modules:
  0.0 198.0 jit_solution(10304295314667017944)
XLA Ops:
  6.5 2.6 %reshape.98 = bf16[2,2,4,16,16,2,128]{6,5,4,3,2,1,0:T(2,128)(2,1)S(1)} reshape(bf16[2,2,4,256,256]{4,3,2,1,0:T(8,128)(2,1)} %param.8) | data formatting | bytes 4194304 | tf_op jit(solution)/shard_map/reshape | solution.py:307
  9.2 1.9 copy.25
  11.1 13.3 %all-to-all-start = ((bf16[64,8,16,128]{3,2,1,0:T(8,128)(2,1)}), bf16[64,8,16,128]{3,2,1,0:T(8,128)(2,1)S(1)}, u32[]{:S(2)}, u32[]{:S(2)}) async-start(bf16[64,8,16,128]{3,2,1,0:T(8,128)(2,1)} %bitcast.57), calls=%async_computation | async-start | bytes 4194304 | tf_op jit(solution)/shard_map/all_to_all | solution.py:309
  24.4 0.0 all-gather.3.cloned.1.call-start
  24.4 0.1 compare_bitcast_fusion.3
  24.5 0.1 broadcast_in_dim.52
  24.6 0.1 eq.65
  24.7 0.1 broadcast_in_dim.54
  24.8 0.1 eq.69
  24.9 0.1 broadcast_in_dim.56
  24.9 0.1 eq.73
  25.0 0.1 broadcast_in_dim.50
  25.1 0.1 eq.61
  25.2 0.0 copy-done
  25.2 4.6 %reshape.93 = bf16[8,8,12,12,12]{4,3,2,1,0:T(8,128)(2,1)} reshape(bf16[8,8,1728]{2,1,0:T(8,128)(2,1)S(1)} %constant_dynamic-slice_fusion) | data formatting | bytes 442368 | tf_op jit(solution)/shard_map/reshape | solution.py:280
  29.8 4.7 %copy.29 = bf16[8,12,12,8,12]{4,3,2,1,0:T(8,128)(2,1)S(1)} copy(bf16[8,12,12,8,12]{4,2,1,0,3:T(8,128)(2,1)} %bitcast.55) | data formatting | bytes 442368
  34.5 2.4 %pad.44.clone = bf16[8,12,16,8,16]{4,3,2,1,0:T(8,128)(2,1)} pad(bf16[8,12,12,8,12]{4,3,2,1,0:T(8,128)(2,1)S(1)} %copy.29, bf16[]{:T(256)} %constant.49.clone.1), padding=0_0x0_0x0_4x0_0x0_4 | pad | bytes 614402 | tf_op jit(solution)/shard_map/jit(_pad)/pad | solution.py:281
  36.9 4.0 %reshape.94 = bf16[8,12,16,128]{3,2,1,0:T(8,128)(2,1)S(1)} reshape(bf16[8,12,16,8,16]{4,3,2,1,0:T(8,128)(2,1)} %pad.44.clone) | data formatting | bytes 786432 | tf_op jit(solution)/shard_map/reshape | solution.py:282
  40.9 0.0 copy-start.4
  40.9 0.1 select_select_fusion
  41.0 0.0 copy-start.3
  41.0 1.7 collective-permute-start.3
  42.7 1.2 collective-permute-start.4
  43.9 1.3 collective-permute-start.5
  45.2 26.4 %collective-permute-done.3 = bf16[8,64,128]{2,1,0:T(8,128)(2,1)S(1)} collective-permute-done((bf16[8,64,128]{2,1,0:T(8,128)(2,1)S(1)}, bf16[8,64,128]{2,1,0:T(8,128)(2,1)S(1)}, u32[]{:S(2)}, u32[]{:S(2)}) %collective-permute-start.3) | collective-permute-done | bytes 131104 | tf_op jit(solution)/shard_map/ppermute | solution.py:273
  71.7 8.6 %collective-permute-done.4 = bf16[8,64,128]{2,1,0:T(8,128)(2,1)S(1)} collective-permute-done((bf16[8,64,128]{2,1,0:T(8,128)(2,1)S(1)}, bf16[8,64,128]{2,1,0:T(8,128)(2,1)S(1)}, u32[]{:S(2)}, u32[]{:S(2)}) %collective-permute-start.4) | collective-permute-done | bytes 131104 | tf_op jit(solution)/shard_map/ppermute | solution.py:273
  80.2 1.3 collective-permute-done.5
  81.5 0.9 pad_maximum_fusion
  82.4 0.0 all-gather.3.cloned.1.call-update
  83.1 0.1 pad_add_fusion.2
  83.2 3.3 %collective-permute-start = (s32[128]{0:T(128)S(1)}, s32[128]{0:T(128)S(1)}, u32[]{:S(2)}, u32[]{:S(2)}) collective-permute-start(s32[128]{0:T(128)S(1)} %pad_add_fusion.2), channel_id=1, source_target_pairs={{0,4},{4,8},{8,12},{12,16},{16,20},{20,24},{24,28},{28,32},{32,36}... | collective-permute-start | bytes 1544 | tf_op jit(solution)/shard_map/ppermute | solution.py:273
  86.5 0.0 collective-permute-start.1
  86.5 0.0 collective-permute-start.2
  86.5 0.1 copy.23
  86.5 0.1 copy.24
  86.7 0.1 broadcast_multiply_fusion
  86.7 1.7 multiply_bitcast_fusion
  88.4 1.4 copy-done.1
  89.8 10.9 %along_z.1 = bf16[8192,128]{1,0:T(8,128)(2,1)} custom-call(bf16[256,256]{1,0:T(8,128)(2,1)} %constant.82.high_ref, bf16[256,256]{1,0:T(8,128)(2,1)} %constant.85.low_ref, bf16[8192,128]{1,0:T(8,128)(2,1)} %bitcast.56), custom_call_target="tpu_custom_call" | custom-call | flops 1073741824 | bytes 4194304 | tf_op jit(solution)/shard_map/along_z/pallas_call | solution.py:64
  100.7 9.9 %all-to-all-start.1 = ((bf16[64,8,16,128]{3,2,1,0:T(8,128)(2,1)}), bf16[64,8,16,128]{3,2,1,0:T(8,128)(2,1)}, u32[]{:S(2)}, u32[]{:S(2)}) async-start(bf16[64,8,16,128]{3,2,1,0:T(8,128)(2,1)} %bitcast.58), calls=%async_computation.1 | async-start | bytes 4194304 | tf_op jit(solution)/shard_map/all_to_all | solution.py:344
  110.5 11.9 %all_gather.11.potential_ref = bf16[4,256,256]{2,1,0:T(8,128)(2,1)} all-gather(bf16[4,64,256]{2,1,0:T(8,128)(2,1)S(1)} %convert_element_type.43), channel_id=1, replica_groups=mesh['slab'=64,'band'=4] {'band'}, dimensions={1}, use_global_device_ids=true | all-gather | bytes 655360 | tf_op jit(solution)/shard_map/all_gather | solution.py:339
  122.4 0.1 broadcast_in_dim.48
  122.5 2.3 %reshape.97.mix_ref = f32[128,128]{1,0:T(8,128)} reshape(f32[4,8,4,4,8,4]{5,4,3,2,1,0:T(8,128)S(1)} %copy-done.2) | data formatting | bytes 131072 | tf_op jit(solution)/shard_map/reshape | solution.py:338
  124.8 0.1 fusion.8
  124.9 0.1 iota_add_fusion
  125.0 0.1 add.91
  125.1 0.6 reshape.91.y_ref
  125.7 0.2 slice_reduce_fusion
  125.9 0.6 fusion.1.xt_ref
  126.5 11.7 %project.1 = f32[4,8,128]{2,1,0:T(8,128)} custom-call(s32[128]{0:T(128)} %reshape.91.y_ref, s32[16,128]{1,0:T(8,128)} %fusion.1.xt_ref, bf16[16,256,256]{2,1,0:T(8,128)(2,1)} %bitcast.61, bf16[4,4,8,64,128]{4,3,2,1,0:T(8,128)(2,1)} %bitcast.70), custom_call_target="tpu_custom_call" | custom-call | flops 10000000000 | bytes 5000000 | tf_op jit(solution)/shard_map/project/pallas_call | solution.py:133
  138.2 0.7 fusion.6
  138.9 7.2 %collective-permute-start.10 = (f32[1,8,128]{2,1,0:T(8,128)S(1)}, f32[1,8,128]{2,1,0:T(8,128)S(1)}, u32[]{:S(2)}, u32[]{:S(2)}) collective-permute-start(f32[1,8,128]{2,1,0:T(8,128)S(1)} %get-tuple-element.15), channel_id=1, source_target_pairs={{0,244},{4,248},{8,252},{12,0},{16,4},{20,8},{24,12},{28,16},{32,2... | collective-permute-start | bytes 12296 | tf_op jit(solution)/shard_map/ppermute | solution.py:273
  146.1 0.8 fusion.4
  146.9 0.7 fusion.5
  147.6 1.7 collective-permute-start.7
  149.4 4.5 %collective-permute-start.8 = (f32[2,8,128]{2,1,0:T(8,128)S(1)}, f32[2,8,128]{2,1,0:T(8,128)S(1)}, u32[]{:S(2)}, u32[]{:S(2)}) collective-permute-start(f32[2,8,128]{2,1,0:T(8,128)S(1)} %get-tuple-element.13), channel_id=1, source_target_pairs={{0,248},{4,252},{8,0},{12,4},{16,8},{20,12},{24,16},{28,20},{32,24... | collective-permute-start | bytes 24584 | tf_op jit(solution)/shard_map/ppermute | solution.py:273
  153.9 3.9 %collective-permute-done.10 = f32[1,8,128]{2,1,0:T(8,128)S(1)} collective-permute-done((f32[1,8,128]{2,1,0:T(8,128)S(1)}, f32[1,8,128]{2,1,0:T(8,128)S(1)}, u32[]{:S(2)}, u32[]{:S(2)}) %collective-permute-start.10) | collective-permute-done | bytes 4128 | tf_op jit(solution)/shard_map/ppermute | solution.py:273
  157.8 0.1 compare_convert_fusion
  157.9 0.1 broadcast_in_dim.59
  158.0 0.7 reshape.96.live_ref
  158.7 5.5 %collective-permute-done.11 = f32[1,8,128]{2,1,0:T(8,128)S(1)} collective-permute-done((f32[1,8,128]{2,1,0:T(8,128)S(1)}, f32[1,8,128]{2,1,0:T(8,128)S(1)}, u32[]{:S(2)}, u32[]{:S(2)}) %collective-permute-start.11) | collective-permute-done | bytes 4128 | tf_op jit(solution)/shard_map/ppermute | solution.py:273
  164.2 1.3 pad_add_fusion.full_ref
  165.5 19.1 %local.1.local_ref = f32[16,256,256]{2,1,0:T(8,128)} custom-call(s32[128]{0:T(128)} %reshape.91.y_ref, s32[16,128]{1,0:T(8,128)} %fusion.1.xt_ref, f32[4,8,128]{2,1,0:T(8,128)} %pad_add_fusion.full_ref, f32[4,8,128]{2,1,0:T(8,128)} %reshape.96.live_ref, f32[128,128]{1,0:T(8,128)} %reshape.97.mix_ref, bf16[256,256]{1,0:T(8,128)(2,1)} %constant.82.high_ref, ...), custom_call_target="tpu_custom_call" | custom-call | flops 10000000000 | bytes 10000000 | tf_op jit(solution)/shard_map/local/pallas_call | solution.py:215
  184.6 6.5 %join.1 = bf16[16,256,256]{2,1,0:T(8,128)(2,1)} custom-call(f32[16,256,256]{2,1,0:T(8,128)} %local.1.local_ref, bf16[2,16,2,4,2,16,128]{6,5,4,3,2,1,0:T(8,128)(2,1)} %bitcast.28.arrived_ref), custom_call_target="tpu_custom_call" | custom-call | flops 2097152 | bytes 8388608 | tf_op jit(solution)/shard_map/join/pallas_call | solution.py:251
  (34 shorter events, 0.2 us)
Async XLA Ops:
  6.5 18.7 %copy-start = (bf16[32,8,1728]{2,1,0:T(8,128)(2,1)S(1)}, bf16[32,8,1728]{2,1,0:T(8,128)(2,1)}, u32[]{:S(2)}) copy-start(bf16[32,8,1728]{2,1,0:T(8,128)(2,1)} %param.12) | copy-start | bytes 2654212
  11.1 13.4 %copy-start.5 = (s32[3,32]{1,0:T(4,128)S(1)}, s32[3,32]{1,0:T(4,128)}, u32[]{:S(2)}) copy-start(s32[3,32]{1,0:T(4,128)} %param.10) | copy-start | bytes 1156
  11.1 77.3 %all-to-all-start = ((bf16[64,8,16,128]{3,2,1,0:T(8,128)(2,1)}), bf16[64,8,16,128]{3,2,1,0:T(8,128)(2,1)S(1)}, u32[]{:S(2)}, u32[]{:S(2)}) async-start(bf16[64,8,16,128]{3,2,1,0:T(8,128)(2,1)} %bitcast.57), calls=%async_computation | async-start | bytes 4194304 | tf_op jit(solution)/shard_map/all_to_all | solution.py:309
  24.4 102.1 %all-gather.3.cloned.1.call-start = ((), (), s32[]{:S(2)}) async-start(), calls=%async_computation.2 | async-start | bytes 2621440 | tf_op jit(solution)/shard_map/all_gather | solution.py:313
  40.9 45.6 %copy-start.4 = (f32[8,8]{1,0:T(8,128)S(1)}, f32[8,8]{1,0:T(8,128)}, u32[]{:S(2)}) copy-start(f32[8,8]{1,0:T(8,128)} %param.13) | copy-start | bytes 772
  41.0 45.7 %copy-start.3 = (f32[4,64,256]{2,1,0:T(8,128)S(1)}, f32[4,64,256]{2,1,0:T(8,128)}, u32[]{:S(2)}) copy-start(f32[4,64,256]{2,1,0:T(8,128)} %param.9) | copy-start | bytes 786436
  41.0 30.6 %collective-permute-start.3 = (bf16[8,64,128]{2,1,0:T(8,128)(2,1)S(1)}, bf16[8,64,128]{2,1,0:T(8,128)(2,1)S(1)}, u32[]{:S(2)}, u32[]{:S(2)}) collective-permute-start(bf16[8,64,128]{2,1,0:T(8,128)(2,1)S(1)} %get-tuple-element.8), channel_id=1, source_target_pairs={{0,4},{4,8},{8,12},{12,16},{16,20},{20,24},{24,28},{28,32},{32,36}... | collective-permute-start | bytes 393224 | tf_op jit(solution)/shard_map/ppermute | solution.py:273
  42.7 37.5 %collective-permute-start.4 = (bf16[8,64,128]{2,1,0:T(8,128)(2,1)S(1)}, bf16[8,64,128]{2,1,0:T(8,128)(2,1)S(1)}, u32[]{:S(2)}, u32[]{:S(2)}) collective-permute-start(bf16[8,64,128]{2,1,0:T(8,128)(2,1)S(1)} %get-tuple-element.10), channel_id=1, source_target_pairs={{0,8},{4,12},{8,16},{12,20},{16,24},{20,28},{24,32},{28,36},{32,40... | collective-permute-start | bytes 393224 | tf_op jit(solution)/shard_map/ppermute | solution.py:273
  43.9 37.6 %collective-permute-start.5 = (bf16[8,64,128]{2,1,0:T(8,128)(2,1)S(1)}, bf16[8,64,128]{2,1,0:T(8,128)(2,1)S(1)}, u32[]{:S(2)}, u32[]{:S(2)}) collective-permute-start(bf16[8,64,128]{2,1,0:T(8,128)(2,1)S(1)} %get-tuple-element.9), channel_id=1, source_target_pairs={{0,12},{4,16},{8,20},{12,24},{16,28},{20,32},{24,36},{28,40},{32,4... | collective-permute-start | bytes 393224 | tf_op jit(solution)/shard_map/ppermute | solution.py:273
  83.2 41.6 %collective-permute-start = (s32[128]{0:T(128)S(1)}, s32[128]{0:T(128)S(1)}, u32[]{:S(2)}, u32[]{:S(2)}) collective-permute-start(s32[128]{0:T(128)S(1)} %pad_add_fusion.2), channel_id=1, source_target_pairs={{0,4},{4,8},{8,12},{12,16},{16,20},{20,24},{24,28},{28,32},{32,36}... | collective-permute-start | bytes 1544 | tf_op jit(solution)/shard_map/ppermute | solution.py:273
  86.5 38.4 %collective-permute-start.1 = (s32[128]{0:T(128)S(1)}, s32[128]{0:T(128)S(1)}, u32[]{:S(2)}, u32[]{:S(2)}) collective-permute-start(s32[128]{0:T(128)S(1)} %pad_add_fusion.2), channel_id=1, source_target_pairs={{0,8},{4,12},{8,16},{12,20},{16,24},{20,28},{24,32},{28,36},{32,40... | collective-permute-start | bytes 1544 | tf_op jit(solution)/shard_map/ppermute | solution.py:273
  86.5 38.4 %collective-permute-start.2 = (s32[128]{0:T(128)S(1)}, s32[128]{0:T(128)S(1)}, u32[]{:S(2)}, u32[]{:S(2)}) collective-permute-start(s32[128]{0:T(128)S(1)} %pad_add_fusion.2), channel_id=1, source_target_pairs={{0,12},{4,16},{8,20},{12,24},{16,28},{20,32},{24,36},{28,40},{32,4... | collective-permute-start | bytes 1544 | tf_op jit(solution)/shard_map/ppermute | solution.py:273
  88.4 1.4 copy-start.1
  100.7 21.9 %copy-start.2 = (f32[4,8,4,4,8,4]{5,4,3,2,1,0:T(8,128)S(1)}, f32[4,8,4,4,8,4]{5,4,3,2,1,0:T(8,128)}, u32[]{:S(2)}) copy-start(f32[4,8,4,4,8,4]{5,4,3,2,1,0:T(8,128)} %multiply_bitcast_fusion) | copy-start | bytes 196612
  100.7 84.0 %all-to-all-start.1 = ((bf16[64,8,16,128]{3,2,1,0:T(8,128)(2,1)}), bf16[64,8,16,128]{3,2,1,0:T(8,128)(2,1)}, u32[]{:S(2)}, u32[]{:S(2)}) async-start(bf16[64,8,16,128]{3,2,1,0:T(8,128)(2,1)} %bitcast.58), calls=%async_computation.1 | async-start | bytes 4194304 | tf_op jit(solution)/shard_map/all_to_all | solution.py:344
  138.9 18.9 %collective-permute-start.10 = (f32[1,8,128]{2,1,0:T(8,128)S(1)}, f32[1,8,128]{2,1,0:T(8,128)S(1)}, u32[]{:S(2)}, u32[]{:S(2)}) collective-permute-start(f32[1,8,128]{2,1,0:T(8,128)S(1)} %get-tuple-element.15), channel_id=1, source_target_pairs={{0,244},{4,248},{8,252},{12,0},{16,4},{20,8},{24,12},{28,16},{32,2... | collective-permute-start | bytes 12296 | tf_op jit(solution)/shard_map/ppermute | solution.py:273
  147.6 16.5 %collective-permute-start.6 = (f32[3,8,128]{2,1,0:T(8,128)S(1)}, f32[3,8,128]{2,1,0:T(8,128)S(1)}, u32[]{:S(2)}, u32[]{:S(2)}) collective-permute-start(f32[3,8,128]{2,1,0:T(8,128)S(1)} %get-tuple-element.11), channel_id=1, source_target_pairs={{0,252},{4,0},{8,4},{12,8},{16,12},{20,16},{24,20},{28,24},{32,28}... | collective-permute-start | bytes 36872 | tf_op jit(solution)/shard_map/ppermute | solution.py:273
  147.6 16.5 %collective-permute-start.7 = (f32[3,8,128]{2,1,0:T(8,128)S(1)}, f32[3,8,128]{2,1,0:T(8,128)S(1)}, u32[]{:S(2)}, u32[]{:S(2)}) collective-permute-start(f32[3,8,128]{2,1,0:T(8,128)S(1)} %get-tuple-element.12), channel_id=1, source_target_pairs={{0,4},{4,8},{8,12},{12,16},{16,20},{20,24},{24,28},{28,32},{32,36}... | collective-permute-start | bytes 36872 | tf_op jit(solution)/shard_map/ppermute | solution.py:273
  149.4 14.8 %collective-permute-start.8 = (f32[2,8,128]{2,1,0:T(8,128)S(1)}, f32[2,8,128]{2,1,0:T(8,128)S(1)}, u32[]{:S(2)}, u32[]{:S(2)}) collective-permute-start(f32[2,8,128]{2,1,0:T(8,128)S(1)} %get-tuple-element.13), channel_id=1, source_target_pairs={{0,248},{4,252},{8,0},{12,4},{16,8},{20,12},{24,16},{28,20},{32,24... | collective-permute-start | bytes 24584 | tf_op jit(solution)/shard_map/ppermute | solution.py:273
  153.9 10.3 %collective-permute-start.9 = (f32[2,8,128]{2,1,0:T(8,128)S(1)}, f32[2,8,128]{2,1,0:T(8,128)S(1)}, u32[]{:S(2)}, u32[]{:S(2)}) collective-permute-start(f32[2,8,128]{2,1,0:T(8,128)S(1)} %get-tuple-element.14), channel_id=1, source_target_pairs={{0,8},{4,12},{8,16},{12,20},{16,24},{20,28},{24,32},{28,36},{32,40... | collective-permute-start | bytes 24584 | tf_op jit(solution)/shard_map/ppermute | solution.py:273
  157.8 6.4 %collective-permute-start.11 = (f32[1,8,128]{2,1,0:T(8,128)S(1)}, f32[1,8,128]{2,1,0:T(8,128)S(1)}, u32[]{:S(2)}, u32[]{:S(2)}) collective-permute-start(f32[1,8,128]{2,1,0:T(8,128)S(1)} %get-tuple-element.16), channel_id=1, source_target_pairs={{0,12},{4,16},{8,20},{12,24},{16,28},{20,32},{24,36},{28,40},{32,4... | collective-permute-start | bytes 12296 | tf_op jit(solution)/shard_map/ppermute | solution.py:273
Sparse Core Ops, SparseCore 0:
  82.6 31.9 all-gather.2

commit v2 on v1

v2 whole, which is shorter than its diff:
```python
import functools

import numpy as np

import jax
import jax.numpy as jnp
from jax import lax
from jax.experimental import pallas as pl
from jax.experimental.pallas import tpu as pltpu
from jax.sharding import PartitionSpec as P

NG = 256
BOX = 12
SLAB_PLANES = 4
PAD = 16
LANES = 128
HEAP = LANES // PAD
F32 = jnp.float32
BF16 = jnp.bfloat16
HIGHEST = lax.Precision.HIGHEST
VMEM_LIMIT = 28 * 1024 * 1024
NT = (((1,), (1,)), ((), ()))
TN = (((0,), (0,)), ((), ()))


def kinetic_table(length):
    counter = np.arange(length)
    signed = np.where(counter < length // 2, counter, counter - length).astype(np.float64)
    angle = 2.0 * np.pi * ((counter[:, None] * counter[None, :]) % length) / length
    spectrum = signed**2 / (3.0 * (length // 2) ** 2)
    row = (np.cos(angle) * spectrum[None, :]).sum(1) / length
    table = row[(counter[:, None] - counter[None, :]) % length]
    high = jnp.asarray(table, F32).astype(BF16)
    low = (jnp.asarray(table, F32) - high.astype(F32)).astype(BF16)
    return high, low


def whole(space=pltpu.VMEM):
    return pl.BlockSpec(memory_space=space)


def dot(a, b, dims=None, precision=None):
    if dims is None:
        dims = (((1,), (0,)), ((), ()))
    return lax.dot_general(a, b, dims, precision=precision, preferred_element_type=F32)


def along_z_kernel(high_ref, low_ref, in_ref, *refs):
    out_ref, here, wide, result, there, in_sem, out_sem = refs[-7:]
    length = high_ref.shape[0]
    comps = here.shape[0]
    loads, stores = [], []
    for c in range(comps):
        loads.append(pltpu.make_async_copy(in_ref.at[:, c], here.at[c], in_sem.at[c]))
        stores.append(pltpu.make_async_copy(there.at[c], out_ref.at[:, c], out_sem.at[c]))
        loads[c].start()
    for c in range(comps):
        loads[c].wait()
        wide[c] = here[c].astype(F32).reshape(length * 16, LANES)
        for i in range(8):
            left = wide[c, pl.ds(2 * i, length, stride=16), :]
            right = wide[c, pl.ds(2 * i + 1, length, stride=16), :]
            both = jnp.concatenate([left, right], axis=1).astype(BF16)
            out = dot(high_ref[...], both) + dot(low_ref[...], both)
            result[c, pl.ds(2 * i, length, stride=16), :] = out[:, :LANES]
            result[c, pl.ds(2 * i + 1, length, stride=16), :] = out[:, LANES:]
        there[c] = result[c].reshape(length, 16, LANES).astype(BF16)
        stores[c].start()
    for c in range(comps):
        stores[c].wait()


def along_z(high, low, block, after):
    length, comps = block.shape[:2]
    return pl.pallas_call(
        along_z_kernel,
        out_shape=jax.ShapeDtypeStruct(block.shape, BF16),
        in_specs=[whole()] * 2 + [whole(pltpu.HBM)] + [whole(pl.ANY)] * len(after),
        out_specs=whole(pltpu.HBM),
        scratch_shapes=[
            pltpu.VMEM((comps, length, 16, LANES), BF16),
            pltpu.VMEM((comps, length * 16, LANES), F32),
            pltpu.VMEM((comps, length * 16, LANES), F32),
            pltpu.VMEM((comps, length, 16, LANES), BF16),
            pltpu.SemaphoreType.DMA((comps,)),
            pltpu.SemaphoreType.DMA((comps,)),
        ],
        compiler_params=pltpu.CompilerParams(vmem_limit_bytes=VMEM_LIMIT),
        cost_estimate=pl.CostEstimate(
            flops=4 * length * block.size, bytes_accessed=4 * block.size, transcendentals=0
        ),
        name="along_z",
    )(high, low, block, *after)


def select_matrix(facts, length):
    column = lax.broadcasted_iota(jnp.int32, (length, LANES), 0).astype(F32)
    return jnp.where(column == facts[0:1], 1.0, 0.0).astype(BF16)


def heap_matrix():
    lane = lax.broadcasted_iota(jnp.int32, (HEAP, LANES), 1)
    atom = lax.broadcasted_iota(jnp.int32, (HEAP, LANES), 0)
    return jnp.where(lane // PAD == atom, 1.0, 0.0).astype(F32)


def project_kernel(y_ref, wave_ref, cargo_ref, out_ref, field, sums, *, heaps, reach, nproj):
    planes, length = wave_ref.shape[0], wave_ref.shape[1]
    rows = SLAB_PLANES * PAD
    parts = planes // SLAB_PLANES
    stretch = nproj * rows + PAD
    for i in range(planes):
        for half in range(2):
            part = wave_ref[i, :, half * LANES : (half + 1) * LANES].astype(F32)
            field[i, half, 0:length, :] = part
            field[i, half, length : length + PAD, :] = part[0:PAD]
    lane = lax.broadcasted_iota(jnp.int32, (planes * PAD, LANES), 1)

    def step(index, carry):
        base = (index // heaps) * stretch
        heap = index % heaps
        at = pl.multiple_of(base + nproj * rows, 16)
        facts = cargo_ref[heap, pl.ds(at, PAD), :].astype(F32)
        select = select_matrix(facts, length)
        taken = jnp.zeros((planes * PAD, LANES), F32)
        for a in range(HEAP):
            y0 = y_ref[index * HEAP + a]
            left = field[:, 0, pl.ds(y0, PAD), :].reshape(planes * PAD, LANES)
            right = field[:, 1, pl.ds(y0, PAD), :].reshape(planes * PAD, LANES)
            window = jnp.concatenate([left, right], axis=1).astype(BF16)
            taken = jnp.where(lane // PAD == a, dot(window, select), taken)
        lines = []
        for p in range(nproj):
            at = pl.multiple_of(base + p * rows, 16)
            weight = cargo_ref[heap, pl.ds(at, rows), :].astype(F32)
            for part in range(parts):
                product = weight * taken[part * rows : (part + 1) * rows]
                lines.append(jnp.sum(product, axis=0, keepdims=True))
        at = pl.multiple_of(index * nproj * parts, 8)
        sums[pl.ds(at, nproj * parts), :] = jnp.concatenate(lines, axis=0)
        return carry

    lax.fori_loop(0, reach * heaps, step, 0)
    per_reach = heaps * nproj * parts
    for d in range(reach):
        out_ref[d] = dot(
            heap_matrix(), sums[d * per_reach : (d + 1) * per_reach, :], NT, HIGHEST
        )


def project(y0, wave, cargo, reach, nproj):
    heaps = cargo.shape[0]
    planes, length, _ = wave.shape
    parts = planes // SLAB_PLANES
    return pl.pallas_call(
        functools.partial(project_kernel, heaps=heaps, reach=reach, nproj=nproj),
        out_shape=jax.ShapeDtypeStruct((reach, HEAP, heaps * nproj * parts), F32),
        in_specs=[whole(pltpu.SMEM), whole(), whole()],
        out_specs=whole(),
        scratch_shapes=[
            pltpu.VMEM((planes, 2, length + PAD, LANES), F32),
            pltpu.VMEM((reach * heaps * nproj * parts, LANES), F32),
        ],
        compiler_params=pltpu.CompilerParams(vmem_limit_bytes=VMEM_LIMIT),
        cost_estimate=pl.CostEstimate(
            flops=10_000_000_000, bytes_accessed=5_000_000, transcendentals=0
        ),
        name="project",
    )(y0, wave, cargo)


def local_kernel(
    y_ref, partial_ref, mix_ref, high_ref, low_ref, wave_ref, cargo_ref, after_ref, *refs, reach, nproj
):
    out_ref, total, spread, well = refs[-4:]
    ups, downs = refs[0 : reach - 1], refs[reach - 1 : 2 * (reach - 1)]
    heaps = cargo_ref.shape[0]
    planes, length = wave_ref.shape[0], wave_ref.shape[1]
    rows = SLAB_PLANES * PAD
    parts = planes // SLAB_PLANES
    stretch = nproj * rows + PAD
    per_reach = heaps * nproj * parts
    share = length // heaps

    for r in range(heaps):
        place = lax.rem(y_ref[reach * heaps * HEAP] + r, heaps) * share
        for half in range(2):
            for z in range(SLAB_PLANES):
                at = reach * stretch + (half * SLAB_PLANES + z) * share
                well[half, z, pl.ds(pl.multiple_of(place, 16), share), :] = cargo_ref[r, at : at + share, :].astype(F32)

    def fill(i, carry):
        wave = wave_ref[i]
        value = dot(wave, high_ref[...]) + dot(wave, low_ref[...])
        value += dot(high_ref[...], wave) + dot(low_ref[...], wave)
        wide = wave.astype(F32)
        for half in range(2):
            at = slice(half * LANES, (half + 1) * LANES)
            potential = well[half, lax.rem(i, SLAB_PLANES)]
            total[i, half, 0:length, :] = value[:, at] + potential * wide[:, at]
            total[i, half, length : length + PAD, :] = jnp.zeros((PAD, LANES), F32)
        return carry

    lax.fori_loop(0, planes, fill, 0)
    for d in range(reach):
        full = partial_ref[d]
        for o in range(1, reach):
            if d + o < reach:
                full = full + ups[o - 1][d]
            if d >= o:
                full = full + downs[o - 1][d - o]
        coefficients = dot(full, mix_ref[...], None, HIGHEST)
        spread[d * per_reach : (d + 1) * per_reach, :] = dot(
            coefficients, heap_matrix(), TN, HIGHEST
        )
    lane = lax.broadcasted_iota(jnp.int32, (planes * PAD, LANES), 1)

    def step(index, carry):
        base = (index // heaps) * stretch
        heap = index % heaps
        at = pl.multiple_of(base + nproj * rows, 16)
        facts = cargo_ref[heap, pl.ds(at, PAD), :].astype(F32)
        select = select_matrix(facts, length)
        at = pl.multiple_of(index * nproj * parts, 8)
        lines = spread[pl.ds(at, nproj * parts), :] * facts[2:3]
        blocks = [jnp.zeros((rows, LANES), F32) for _ in range(parts)]
        for p in range(nproj):
            at = pl.multiple_of(base + p * rows, 16)
            weight = cargo_ref[heap, pl.ds(at, rows), :].astype(F32)
            for part in range(parts):
                at = p * parts + part
                blocks[part] = blocks[part] + weight * lines[at : at + 1, :]
        blocks = jnp.concatenate(blocks, axis=0)
        for a in range(HEAP):
            y0 = y_ref[index * HEAP + a]
            one = jnp.where(lane // PAD == a, blocks, 0.0).astype(BF16)
            placed = dot(one, select, NT)
            for half in range(2):
                part = placed[:, half * LANES : (half + 1) * LANES]
                total[:, half, pl.ds(y0, PAD), :] += part.reshape(planes, PAD, LANES)
        return carry

    lax.fori_loop(0, reach * heaps, step, 0)

    def finish(i, carry):
        for half in range(2):
            at = slice(half * LANES, (half + 1) * LANES)
            out_ref[i, 0:PAD, at] = total[i, half, 0:PAD, :] + total[i, half, length : length + PAD, :]
            out_ref[i, PAD:length, at] = total[i, half, PAD:length, :]
        return carry

    lax.fori_loop(0, planes, finish, 0)


def local_part(y0, partial, mix, high, low, wave, cargo, after, ups, downs, nproj):
    heaps = cargo.shape[0]
    planes, length, _ = wave.shape
    parts = planes // SLAB_PLANES
    reach = partial.shape[0]
    return pl.pallas_call(
        functools.partial(local_kernel, reach=reach, nproj=nproj),
        out_shape=jax.ShapeDtypeStruct(wave.shape, F32),
        in_specs=[whole(pltpu.SMEM)] + [whole()] * 6 + [whole(pl.ANY)] + [whole()] * (2 * reach - 2),
        out_specs=whole(),
        scratch_shapes=[
            pltpu.VMEM((planes, 2, length + PAD, LANES), F32),
            pltpu.VMEM((reach * heaps * nproj * parts, LANES), F32),
            pltpu.VMEM((2, SLAB_PLANES, length, LANES), F32),
        ],
        compiler_params=pltpu.CompilerParams(vmem_limit_bytes=VMEM_LIMIT),
        cost_estimate=pl.CostEstimate(
            flops=10_000_000_000, bytes_accessed=10_000_000, transcendentals=0
        ),
        name="local",
    )(y0, partial, mix, high, low, wave, cargo, after, *ups, *downs)


def pack_kernel(in_ref, after_ref, out_ref):
    bands, rows, columns, slab_planes, comps = out_ref.shape[:5]
    for b in range(bands):
        for c in range(comps):
            for z in range(slab_planes):
                plane = (b * comps + c) * slab_planes + z
                for r in range(rows):
                    for h in range(columns):
                        at = (plane, slice(r * 16, (r + 1) * 16), slice(h * LANES, (h + 1) * LANES))
                        out_ref[b, r, h, z, c] = in_ref[at]


def pack(wave, bands, after):
    planes, length, _ = wave.shape
    comps = planes // SLAB_PLANES // bands
    count = 4
    row_blocks, halves = length // 16, length // LANES
    shape = (bands, row_blocks, halves, SLAB_PLANES, comps, 16, LANES)
    return pl.pallas_call(
        pack_kernel,
        out_shape=jax.ShapeDtypeStruct(shape, BF16),
        grid=(count,),
        in_specs=[
            pl.BlockSpec((planes, length // count, length), lambda i: (0, i, 0)),
            whole(pl.ANY),
        ],
        out_specs=pl.BlockSpec(
            (bands, row_blocks // count) + shape[2:], lambda i: (0, i, 0, 0, 0, 0, 0)
        ),
        compiler_params=pltpu.CompilerParams(vmem_limit_bytes=VMEM_LIMIT),
        cost_estimate=pl.CostEstimate(flops=0, bytes_accessed=4 * wave.size, transcendentals=0),
        name="pack",
    )(wave, after)


def frame_kernel(where_ref, box_ref, count_ref, share_ref, out_ref, dense):
    heap = share_ref.shape[0]
    nproj, cells = share_ref.shape[1], BOX * BOX
    band, anchor = where_ref[0], where_ref[1] * SLAB_PLANES
    line = lax.broadcasted_iota(jnp.int32, (cells, LANES), 0)
    lane = lax.broadcasted_iota(jnp.int32, (cells, LANES), 1)
    pick = jnp.where(line % BOX == lane % PAD, 1.0, 0.0).astype(BF16)
    row = lax.broadcasted_iota(jnp.int32, (PAD, cells), 0)
    cell = lax.broadcasted_iota(jnp.int32, (PAD, cells), 1)
    on_row = cell // BOX == row
    lane = lax.broadcasted_iota(jnp.int32, (nproj * PAD, LANES), 1)

    def one_atom(a, carry):
        values = share_ref[a].astype(F32)
        for i in range(BOX):
            part = values[:, i * cells : (i + 1) * cells]
            part = jnp.where(on_row[None], part[:, None, :], 0.0)
            part = part.reshape(nproj * PAD, cells).astype(BF16)
            dense[i] = jnp.where(lane // PAD == a, dot(part, pick), dense[i])
        return carry

    dense[...] = jnp.zeros_like(dense)
    lax.fori_loop(0, heap, one_atom, 0)

    lane = lax.broadcasted_iota(jnp.int32, (1, LANES), 1)
    offset = jnp.zeros((1, LANES), jnp.int32)
    row0 = jnp.zeros((1, LANES), jnp.int32)
    column0 = jnp.zeros((1, LANES), jnp.int32)
    live = jnp.zeros((1, LANES), F32)
    for a in range(heap):
        slot = band * heap + a
        mine = lane // PAD == a
        offset = jnp.where(mine, box_ref[0, slot] - anchor, offset)
        row0 = jnp.where(mine, box_ref[1, slot], row0)
        column0 = jnp.where(mine, box_ref[2, slot], column0)
        live = jnp.where(mine, jnp.where(slot < count_ref[0], 1.0, 0.0), live)
    k = lane % PAD
    target = jnp.where(k < BOX, (column0 + k) % NG, -1)
    facts = jnp.concatenate(
        [target.astype(F32), row0.astype(F32), live, jnp.zeros((PAD - 3, LANES), F32)], axis=0
    ).astype(BF16)

    rows = SLAB_PLANES * PAD
    for f in range(BOX + SLAB_PLANES):
        d, z = f // SLAB_PLANES, f % SLAB_PLANES
        framed = jnp.zeros((nproj * PAD, LANES), F32)
        for o in range(SLAB_PLANES):
            if 0 <= f - o < BOX:
                framed = jnp.where(offset == o, dense[f - o], framed)
        framed = framed.astype(BF16)
        for p in range(nproj):
            out_ref[d, p * rows + z * PAD : p * rows + (z + 1) * PAD, :] = framed[p * PAD : (p + 1) * PAD]
    for d in range(out_ref.shape[0]):
        out_ref[d, nproj * rows : nproj * rows + PAD, :] = facts


def frame(projectors, atom_box, atom_count):
    _, nproj, cells = projectors.shape
    reach = (BOX + SLAB_PLANES) // SLAB_PLANES
    where = jnp.stack([lax.axis_index("band"), lax.axis_index("slab")]).astype(jnp.int32)
    shape = (reach, nproj * SLAB_PLANES * PAD + PAD, LANES)
    return pl.pallas_call(
        frame_kernel,
        out_shape=jax.ShapeDtypeStruct(shape, BF16),
        grid_spec=pltpu.PrefetchScalarGridSpec(
            num_scalar_prefetch=3,
            grid=(1,),
            in_specs=[pl.BlockSpec((HEAP, nproj, cells), lambda i, where, box, count: (where[0], 0, 0))],
            out_specs=pl.BlockSpec(shape, lambda i, where, box, count: (0, 0, 0)),
            scratch_shapes=[pltpu.VMEM((BOX, nproj * PAD, LANES), F32)],
        ),
        compiler_params=pltpu.CompilerParams(vmem_limit_bytes=VMEM_LIMIT),
        cost_estimate=pl.CostEstimate(
            flops=1_000_000_000, bytes_accessed=1_000_000, transcendentals=0
        ),
        name="frame",
    )(where, atom_box, atom_count, projectors)


def join_kernel(local_ref, arrived_ref, out_ref, here, there, in_sem, out_sem):
    bands, rows, columns, slab_planes, comps = arrived_ref.shape[:5]
    count = in_sem.shape[0]
    step = rows // count
    loads, stores = [], []
    for i in range(count):
        at = slice(i * step, (i + 1) * step)
        lines = slice(i * step * 16, (i + 1) * step * 16)
        loads.append(pltpu.make_async_copy(arrived_ref.at[:, at], here.at[:, at], in_sem.at[i]))
        stores.append(pltpu.make_async_copy(there.at[:, lines], out_ref.at[:, lines], out_sem.at[i]))
        loads[i].start()
    for i in range(count):
        loads[i].wait()
        for r in range(i * step, (i + 1) * step):
            for b in range(bands):
                for c in range(comps):
                    for z in range(slab_planes):
                        plane = (b * comps + c) * slab_planes + z
                        for h in range(columns):
                            at = (plane, slice(r * 16, (r + 1) * 16), slice(h * LANES, (h + 1) * LANES))
                            there[at] = (local_ref[at] + here[b, r, h, z, c].astype(F32)).astype(BF16)
        stores[i].start()
    for i in range(count):
        stores[i].wait()


def join(local, arrived):
    count = 8
    return pl.pallas_call(
        join_kernel,
        out_shape=jax.ShapeDtypeStruct(local.shape, BF16),
        in_specs=[whole(), whole(pltpu.HBM)],
        out_specs=whole(pltpu.HBM),
        scratch_shapes=[
            pltpu.VMEM(arrived.shape, BF16),
            pltpu.VMEM(local.shape, BF16),
            pltpu.SemaphoreType.DMA((count,)),
            pltpu.SemaphoreType.DMA((count,)),
        ],
        compiler_params=pltpu.CompilerParams(vmem_limit_bytes=VMEM_LIMIT),
        cost_estimate=pl.CostEstimate(
            flops=2 * local.size, bytes_accessed=8 * local.size, transcendentals=0
        ),
        name="join",
    )(local, arrived)


def ahead(block, distance, axis="slab"):
    size = lax.axis_size(axis)
    return lax.ppermute(block, axis, [(i, (i + distance) % size) for i in range(size)])


def shards(wavefunctions, potential, atom_box, atom_count, projectors, coupling):
    bands, comps, slab_planes, length, _ = wavefunctions.shape
    parts = bands * comps
    planes = parts * slab_planes
    slabs = lax.axis_size("slab")
    heaps = lax.axis_size("band")
    nproj = projectors.shape[1]
    high, low = kinetic_table(length)
    wave = wavefunctions.reshape(planes, length, length)

    framed = frame(projectors, atom_box, atom_count)
    reach = framed.shape[0]
    arrived = [framed[0]] + [ahead(framed[d], d) for d in range(1, reach)]

    send = pack(wave, bands, arrived[1]).reshape(slabs, slab_planes * comps, 16, LANES)
    columns = lax.all_to_all(send, "slab", split_axis=0, concat_axis=0, tiled=True)

    well = potential.astype(BF16).reshape(slab_planes, length // heaps, 2, LANES)
    well = well.transpose(2, 0, 1, 3).reshape(-1, LANES)
    cargo = jnp.concatenate(arrived + [well], axis=0)
    cargo = jnp.stack([cargo] + [ahead(cargo, -r, "band") for r in range(1, heaps)])
    stretch = framed.shape[1]
    tops = jnp.stack([cargo[:, d * stretch + stretch - PAD + 1, ::PAD] for d in range(reach)])
    y0 = jnp.concatenate([tops.astype(jnp.int32).reshape(-1), lax.axis_index("band").astype(jnp.int32)[None]])

    partial = project(y0, wave, cargo, reach, nproj)
    ups = [ahead(partial[o:], -o) for o in range(1, reach)]
    downs = [ahead(partial[: reach - o], o) for o in range(1, reach)]

    symmetric = (coupling + coupling.T) * 0.5
    mix = jnp.einsum(
        "gh,pq,bc->gqbhpc", jnp.eye(heaps, dtype=F32), symmetric, jnp.eye(parts, dtype=F32),
        precision=HIGHEST,
    ).reshape(heaps * nproj * parts, heaps * nproj * parts)

    columns = along_z(high, low, columns.reshape(length, comps, 16, LANES), ups + downs)
    local = local_part(y0, partial, mix, high, low, wave, cargo, columns, ups, downs, nproj)
    columns = columns.reshape(slabs, slab_planes * comps, 16, LANES)
    back = lax.all_to_all(columns, "slab", split_axis=0, concat_axis=0, tiled=True)
    back = back.reshape(bands, length // 16, length // LANES, slab_planes, comps, 16, LANES)
    return join(local, back).reshape(wavefunctions.shape)


def solution(mesh):
    placed = (
        P("band", None, "slab", None, None),
        P("slab", "band", None),
        P(None, "slab"),
        P("slab"),
        P("slab", None, None),
        P(),
    )
    return jax.shard_map(
        shards,
        mesh=mesh,
        in_specs=placed,
        out_specs=P("band", None, "slab", None, None),
        check_vma=False,
    )
```

time: 199 us -> 165 us (0.83)
  between operations: 14.3 us -> 1.05 us
  blocking collectives: 11.9 us -> 0 us
  Pallas kernels: 48.2 us -> 37.4 us
  waiting for transfers between devices: 45.7 us -> 54.8 us
  local copies, waits for them, and re-layouts: 28.8 us -> 21.8 us
  starting transfers between devices: 44.2 us -> 46.2 us
    all_to_all x1, waiting for transfers between devices: 0.01 us -> 25.2 us  [shards(): lax.all_to_all(columns, 'slab', split_axis=0, concat_axis=0, tiled=True)]
    ppermute x12, waiting for transfers between devices: 45.7 us -> 29.6 us  [ahead(): lax.ppermute(block, axis, [(i, (i + distance) % size) for i in range(size)])]
    reshape x5 -> x0, local copies, waits for them, and re-layouts: 12.5 us -> none  [the longest x1 4.59 us: framed_weights(): share = share.reshape(HEAP, nproj, BOX, BOX, BOX).transpose(1, 2, 3, 0, 4)]
    all_gather x1 -> x0, blocking collectives: 11.9 us -> none  [shards(): lax.all_gather(potential.astype(BF16), 'band', axis=1, tiled=True)]
    unnamed x15 -> x37, local copies, waits for them, and re-layouts: 6.2 us -> 15.2 us
    pallas_call x1, Pallas kernels: 10.9 us -> 3.71 us  [along_z(): pl.pallas_call(along_z_kernel, out_shape=jax.ShapeDtypeStruct(block.shape...]
    pallas_call x1, Pallas kernels: 6.54 us -> 2.45 us  [join(): pl.pallas_call(join_kernel, out_shape=jax.ShapeDtypeStruct(local.shape, B...]
    ppermute x12, starting transfers between devices: 21 us -> 24.1 us  [ahead(): lax.ppermute(block, axis, [(i, (i + distance) % size) for i in range(size)])]
  transfers between devices with their start and end apart: 15 -> 14, of which waited for: 5 -> 4; matrix products, arithmetic and copies ran while one was open for 14% -> 7% of each run, Pallas kernels for 21% -> 16%
where the time goes in v2:
time: 165 us
  waiting for transfers between devices  54.8 us (33%)
  starting transfers between devices  46.2 us (28%)
  Pallas kernels  37.4 us (23%)
  local copies, waits for them, and re-layouts  21.8 us (13%)
  other arithmetic  3.51 us (2%)
    ppermute x12, waiting for transfers between devices, ahead(): lax.ppermute(block, axis, [(i, (i + distance) % size) for i in range(size)])  29.6 us
    all_to_all x1, waiting for transfers between devices, shards(): lax.all_to_all(columns, 'slab', split_axis=0, concat_axis=0, tiled=True)  25.2 us
    ppermute x12, starting transfers between devices, ahead(): lax.ppermute(block, axis, [(i, (i + distance) % size) for i in range(size)])  24.1 us
    pallas_call x1, Pallas kernels, local_part(): pl.pallas_call(functools.partial(local_kernel, reach=reach, nproj=nproj),...  15.5 us
    unnamed x37, local copies, waits for them, and re-layouts  15.2 us
    all_to_all x1, starting transfers between devices, shards(): lax.all_to_all(send, 'slab', split_axis=0, concat_axis=0, tiled=True)  13.4 us
    pallas_call x1, Pallas kernels, project(): pl.pallas_call(functools.partial(project_kernel, heaps=heaps, reach=reach...  9.48 us
    all_to_all x1, starting transfers between devices, shards(): lax.all_to_all(columns, 'slab', split_axis=0, concat_axis=0, tiled=True)  8.73 us
  transfers between devices with their start and end apart: 14, of which 4 were waited for; matrix products, arithmetic and copies ran while one was open for 7% of the time, Pallas kernels for 16%

profile of v2, /device:TPU:1, one launch (start us, length us, event | category | flops | bytes accessed | tf_op | source)
XLA Modules:
  0.0 164.7 jit_solution(17604621310252828567)
XLA Ops:
  0.7 0.1 pad_add_fusion.1.where_ref
  0.7 1.2 copy-done.11
  1.9 0.7 copy-done.12
  2.6 4.2 %frame.1 = bf16[4,528,128]{2,1,0:T(8,128)(2,1)S(1)} custom-call(s32[2]{0:T(128)S(1)} %pad_add_fusion.1.where_ref, s32[3,32]{1,0:T(4,128)S(1)} %copy-done.12, s32[1]{0:T(128)S(6)} %copy.29.count_ref, bf16[32,8,1728]{2,1,0:T(8,128)(2,1)S(1)} %copy-done.11), custom_call_target="tpu_custom_call" | custom-call | flops 1000000000 | bytes 1000000 | tf_op jit(solution)/shard_map/frame/pallas_call | solution.py:374
  6.8 3.1 %collective-permute-start = (bf16[528,128]{1,0:T(8,128)(2,1)S(1)}, bf16[528,128]{1,0:T(8,128)(2,1)S(1)}, u32[]{:S(2)}, u32[]{:S(2)}) collective-permute-start(bf16[528,128]{1,0:T(8,128)(2,1)S(1)} %get-tuple-element.7), channel_id=1, source_target_pairs={{0,4},{4,8},{8,12},{12,16},{16,20},{20,24},{24,28},{28,32},{32,36}... | collective-permute-start | bytes 405512 | tf_op jit(solution)/shard_map/ppermute | solution.py:441
  9.9 1.7 %collective-permute-start.1 = (bf16[528,128]{1,0:T(8,128)(2,1)S(1)}, bf16[528,128]{1,0:T(8,128)(2,1)}, u32[]{:S(2)}, u32[]{:S(2)}) collective-permute-start(bf16[528,128]{1,0:T(8,128)(2,1)S(1)} %get-tuple-element.6), channel_id=1, source_target_pairs={{0,8},{4,12},{8,16},{12,20},{16,24},{20,28},{24,32},{28,36},{32,40... | collective-permute-start | bytes 405512 | tf_op jit(solution)/shard_map/ppermute | solution.py:441
  11.5 1.7 %collective-permute-start.2 = (bf16[528,128]{1,0:T(8,128)(2,1)S(1)}, bf16[528,128]{1,0:T(8,128)(2,1)S(1)}, u32[]{:S(2)}, u32[]{:S(2)}) collective-permute-start(bf16[528,128]{1,0:T(8,128)(2,1)S(1)} %get-tuple-element.5), channel_id=1, source_target_pairs={{0,12},{4,16},{8,20},{12,24},{16,28},{20,32},{24,36},{28,40},{32,4... | collective-permute-start | bytes 405512 | tf_op jit(solution)/shard_map/ppermute | solution.py:441
  13.2 0.0 collective-permute-done.after_ref
  13.2 0.0 copy-done.6
  13.2 2.1 %pack.1 = bf16[2,16,2,4,2,16,128]{6,5,4,3,2,1,0:T(8,128)(2,1)} custom-call(bf16[16,256,256]{2,1,0:T(8,128)(2,1)S(1)} %bitcast.48, bf16[528,128]{1,0:T(8,128)(2,1)S(1)} %collective-permute-done.after_ref), custom_call_target="tpu_custom_call" | custom-call | bytes 4194304 | tf_op jit(solution)/shard_map/pack/pallas_call | solution.py:296
  15.3 13.4 %all-to-all-start = ((bf16[64,8,16,128]{3,2,1,0:T(8,128)(2,1)}), bf16[64,8,16,128]{3,2,1,0:T(8,128)(2,1)S(1)}, u32[]{:S(2)}, u32[]{:S(2)}) async-start(bf16[64,8,16,128]{3,2,1,0:T(8,128)(2,1)} %bitcast.15), calls=%async_computation | async-start | bytes 4194304 | tf_op jit(solution)/shard_map/all_to_all | solution.py:459
  28.7 0.0 copy-done.13
  28.8 0.0 collective-permute-done.1
  28.8 0.9 constant_dynamic-update-slice_fusion.2
  29.7 0.0 collective-permute-done.2
  29.8 2.9 %collective-permute-start.4 = (bf16[2624,128]{1,0:T(8,128)(2,1)S(1)}, bf16[2624,128]{1,0:T(8,128)(2,1)S(1)}, u32[]{:S(2)}, u32[]{:S(2)}) collective-permute-start(bf16[2624,128]{1,0:T(8,128)(2,1)S(1)} %constant_dynamic-update-slice_fusion), channel_id=1, source_target_pairs={{0,2},{1,3},{2,0},{3,1},{4,6},{5,7},{6,4},{7,5},{8,10},{9,11},{10,... | collective-permute-start | bytes 2015240 | tf_op jit(solution)/shard_map/ppermute | solution.py:441
  32.6 0.3 collective-permute-start.5
  32.9 2.4 %collective-permute-start.3 = (bf16[2624,128]{1,0:T(8,128)(2,1)S(1)}, bf16[2624,128]{1,0:T(8,128)(2,1)S(1)}, u32[]{:S(2)}, u32[]{:S(2)}) collective-permute-start(bf16[2624,128]{1,0:T(8,128)(2,1)S(1)} %constant_dynamic-update-slice_fusion), channel_id=1, source_target_pairs={{0,3},{1,0},{2,1},{3,2},{4,7},{5,4},{6,5},{7,6},{8,11},{9,8},{10,9... | collective-permute-start | bytes 2015240 | tf_op jit(solution)/shard_map/ppermute | solution.py:441
  35.3 12.3 %collective-permute-done.4 = bf16[2624,128]{1,0:T(8,128)(2,1)S(1)} collective-permute-done((bf16[2624,128]{1,0:T(8,128)(2,1)S(1)}, bf16[2624,128]{1,0:T(8,128)(2,1)S(1)}, u32[]{:S(2)}, u32[]{:S(2)}) %collective-permute-start.4) | collective-permute-done | bytes 671776 | tf_op jit(solution)/shard_map/ppermute | solution.py:441
  47.6 15.2 %collective-permute-done.5 = bf16[2624,128]{1,0:T(8,128)(2,1)S(1)} collective-permute-done((bf16[2624,128]{1,0:T(8,128)(2,1)S(1)}, bf16[2624,128]{1,0:T(8,128)(2,1)S(1)}, u32[]{:S(2)}, u32[]{:S(2)}) %collective-permute-start.5) | collective-permute-done | bytes 671776 | tf_op jit(solution)/shard_map/ppermute | solution.py:441
  62.8 0.0 collective-permute-done.3
  62.8 1.7 %pad_maximum_fusion.cargo_ref = bf16[4,2624,128]{2,1,0:T(8,128)(2,1)} fusion(bf16[1,2624,128]{2,1,0:T(8,128)(2,1)S(1)} %bitcast.53, bf16[1,2624,128]{2,1,0:T(8,128)(2,1)S(1)} %bitcast.52, bf16[1,2624,128]{2,1,0:T(8,128)(2,1)S(1)} %bitcast.54, bf16[1,2624,128]{2,1,0:T(8,128)(2,1)S(1)} %bitcast.51), kind=kLoop, calls=%fused_computation | loop fusion | flops 4030464 | bytes 5373952 | tf_op jit(solution)/shard_map/stack | solution.py:464
  64.4 0.8 slice.46
  65.2 0.8 slice.47
  66.0 0.8 slice.48
  66.8 0.8 slice.49
  67.6 0.1 reshape.40
  67.7 0.0 copy-start.4
  67.7 1.7 %copy-done.4 = bf16[4,2624,128]{2,1,0:T(8,128)(2,1)S(1)} copy-done((bf16[4,2624,128]{2,1,0:T(8,128)(2,1)S(1)}, bf16[4,2624,128]{2,1,0:T(8,128)(2,1)}, u32[]{:S(2)}) %copy-start.4) | copy-done | bytes 2687000
  69.5 1.6 copy-done.7
  71.1 9.5 %project.1.partial_ref = f32[4,8,128]{2,1,0:T(8,128)S(1)} custom-call(s32[129]{0:T(256)S(1)} %pad_add_fusion.y_ref, bf16[16,256,256]{2,1,0:T(8,128)(2,1)S(1)} %bitcast.49, bf16[4,2624,128]{2,1,0:T(8,128)(2,1)S(1)} %copy-done.4), custom_call_target="tpu_custom_call" | custom-call | flops 10000000000 | bytes 5000000 | tf_op jit(solution)/shard_map/project/pallas_call | solution.py:155
  80.6 0.7 collective-permute-start.6
  81.2 1.3 collective-permute-start.9
  82.6 1.4 collective-permute-start.11
  84.0 1.2 collective-permute-start.10
  85.1 5.7 %collective-permute-start.7 = (f32[2,8,128]{2,1,0:T(8,128)S(1)}, f32[2,8,128]{2,1,0:T(8,128)S(1)}, u32[]{:S(2)}, u32[]{:S(2)}) collective-permute-start(f32[2,8,128]{2,1,0:T(8,128)S(1)} %get-tuple-element.11), channel_id=1, source_target_pairs={{0,248},{4,252},{8,0},{12,4},{16,8},{20,12},{24,16},{28,20},{32,24... | collective-permute-start | bytes 24584 | tf_op jit(solution)/shard_map/ppermute | solution.py:441
  90.9 0.0 collective-permute-done.11.refs_5_
  90.9 1.9 %collective-permute-start.8 = (f32[1,8,128]{2,1,0:T(8,128)S(1)}, f32[1,8,128]{2,1,0:T(8,128)S(1)}, u32[]{:S(2)}, u32[]{:S(2)}) collective-permute-start(f32[1,8,128]{2,1,0:T(8,128)S(1)} %get-tuple-element.9), channel_id=1, source_target_pairs={{0,244},{4,248},{8,252},{12,0},{16,4},{20,8},{24,12},{28,16},{32,2... | collective-permute-start | bytes 12296 | tf_op jit(solution)/shard_map/ppermute | solution.py:441
  92.7 2.1 %collective-permute-done.8.refs_2_ = f32[1,8,128]{2,1,0:T(8,128)S(1)} collective-permute-done((f32[1,8,128]{2,1,0:T(8,128)S(1)}, f32[1,8,128]{2,1,0:T(8,128)S(1)}, u32[]{:S(2)}, u32[]{:S(2)}) %collective-permute-start.8) | collective-permute-done | bytes 4128 | tf_op jit(solution)/shard_map/ppermute | solution.py:441
  94.8 0.0 collective-permute-done.10.refs_4_
  94.8 0.0 collective-permute-done.7.refs_1_
  94.8 0.0 collective-permute-done.6.refs_0_
  94.8 0.0 collective-permute-done.9.refs_3_
  94.8 0.0 all-to-all-done
  94.8 0.0 copy-done.9
  94.9 0.0 copy-done.10
  94.9 3.7 %along_z.1.after_ref = bf16[256,2,16,128]{3,2,1,0:T(8,128)(2,1)S(1)} custom-call(bf16[256,256]{1,0:T(8,128)(2,1)S(1)} %copy-done.9, bf16[256,256]{1,0:T(8,128)(2,1)S(1)} %copy-done.10, bf16[256,2,16,128]{3,2,1,0:T(8,128)(2,1)S(1)} %bitcast.46, f32[3,8,128]{2,1,0:T(8,128)S(1)} %collective-permute-done.6.refs_0_, ...), custom_call_target="tpu_custom_call" | custom-call | flops 1073741824 | bytes 4194304 | tf_op jit(solution)/shard_map/along_z/pallas_call | solution.py:75
  98.6 0.0 copy-start
  98.6 1.4 copy-done
  100.0 8.7 %all-to-all-start.1 = ((bf16[64,8,16,128]{3,2,1,0:T(8,128)(2,1)}), bf16[64,8,16,128]{3,2,1,0:T(8,128)(2,1)}, u32[]{:S(2)}, u32[]{:S(2)}) async-start(bf16[64,8,16,128]{3,2,1,0:T(8,128)(2,1)} %bitcast.47), calls=%async_computation.1 | async-start | bytes 4194304 | tf_op jit(solution)/shard_map/all_to_all | solution.py:482
  108.7 0.0 copy-done.14
  108.7 0.1 copy.13
  108.8 0.1 copy.14
  108.9 0.1 broadcast_multiply_fusion
  109.0 1.7 %multiply_bitcast_fusion = f32[4,8,4,4,8,4]{5,4,3,2,1,0:T(8,128)} fusion(f32[8,8]{0,1:T(8,128)S(1)} %copy.14, f32[4,4,4,4]{1,3,0,2:T(4,128)S(1)} %broadcast_multiply_fusion), kind=kLoop, calls=%fused_computation.1 | loop fusion | flops 16384 | bytes 66816 | tf_op jit(solution)/shard_map/gh,pq,bc->gqbhpc/transpose | solution.py:474
  110.6 3.2 %reshape.34.mix_ref = f32[128,128]{1,0:T(8,128)S(1)} reshape(f32[4,8,4,4,8,4]{5,4,3,2,1,0:T(8,128)} %multiply_bitcast_fusion) | data formatting | bytes 131072 | tf_op jit(solution)/shard_map/reshape | solution.py:477
  113.8 0.0 copy-done.8
  113.8 1.6 copy-done.1
  115.4 1.8 %copy-done.5 = bf16[4,2624,128]{2,1,0:T(8,128)(2,1)S(1)} copy-done((bf16[4,2624,128]{2,1,0:T(8,128)(2,1)S(1)}, bf16[4,2624,128]{2,1,0:T(8,128)(2,1)}, u32[]{:S(2)}) %copy-start.5) | copy-done | bytes 2687000
  117.2 15.5 %local.1.local_ref = f32[16,256,256]{2,1,0:T(8,128)S(1)} custom-call(s32[129]{0:T(256)S(1)} %pad_add_fusion.y_ref, f32[4,8,128]{2,1,0:T(8,128)S(1)} %project.1.partial_ref, f32[128,128]{1,0:T(8,128)S(1)} %reshape.34.mix_ref, bf16[256,256]{1,0:T(8,128)(2,1)S(1)} %copy-done.9, bf16[256,256]{1,0:T(8,128)(2,1)S(1)} %copy-done.10, ...), custom_call_target="tpu_custom_call" | custom-call | flops 10000000000 | bytes 10000000 | tf_op jit(solution)/shard_map/local/pallas_call | solution.py:260
  132.7 2.0 %copy-done.2 = f32[16,256,256]{2,1,0:T(8,128)} copy-done((f32[16,256,256]{2,1,0:T(8,128)}, f32[16,256,256]{2,1,0:T(8,128)S(1)}, u32[]{:S(2)}) %copy-start.2) | copy-done | bytes 4194328
  134.6 25.2 %all-to-all-done.1 = bf16[64,8,16,128]{3,2,1,0:T(8,128)(2,1)} async-done(((bf16[64,8,16,128]{3,2,1,0:T(8,128)(2,1)}), bf16[64,8,16,128]{3,2,1,0:T(8,128)(2,1)}, u32[]{:S(2)}, u32[]{:S(2)}) %all-to-all-start.1) | async-done | bytes 2097184 | tf_op jit(solution)/shard_map/all_to_all | solution.py:482
  159.9 2.2 %copy-done.3 = f32[16,256,256]{2,1,0:T(8,128)S(1)} copy-done((f32[16,256,256]{2,1,0:T(8,128)S(1)}, f32[16,256,256]{2,1,0:T(8,128)}, u32[]{:S(2)}) %copy-start.3) | copy-done | bytes 4194328
  162.1 2.4 %join.1 = bf16[16,256,256]{2,1,0:T(8,128)(2,1)} custom-call(f32[16,256,256]{2,1,0:T(8,128)S(1)} %copy-done.3, bf16[2,16,2,4,2,16,128]{6,5,4,3,2,1,0:T(8,128)(2,1)} %bitcast.18.arrived_ref), custom_call_target="tpu_custom_call" | custom-call | flops 2097152 | bytes 8388608 | tf_op jit(solution)/shard_map/join/pallas_call | solution.py:420
  (28 shorter events, 0.2 us)
Async XLA Ops:
  0.7 1.2 copy-start.11
  1.9 0.7 copy-start.12
  2.6 10.6 %copy-start.6 = (bf16[2,2,4,256,256]{4,3,2,1,0:T(8,128)(2,1)S(1)}, bf16[2,2,4,256,256]{4,3,2,1,0:T(8,128)(2,1)}, u32[]{:S(2)}) copy-start(bf16[2,2,4,256,256]{4,3,2,1,0:T(8,128)(2,1)} %param.8) | copy-start | bytes 6291460
  6.8 6.4 %collective-permute-start = (bf16[528,128]{1,0:T(8,128)(2,1)S(1)}, bf16[528,128]{1,0:T(8,128)(2,1)S(1)}, u32[]{:S(2)}, u32[]{:S(2)}) collective-permute-start(bf16[528,128]{1,0:T(8,128)(2,1)S(1)} %get-tuple-element.7), channel_id=1, source_target_pairs={{0,4},{4,8},{8,12},{12,16},{16,20},{20,24},{24,28},{28,32},{32,36}... | collective-permute-start | bytes 405512 | tf_op jit(solution)/shard_map/ppermute | solution.py:441
  9.9 18.9 %collective-permute-start.1 = (bf16[528,128]{1,0:T(8,128)(2,1)S(1)}, bf16[528,128]{1,0:T(8,128)(2,1)}, u32[]{:S(2)}, u32[]{:S(2)}) collective-permute-start(bf16[528,128]{1,0:T(8,128)(2,1)S(1)} %get-tuple-element.6), channel_id=1, source_target_pairs={{0,8},{4,12},{8,16},{12,20},{16,24},{20,28},{24,32},{28,36},{32,40... | collective-permute-start | bytes 405512 | tf_op jit(solution)/shard_map/ppermute | solution.py:441
  11.5 18.2 %collective-permute-start.2 = (bf16[528,128]{1,0:T(8,128)(2,1)S(1)}, bf16[528,128]{1,0:T(8,128)(2,1)S(1)}, u32[]{:S(2)}, u32[]{:S(2)}) collective-permute-start(bf16[528,128]{1,0:T(8,128)(2,1)S(1)} %get-tuple-element.5), channel_id=1, source_target_pairs={{0,12},{4,16},{8,20},{12,24},{16,28},{20,32},{24,36},{28,40},{32,4... | collective-permute-start | bytes 405512 | tf_op jit(solution)/shard_map/ppermute | solution.py:441
  15.3 13.4 %copy-start.13 = (f32[4,64,256]{2,1,0:T(8,128)S(1)}, f32[4,64,256]{2,1,0:T(8,128)}, u32[]{:S(2)}) copy-start(f32[4,64,256]{2,1,0:T(8,128)} %param.9) | copy-start | bytes 786436
  15.3 79.5 %all-to-all-start = ((bf16[64,8,16,128]{3,2,1,0:T(8,128)(2,1)}), bf16[64,8,16,128]{3,2,1,0:T(8,128)(2,1)S(1)}, u32[]{:S(2)}, u32[]{:S(2)}) async-start(bf16[64,8,16,128]{3,2,1,0:T(8,128)(2,1)} %bitcast.15), calls=%async_computation | async-start | bytes 4194304 | tf_op jit(solution)/shard_map/all_to_all | solution.py:459
  29.8 17.8 %collective-permute-start.4 = (bf16[2624,128]{1,0:T(8,128)(2,1)S(1)}, bf16[2624,128]{1,0:T(8,128)(2,1)S(1)}, u32[]{:S(2)}, u32[]{:S(2)}) collective-permute-start(bf16[2624,128]{1,0:T(8,128)(2,1)S(1)} %constant_dynamic-update-slice_fusion), channel_id=1, source_target_pairs={{0,2},{1,3},{2,0},{3,1},{4,6},{5,7},{6,4},{7,5},{8,10},{9,11},{10,... | collective-permute-start | bytes 2015240 | tf_op jit(solution)/shard_map/ppermute | solution.py:441
  32.6 30.1 %collective-permute-start.5 = (bf16[2624,128]{1,0:T(8,128)(2,1)S(1)}, bf16[2624,128]{1,0:T(8,128)(2,1)S(1)}, u32[]{:S(2)}, u32[]{:S(2)}) collective-permute-start(bf16[2624,128]{1,0:T(8,128)(2,1)S(1)} %constant_dynamic-update-slice_fusion), channel_id=1, source_target_pairs={{0,1},{1,2},{2,3},{3,0},{4,5},{5,6},{6,7},{7,4},{8,9},{9,10},{10,1... | collective-permute-start | bytes 2015240 | tf_op jit(solution)/shard_map/ppermute | solution.py:441
  32.9 29.8 %collective-permute-start.3 = (bf16[2624,128]{1,0:T(8,128)(2,1)S(1)}, bf16[2624,128]{1,0:T(8,128)(2,1)S(1)}, u32[]{:S(2)}, u32[]{:S(2)}) collective-permute-start(bf16[2624,128]{1,0:T(8,128)(2,1)S(1)} %constant_dynamic-update-slice_fusion), channel_id=1, source_target_pairs={{0,3},{1,0},{2,1},{3,2},{4,7},{5,4},{6,5},{7,6},{8,11},{9,8},{10,9... | collective-permute-start | bytes 2015240 | tf_op jit(solution)/shard_map/ppermute | solution.py:441
  67.7 1.8 %copy-start.4 = (bf16[4,2624,128]{2,1,0:T(8,128)(2,1)S(1)}, bf16[4,2624,128]{2,1,0:T(8,128)(2,1)}, u32[]{:S(2)}) copy-start(bf16[4,2624,128]{2,1,0:T(8,128)(2,1)} %pad_maximum_fusion.cargo_ref) | copy-start | bytes 8060932
  69.5 1.6 copy-start.7
  71.1 23.8 %copy-start.9 = (bf16[256,256]{1,0:T(8,128)(2,1)S(1)}, bf16[256,256]{1,0:T(8,128)(2,1)}, u32[]{:S(2)}) copy-start(bf16[256,256]{1,0:T(8,128)(2,1)} %constant.19.high_ref) | copy-start | bytes 393220
  71.1 23.8 %copy-start.10 = (bf16[256,256]{1,0:T(8,128)(2,1)S(1)}, bf16[256,256]{1,0:T(8,128)(2,1)}, u32[]{:S(2)}) copy-start(bf16[256,256]{1,0:T(8,128)(2,1)} %constant.22.low_ref) | copy-start | bytes 393220
  80.6 14.2 %collective-permute-start.6 = (f32[3,8,128]{2,1,0:T(8,128)S(1)}, f32[3,8,128]{2,1,0:T(8,128)S(1)}, u32[]{:S(2)}, u32[]{:S(2)}) collective-permute-start(f32[3,8,128]{2,1,0:T(8,128)S(1)} %get-tuple-element.13), channel_id=1, source_target_pairs={{0,252},{4,0},{8,4},{12,8},{16,12},{20,16},{24,20},{28,24},{32,28}... | collective-permute-start | bytes 36872 | tf_op jit(solution)/shard_map/ppermute | solution.py:441
  81.2 13.6 %collective-permute-start.9 = (f32[3,8,128]{2,1,0:T(8,128)S(1)}, f32[3,8,128]{2,1,0:T(8,128)S(1)}, u32[]{:S(2)}, u32[]{:S(2)}) collective-permute-start(f32[3,8,128]{2,1,0:T(8,128)S(1)} %get-tuple-element.12), channel_id=1, source_target_pairs={{0,4},{4,8},{8,12},{12,16},{16,20},{20,24},{24,28},{28,32},{32,36}... | collective-permute-start | bytes 36872 | tf_op jit(solution)/shard_map/ppermute | solution.py:441
  82.6 8.3 %collective-permute-start.11 = (f32[1,8,128]{2,1,0:T(8,128)S(1)}, f32[1,8,128]{2,1,0:T(8,128)S(1)}, u32[]{:S(2)}, u32[]{:S(2)}) collective-permute-start(f32[1,8,128]{2,1,0:T(8,128)S(1)} %get-tuple-element.8), channel_id=1, source_target_pairs={{0,12},{4,16},{8,20},{12,24},{16,28},{20,32},{24,36},{28,40},{32,4... | collective-permute-start | bytes 12296 | tf_op jit(solution)/shard_map/ppermute | solution.py:441
  84.0 10.9 %collective-permute-start.10 = (f32[2,8,128]{2,1,0:T(8,128)S(1)}, f32[2,8,128]{2,1,0:T(8,128)S(1)}, u32[]{:S(2)}, u32[]{:S(2)}) collective-permute-start(f32[2,8,128]{2,1,0:T(8,128)S(1)} %get-tuple-element.10), channel_id=1, source_target_pairs={{0,8},{4,12},{8,16},{12,20},{16,24},{20,28},{24,32},{28,36},{32,40... | collective-permute-start | bytes 24584 | tf_op jit(solution)/shard_map/ppermute | solution.py:441
  85.1 9.7 %collective-permute-start.7 = (f32[2,8,128]{2,1,0:T(8,128)S(1)}, f32[2,8,128]{2,1,0:T(8,128)S(1)}, u32[]{:S(2)}, u32[]{:S(2)}) collective-permute-start(f32[2,8,128]{2,1,0:T(8,128)S(1)} %get-tuple-element.11), channel_id=1, source_target_pairs={{0,248},{4,252},{8,0},{12,4},{16,8},{20,12},{24,16},{28,20},{32,24... | collective-permute-start | bytes 24584 | tf_op jit(solution)/shard_map/ppermute | solution.py:441
  90.9 3.9 %collective-permute-start.8 = (f32[1,8,128]{2,1,0:T(8,128)S(1)}, f32[1,8,128]{2,1,0:T(8,128)S(1)}, u32[]{:S(2)}, u32[]{:S(2)}) collective-permute-start(f32[1,8,128]{2,1,0:T(8,128)S(1)} %get-tuple-element.9), channel_id=1, source_target_pairs={{0,244},{4,248},{8,252},{12,0},{16,4},{20,8},{24,12},{28,16},{32,2... | collective-permute-start | bytes 12296 | tf_op jit(solution)/shard_map/ppermute | solution.py:441
  98.6 1.4 copy-start
  100.0 8.7 %copy-start.14 = (f32[8,8]{1,0:T(8,128)S(1)}, f32[8,8]{1,0:T(8,128)}, u32[]{:S(2)}) copy-start(f32[8,8]{1,0:T(8,128)} %param.13) | copy-start | bytes 772
  100.0 59.9 %all-to-all-start.1 = ((bf16[64,8,16,128]{3,2,1,0:T(8,128)(2,1)}), bf16[64,8,16,128]{3,2,1,0:T(8,128)(2,1)}, u32[]{:S(2)}, u32[]{:S(2)}) async-start(bf16[64,8,16,128]{3,2,1,0:T(8,128)(2,1)} %bitcast.47), calls=%async_computation.1 | async-start | bytes 4194304 | tf_op jit(solution)/shard_map/all_to_all | solution.py:482
  109.0 4.9 %copy-start.8 = (bf16[2,2,4,256,256]{4,3,2,1,0:T(8,128)(2,1)S(1)}, bf16[2,2,4,256,256]{4,3,2,1,0:T(8,128)(2,1)}, u32[]{:S(2)}) copy-start(bf16[2,2,4,256,256]{4,3,2,1,0:T(8,128)(2,1)} %param.8) | copy-start | bytes 6291460
  113.8 1.6 copy-start.1
  115.4 1.8 %copy-start.5 = (bf16[4,2624,128]{2,1,0:T(8,128)(2,1)S(1)}, bf16[4,2624,128]{2,1,0:T(8,128)(2,1)}, u32[]{:S(2)}) copy-start(bf16[4,2624,128]{2,1,0:T(8,128)(2,1)} %pad_maximum_fusion.cargo_ref) | copy-start | bytes 8060932
  132.7 2.0 %copy-start.2 = (f32[16,256,256]{2,1,0:T(8,128)}, f32[16,256,256]{2,1,0:T(8,128)S(1)}, u32[]{:S(2)}) copy-start(f32[16,256,256]{2,1,0:T(8,128)S(1)} %local.1.local_ref) | copy-start | bytes 12582916
  159.9 2.2 %copy-start.3 = (f32[16,256,256]{2,1,0:T(8,128)S(1)}, f32[16,256,256]{2,1,0:T(8,128)}, u32[]{:S(2)}) copy-start(f32[16,256,256]{2,1,0:T(8,128)} %copy-done.2) | copy-start | bytes 12582916

commit v3 on v2

v3 whole, which is shorter than its diff:
```python
import functools

import numpy as np

import jax
import jax.numpy as jnp
from jax import lax
from jax.experimental import pallas as pl
from jax.experimental.pallas import tpu as pltpu
from jax.sharding import PartitionSpec as P

NG = 256
BOX = 12
SLAB_PLANES = 4
PAD = 16
LANES = 128
HEAP = LANES // PAD
F32 = jnp.float32
BF16 = jnp.bfloat16
HIGHEST = lax.Precision.HIGHEST
VMEM_LIMIT = 28 * 1024 * 1024
VMEM_MOST = 62 * 1024 * 1024
NT = (((1,), (1,)), ((), ()))
TN = (((0,), (0,)), ((), ()))


def kinetic_table(length):
    counter = np.arange(length)
    signed = np.where(counter < length // 2, counter, counter - length).astype(np.float64)
    angle = 2.0 * np.pi * ((counter[:, None] * counter[None, :]) % length) / length
    spectrum = signed**2 / (3.0 * (length // 2) ** 2)
    row = (np.cos(angle) * spectrum[None, :]).sum(1) / length
    table = row[(counter[:, None] - counter[None, :]) % length]
    high = jnp.asarray(table, F32).astype(BF16)
    low = (jnp.asarray(table, F32) - high.astype(F32)).astype(BF16)
    return high, low


def whole(space=pltpu.VMEM):
    return pl.BlockSpec(memory_space=space)


def dot(a, b, dims=None, precision=None):
    if dims is None:
        dims = (((1,), (0,)), ((), ()))
    return lax.dot_general(a, b, dims, precision=precision, preferred_element_type=F32)


def along_z_kernel(high_ref, low_ref, in_ref, *refs):
    out_ref, token_ref, wide, result = refs[-4:]
    token_ref[...] = jnp.zeros_like(token_ref)
    length, comps = in_ref.shape[:2]
    for c in range(comps):
        wide[c] = in_ref[:, c].astype(F32).reshape(length * 16, LANES)
        for i in range(8):
            left = wide[c, pl.ds(2 * i, length, stride=16), :]
            right = wide[c, pl.ds(2 * i + 1, length, stride=16), :]
            both = jnp.concatenate([left, right], axis=1).astype(BF16)
            out = dot(high_ref[...], both) + dot(low_ref[...], both)
            result[c, pl.ds(2 * i, length, stride=16), :] = out[:, :LANES]
            result[c, pl.ds(2 * i + 1, length, stride=16), :] = out[:, LANES:]
        out_ref[:, c] = result[c].reshape(length, 16, LANES).astype(BF16)


def along_z(high, low, block, after):
    length, comps = block.shape[:2]
    return pl.pallas_call(
        along_z_kernel,
        out_shape=(
            jax.ShapeDtypeStruct(block.shape, BF16),
            jax.ShapeDtypeStruct((8, LANES), F32),
        ),
        in_specs=[whole()] * 3 + [whole(pl.ANY)] * len(after),
        out_specs=(whole(), whole()),
        scratch_shapes=[pltpu.VMEM((comps, length * 16, LANES), F32)] * 2,
        compiler_params=pltpu.CompilerParams(vmem_limit_bytes=VMEM_LIMIT),
        cost_estimate=pl.CostEstimate(
            flops=4 * length * block.size, bytes_accessed=4 * block.size, transcendentals=0
        ),
        name="along_z",
    )(high, low, block, *after)


def select_matrix(facts, length):
    column = lax.broadcasted_iota(jnp.int32, (length, LANES), 0).astype(F32)
    return jnp.where(column == facts[0:1], 1.0, 0.0).astype(BF16)


def heap_matrix():
    lane = lax.broadcasted_iota(jnp.int32, (HEAP, LANES), 1)
    atom = lax.broadcasted_iota(jnp.int32, (HEAP, LANES), 0)
    return jnp.where(lane // PAD == atom, 1.0, 0.0).astype(F32)


def read_rows(cargo_refs, facts, rows_ref, sem, reach, stretch):
    heaps = len(cargo_refs)
    for d in range(reach):
        for r in range(heaps):
            block = cargo_refs[r][(d + 1) * stretch - PAD : (d + 1) * stretch, :].astype(F32)
            facts[d * heaps + r] = block
    rows = jnp.concatenate([facts[i, 1:2] for i in range(reach * heaps)], axis=0)
    rows_ref[0][...] = rows.astype(jnp.int32)
    copy = pltpu.make_async_copy(rows_ref[0], rows_ref[1], sem)
    copy.start()
    return copy


def read_weights(cargo_ref, at, count, weights):
    weights[0:count, :] = cargo_ref[pl.ds(pl.multiple_of(at, 16), count), :].astype(F32)


def box_weight(weights, p):
    return jnp.concatenate(
        [weights[(p * SLAB_PLANES + z) * BOX : (p * SLAB_PLANES + z) * BOX + PAD, :] for z in range(SLAB_PLANES)],
        axis=0,
    )


def project_kernel(wave_ref, *refs, heaps, reach, nproj):
    cargo_refs = refs[:heaps]
    out_ref, field, sums, weights, facts, rows_vmem, rows_smem, sem = refs[heaps:]
    planes, length = wave_ref.shape[0], wave_ref.shape[1]
    parts = planes // SLAB_PLANES
    count = nproj * SLAB_PLANES * BOX
    stretch = count + PAD
    size = SLAB_PLANES * PAD
    copy = read_rows(cargo_refs, facts, (rows_vmem, rows_smem), sem, reach, stretch)
    for i in range(planes):
        for half in range(2):
            part = wave_ref[i, :, half * LANES : (half + 1) * LANES].astype(F32)
            field[i, half, 0:length, :] = part
            field[i, half, length : length + PAD, :] = part[0:PAD]
    weights[count : count + PAD, :] = jnp.zeros((PAD, LANES), F32)
    lane = lax.broadcasted_iota(jnp.int32, (planes * PAD, LANES), 1)
    line = lax.broadcasted_iota(jnp.int32, (planes * PAD, LANES), 0)
    lane = jnp.where(line % PAD < BOX, lane // PAD, -1)
    copy.wait()

    for heap in range(heaps):

        def step(d, carry, heap=heap):
            index = d * heaps + heap
            select = select_matrix(facts[index], length)
            taken = jnp.zeros((planes * PAD, LANES), F32)
            for a in range(HEAP):
                y0 = rows_smem[index, a * PAD]
                left = field[:, 0, pl.ds(y0, PAD), :].reshape(planes * PAD, LANES)
                right = field[:, 1, pl.ds(y0, PAD), :].reshape(planes * PAD, LANES)
                window = jnp.concatenate([left, right], axis=1).astype(BF16)
                taken = jnp.where(lane == a, dot(window, select), taken)
            read_weights(cargo_refs[heap], d * stretch, count, weights)
            lines = []
            for p in range(nproj):
                weight = box_weight(weights, p)
                for part in range(parts):
                    product = weight * taken[part * size : (part + 1) * size]
                    lines.append(jnp.sum(product, axis=0, keepdims=True))
            at = pl.multiple_of(index * nproj * parts, 8)
            sums[pl.ds(at, nproj * parts), :] = jnp.concatenate(lines, axis=0)
            return carry

        lax.fori_loop(0, reach, step, 0)
    per_reach = heaps * nproj * parts
    for d in range(reach):
        out_ref[d] = dot(
            heap_matrix(), sums[d * per_reach : (d + 1) * per_reach, :], NT, HIGHEST
        )


def cargo_scratch(groups, nproj):
    return [
        pltpu.VMEM((nproj * SLAB_PLANES * BOX + PAD, LANES), F32),
        pltpu.VMEM((groups, PAD, LANES), F32),
        pltpu.VMEM((groups, LANES), jnp.int32),
        pltpu.SMEM((groups, LANES), jnp.int32),
        pltpu.SemaphoreType.DMA,
    ]


def project(wave, cargo, reach, nproj):
    heaps = len(cargo)
    planes, length, _ = wave.shape
    parts = planes // SLAB_PLANES
    return pl.pallas_call(
        functools.partial(project_kernel, heaps=heaps, reach=reach, nproj=nproj),
        out_shape=jax.ShapeDtypeStruct((reach, HEAP, heaps * nproj * parts), F32),
        in_specs=[whole()] * (1 + heaps),
        out_specs=whole(),
        scratch_shapes=[
            pltpu.VMEM((planes, 2, length + PAD, LANES), F32),
            pltpu.VMEM((reach * heaps * nproj * parts, LANES), F32),
            *cargo_scratch(reach * heaps, nproj),
        ],
        compiler_params=pltpu.CompilerParams(vmem_limit_bytes=VMEM_LIMIT),
        cost_estimate=pl.CostEstimate(
            flops=33_000_000_000, bytes_accessed=5_000_000, transcendentals=0
        ),
        name="project",
    )(wave, *cargo)


def local_kernel(where_ref, mix_ref, high_ref, low_ref, wave_ref, *refs, heaps, reach, nproj):
    cargo_refs, well_refs = refs[:heaps], refs[heaps : 2 * heaps]
    mine_ref, pair_ref, above_ref, below_ref, far_ref, _, out_ref = refs[2 * heaps : 2 * heaps + 7]
    total, spread, well, weights, facts, rows_vmem, rows_smem, sem = refs[2 * heaps + 7 :]
    planes, length = wave_ref.shape[0], wave_ref.shape[1]
    parts = planes // SLAB_PLANES
    count = nproj * SLAB_PLANES * BOX
    stretch = count + PAD
    size = SLAB_PLANES * PAD
    per_reach = heaps * nproj * parts
    share = length // heaps
    copy = read_rows(cargo_refs, facts, (rows_vmem, rows_smem), sem, reach, stretch)

    for r in range(heaps):
        place = lax.rem(where_ref[0] + r, heaps) * share
        for half in range(2):
            for z in range(SLAB_PLANES):
                at = (half * SLAB_PLANES + z) * share
                well[half, z, pl.ds(pl.multiple_of(place, 16), share), :] = well_refs[r][at : at + share, :].astype(F32)

    def fill(i, carry):
        wave = wave_ref[i]
        value = dot(wave, high_ref[...]) + dot(wave, low_ref[...])
        value += dot(high_ref[...], wave) + dot(low_ref[...], wave)
        wide = wave.astype(F32)
        for half in range(2):
            at = slice(half * LANES, (half + 1) * LANES)
            potential = well[half, lax.rem(i, SLAB_PLANES)]
            total[i, half, 0:length, :] = value[:, at] + potential * wide[:, at]
            total[i, half, length : length + PAD, :] = jnp.zeros((PAD, LANES), F32)
        return carry

    lax.fori_loop(0, planes, fill, 0)
    even = [far_ref, below_ref.at[0], below_ref.at[1], mine_ref, pair_ref.at[1], above_ref.at[0], above_ref.at[1]]
    odd = [below_ref.at[0], below_ref.at[1], pair_ref.at[0], mine_ref, above_ref.at[0], above_ref.at[1], far_ref]
    is_even = lax.rem(where_ref[1], 2) == 0
    for e in range(reach):
        full = None
        for d in range(reach):
            at = reach - 1 + d - e
            value = jnp.where(is_even, even[at][d], odd[at][d])
            full = value if full is None else full + value
        coefficients = dot(full, mix_ref[...], None, HIGHEST)
        spread[e * per_reach : (e + 1) * per_reach, :] = dot(
            coefficients, heap_matrix(), TN, HIGHEST
        )
    weights[count : count + PAD, :] = jnp.zeros((PAD, LANES), F32)
    lane = lax.broadcasted_iota(jnp.int32, (planes * PAD, LANES), 1)
    line = lax.broadcasted_iota(jnp.int32, (planes * PAD, LANES), 0)
    lane = jnp.where(line % PAD < BOX, lane // PAD, -1)
    copy.wait()

    for heap in range(heaps):

        def step(d, carry, heap=heap):
            index = d * heaps + heap
            select = select_matrix(facts[index], length)
            at = pl.multiple_of(index * nproj * parts, 8)
            lines = spread[pl.ds(at, nproj * parts), :] * facts[index, 2:3]
            read_weights(cargo_refs[heap], d * stretch, count, weights)
            blocks = [jnp.zeros((size, LANES), F32) for _ in range(parts)]
            for p in range(nproj):
                weight = box_weight(weights, p)
                for part in range(parts):
                    at = p * parts + part
                    blocks[part] = blocks[part] + weight * lines[at : at + 1, :]
            blocks = jnp.concatenate(blocks, axis=0)
            for a in range(HEAP):
                y0 = rows_smem[index, a * PAD]
                one = jnp.where(lane == a, blocks, 0.0).astype(BF16)
                placed = dot(one, select, NT)
                for half in range(2):
                    part = placed[:, half * LANES : (half + 1) * LANES]
                    total[:, half, pl.ds(y0, PAD), :] += part.reshape(planes, PAD, LANES)
            return carry

        lax.fori_loop(0, reach, step, 0)

    def finish(i, carry):
        for half in range(2):
            at = slice(half * LANES, (half + 1) * LANES)
            first = total[i, half, 0:PAD, :] + total[i, half, length : length + PAD, :]
            out_ref[i, 0:PAD, at] = first.astype(BF16)
            out_ref[i, PAD:length, at] = total[i, half, PAD:length, :].astype(BF16)
        return carry

    lax.fori_loop(0, planes, finish, 0)


def local_part(where, mix, high, low, wave, cargo, wells, exchanged, after, nproj):
    heaps = len(cargo)
    planes, length, _ = wave.shape
    parts = planes // SLAB_PLANES
    reach = exchanged[0].shape[0]
    return pl.pallas_call(
        functools.partial(local_kernel, heaps=heaps, reach=reach, nproj=nproj),
        out_shape=jax.ShapeDtypeStruct(wave.shape, BF16),
        in_specs=[whole(pltpu.SMEM)] + [whole()] * (4 + 2 * heaps + len(exchanged)) + [whole(pl.ANY)],
        out_specs=whole(),
        scratch_shapes=[
            pltpu.VMEM((planes, 2, length + PAD, LANES), F32),
            pltpu.VMEM((reach * heaps * nproj * parts, LANES), F32),
            pltpu.VMEM((2, SLAB_PLANES, length, LANES), F32),
            *cargo_scratch(reach * heaps, nproj),
        ],
        compiler_params=pltpu.CompilerParams(vmem_limit_bytes=VMEM_LIMIT),
        cost_estimate=pl.CostEstimate(
            flops=10_000_000_000, bytes_accessed=10_000_000, transcendentals=0
        ),
        name="local",
    )(where, mix, high, low, wave, *cargo, *wells, *exchanged, after)


def pack_kernel(in_ref, after_ref, out_ref):
    bands, rows, columns, slab_planes, comps = out_ref.shape[:5]
    for b in range(bands):
        for c in range(comps):
            for z in range(slab_planes):
                plane = (b * comps + c) * slab_planes + z
                for r in range(rows):
                    for h in range(columns):
                        at = (plane, slice(r * 16, (r + 1) * 16), slice(h * LANES, (h + 1) * LANES))
                        out_ref[b, r, h, z, c] = in_ref[at]


def pack(wave, bands, after):
    planes, length, _ = wave.shape
    comps = planes // SLAB_PLANES // bands
    count = 4
    row_blocks, halves = length // 16, length // LANES
    shape = (bands, row_blocks, halves, SLAB_PLANES, comps, 16, LANES)
    return pl.pallas_call(
        pack_kernel,
        out_shape=jax.ShapeDtypeStruct(shape, BF16),
        grid=(count,),
        in_specs=[
            pl.BlockSpec((planes, length // count, length), lambda i: (0, i, 0)),
            whole(pl.ANY),
        ],
        out_specs=pl.BlockSpec(
            (bands, row_blocks // count) + shape[2:], lambda i: (0, i, 0, 0, 0, 0, 0)
        ),
        compiler_params=pltpu.CompilerParams(vmem_limit_bytes=VMEM_LIMIT),
        cost_estimate=pl.CostEstimate(flops=0, bytes_accessed=4 * wave.size, transcendentals=0),
        name="pack",
    )(wave, after)


def gather_rows(nproj):
    size = SLAB_PLANES * BOX * nproj
    table = np.zeros((size, size), np.float32)
    for p in range(nproj):
        for z in range(SLAB_PLANES):
            for j in range(BOX):
                table[(p * SLAB_PLANES + z) * BOX + j, (z * BOX + j) * nproj + p] = 1.0
    return jnp.asarray(table, BF16)


def frame_kernel(where_ref, box_ref, count_ref, share_ref, order_ref, *refs):
    out_refs, dense = refs[:-1], refs[-1]
    heap = share_ref.shape[0]
    nproj, cells = share_ref.shape[1:]
    band, anchor = where_ref[0], where_ref[1] * SLAB_PLANES
    lane = lax.broadcasted_iota(jnp.int32, (nproj, LANES), 1)
    for a in range(heap):
        values = share_ref[a].astype(F32)
        tiles = [values[:, t : min(t + LANES, cells)] for t in range(0, cells, LANES)]
        gap = LANES - tiles[-1].shape[1]
        if gap:
            tiles[-1] = jnp.concatenate([tiles[-1], jnp.zeros((nproj, gap), F32)], axis=1)
        mine = (lane // PAD == a) & (lane % PAD < BOX)
        for m in range(cells // BOX):
            tile, skip = m * BOX // LANES, m * BOX % LANES
            source = tiles[tile]
            if skip + BOX > LANES:
                source = jnp.where(lane >= skip, source, tiles[tile + 1])
            shift = (a * PAD - skip) % LANES
            if shift:
                source = pltpu.roll(source, shift, 1)
            at = (m // BOX, slice(m % BOX * nproj, (m % BOX + 1) * nproj))
            dense[at] = jnp.where(mine, source, dense[at] if a else 0.0)

    lane = lax.broadcasted_iota(jnp.int32, (1, LANES), 1)
    offset = jnp.zeros((1, LANES), jnp.int32)
    row0 = jnp.zeros((1, LANES), jnp.int32)
    column0 = jnp.zeros((1, LANES), jnp.int32)
    live = jnp.zeros((1, LANES), F32)
    for a in range(heap):
        slot = band * heap + a
        mine = lane // PAD == a
        offset = jnp.where(mine, box_ref[0, slot] - anchor, offset)
        row0 = jnp.where(mine, box_ref[1, slot], row0)
        column0 = jnp.where(mine, box_ref[2, slot], column0)
        live = jnp.where(mine, jnp.where(slot < count_ref[0], 1.0, 0.0), live)
    k = lane % PAD
    target = jnp.where(k < BOX, (column0 + k) % NG, -1)
    facts = jnp.concatenate(
        [target.astype(F32), row0.astype(F32), live, jnp.zeros((PAD - 3, LANES), F32)], axis=0
    ).astype(BF16)

    rows = nproj * SLAB_PLANES * BOX
    for d in range(len(out_refs)):
        planes = []
        for z in range(SLAB_PLANES):
            f = d * SLAB_PLANES + z
            framed = jnp.zeros((BOX * nproj, LANES), F32)
            for o in range(SLAB_PLANES):
                if 0 <= f - o < BOX:
                    framed = jnp.where(offset == o, dense[f - o], framed)
            planes.append(framed)
        planes = jnp.concatenate(planes, axis=0).astype(BF16)
        out_refs[d][0:rows, :] = dot(order_ref[...], planes).astype(BF16)
        out_refs[d][rows : rows + PAD, :] = facts


def frame(where, projectors, atom_box, atom_count):
    _, nproj, cells = projectors.shape
    reach = (BOX + SLAB_PLANES) // SLAB_PLANES
    order = gather_rows(nproj)
    shape = (nproj * SLAB_PLANES * BOX + PAD, LANES)
    return pl.pallas_call(
        frame_kernel,
        out_shape=(jax.ShapeDtypeStruct(shape, BF16),) * reach,
        grid_spec=pltpu.PrefetchScalarGridSpec(
            num_scalar_prefetch=3,
            grid=(1,),
            in_specs=[
                pl.BlockSpec((HEAP, nproj, cells), lambda i, where, box, count: (where[0], 0, 0)),
                whole(),
            ],
            out_specs=(pl.BlockSpec(shape, lambda i, where, box, count: (0, 0)),) * reach,
            scratch_shapes=[pltpu.VMEM((BOX, nproj * BOX, LANES), F32)],
        ),
        compiler_params=pltpu.CompilerParams(vmem_limit_bytes=VMEM_MOST),
        cost_estimate=pl.CostEstimate(
            flops=1_000_000_000, bytes_accessed=1_000_000, transcendentals=0
        ),
        name="frame",
    )(where, atom_box, atom_count, projectors, order)


def join_kernel(local_ref, arrived_ref, out_ref, near, here, there, near_sem, in_sem, out_sem):
    bands, rows, columns, slab_planes, comps = arrived_ref.shape[:5]
    count = in_sem.shape[0]
    step = rows // count
    loads, stores = [], []
    for i in range(count):
        at = slice(i * step, (i + 1) * step)
        lines = slice(i * step * 16, (i + 1) * step * 16)
        loads.append(pltpu.make_async_copy(local_ref.at[:, lines], near.at[:, lines], near_sem.at[i]))
        loads.append(pltpu.make_async_copy(arrived_ref.at[:, at], here.at[:, at], in_sem.at[i]))
        stores.append(pltpu.make_async_copy(there.at[:, lines], out_ref.at[:, lines], out_sem.at[i]))
    for load in loads:
        load.start()
    for i in range(count):
        loads[2 * i].wait()
        loads[2 * i + 1].wait()
        for r in range(i * step, (i + 1) * step):
            for b in range(bands):
                for c in range(comps):
                    for z in range(slab_planes):
                        plane = (b * comps + c) * slab_planes + z
                        for h in range(columns):
                            at = (plane, slice(r * 16, (r + 1) * 16), slice(h * LANES, (h + 1) * LANES))
                            value = near[at].astype(F32) + here[b, r, h, z, c].astype(F32)
                            there[at] = value.astype(BF16)
        stores[i].start()
    for store in stores:
        store.wait()


def join(local, arrived):
    count = 8
    return pl.pallas_call(
        join_kernel,
        out_shape=jax.ShapeDtypeStruct(local.shape, BF16),
        in_specs=[whole(pltpu.HBM), whole(pltpu.HBM)],
        out_specs=whole(pltpu.HBM),
        scratch_shapes=[
            pltpu.VMEM(local.shape, BF16),
            pltpu.VMEM(arrived.shape, BF16),
            pltpu.VMEM(local.shape, BF16),
            pltpu.SemaphoreType.DMA((count,)),
            pltpu.SemaphoreType.DMA((count,)),
            pltpu.SemaphoreType.DMA((count,)),
        ],
        compiler_params=pltpu.CompilerParams(vmem_limit_bytes=VMEM_MOST),
        cost_estimate=pl.CostEstimate(
            flops=2 * local.size, bytes_accessed=6 * local.size, transcendentals=0
        ),
        name="join",
    )(local, arrived)


def ahead(block, distance, axis="slab"):
    size = lax.axis_size(axis)
    return lax.ppermute(block, axis, [(i, (i + distance) % size) for i in range(size)])


def shards(wavefunctions, potential, atom_box, atom_count, projectors, coupling):
    bands, comps, slab_planes, length, _ = wavefunctions.shape
    parts = bands * comps
    planes = parts * slab_planes
    slabs = lax.axis_size("slab")
    heaps = lax.axis_size("band")
    nproj = projectors.shape[1]
    high, low = kinetic_table(length)
    wave = wavefunctions.reshape(planes, length, length)

    where = jnp.stack([lax.axis_index("band"), lax.axis_index("slab")]).astype(jnp.int32)
    framed = frame(where, projectors, atom_box, atom_count)
    reach = len(framed)
    arrived = [framed[0]] + [ahead(framed[d], d) for d in range(1, reach)]

    send = pack(wave, bands, arrived[1]).reshape(slabs, slab_planes * comps, 16, LANES)
    columns = lax.all_to_all(send, "slab", split_axis=0, concat_axis=0, tiled=True)

    cargo = jnp.concatenate(arrived, axis=0)
    cargo = [cargo] + [ahead(cargo, -r, "band") for r in range(1, heaps)]
    well = potential.astype(BF16).reshape(slab_planes, length // heaps, 2, LANES)
    well = well.transpose(2, 0, 1, 3).reshape(-1, LANES)
    wells = [well] + [ahead(well, -r, "band") for r in range(1, heaps)]

    partial = project(wave, cargo, reach, nproj)
    other = lax.ppermute(partial, "slab", [(i, i ^ 1) for i in range(slabs)])
    even = where[1] % 2 == 0
    pair = jnp.stack([jnp.where(even, partial, other), jnp.where(even, other, partial)])
    above = ahead(pair, -2)
    below = ahead(pair, 2)
    far = lax.ppermute(
        partial, "slab", [(i, (i + 3 if i % 2 else i - 3) % slabs) for i in range(slabs)]
    )

    symmetric = (coupling + coupling.T) * 0.5
    mix = jnp.einsum(
        "gh,pq,bc->gqbhpc", jnp.eye(heaps, dtype=F32), symmetric, jnp.eye(parts, dtype=F32),
        precision=HIGHEST,
    ).reshape(heaps * nproj * parts, heaps * nproj * parts)

    exchanged = [partial, pair, above, below, far]
    columns, token = along_z(high, low, columns.reshape(length, comps, 16, LANES), exchanged[2:])
    local = local_part(where, mix, high, low, wave, cargo, wells, exchanged, token, nproj)
    columns = columns.reshape(slabs, slab_planes * comps, 16, LANES)
    back = lax.all_to_all(columns, "slab", split_axis=0, concat_axis=0, tiled=True)
    back = back.reshape(bands, length // 16, length // LANES, slab_planes, comps, 16, LANES)
    return join(local, back).reshape(wavefunctions.shape)


def solution(mesh):
    placed = (
        P("band", None, "slab", None, None),
        P("slab", "band", None),
        P(None, "slab"),
        P("slab"),
        P("slab", None, None),
        P(),
    )
    return jax.shard_map(
        shards,
        mesh=mesh,
        in_specs=placed,
        out_specs=P("band", None, "slab", None, None),
        check_vma=False,
    )
```

time: 165 us -> 148 us (0.90)
  waiting for transfers between devices: 54.8 us -> 47.3 us
  local copies, waits for them, and re-layouts: 21.8 us -> 16.5 us
  starting transfers between devices: 46.2 us -> 41.6 us
    ppermute x12 -> x11, waiting for transfers between devices: 29.6 us -> 18.6 us  [ahead(): lax.ppermute(block, axis, [(i, (i + distance) % size) for i in range(size)])]
    ppermute x0 -> x2, waiting for transfers between devices: none -> 10.9 us  [the longest x1 10.1 us: shards(): lax.ppermute(partial, 'slab', [(i, (i + 3 if i % 2 else i - 3) % slabs) f...]
    all_to_all x1, waiting for transfers between devices: 25.2 us -> 16.8 us  [shards(): lax.all_to_all(columns, 'slab', split_axis=0, concat_axis=0, tiled=True)]
    slice x7 -> x0, local copies, waits for them, and re-layouts: 3.18 us -> none  [the longest x4 3.17 us: shards(): cargo[:, d * stretch + stretch - PAD + 1, ::PAD]]
    ppermute x12 -> x11, starting transfers between devices: 24.1 us -> 21.3 us  [ahead(): lax.ppermute(block, axis, [(i, (i + distance) % size) for i in range(size)])]
    all_to_all x1, starting transfers between devices: 8.73 us -> 6.51 us  [shards(): lax.all_to_all(columns, 'slab', split_axis=0, concat_axis=0, tiled=True)]
    unnamed x37 -> x50, local copies, waits for them, and re-layouts: 15.2 us -> 13.2 us
  transfers between devices with their start and end apart: 14 -> 15, of which waited for: 4 -> 7; matrix products, arithmetic and copies ran while one was open for 7% -> 4% of each run, Pallas kernels for 16% -> 18%
where the time goes in v3:
time: 148 us; the launch traced here: 147 us
  waiting for transfers between devices  47.3 us (32%)
  starting transfers between devices  41.6 us (28%)
  Pallas kernels  38.4 us (26%)
  local copies, waits for them, and re-layouts  16.5 us (11%)
  other arithmetic  2.35 us (2%)
    ppermute x11, starting transfers between devices, ahead(): lax.ppermute(block, axis, [(i, (i + distance) % size) for i in range(size)])  21.3 us
    ppermute x11, waiting for transfers between devices, ahead(): lax.ppermute(block, axis, [(i, (i + distance) % size) for i in range(size)])  18.6 us
    all_to_all x1, waiting for transfers between devices, shards(): lax.all_to_all(columns, 'slab', split_axis=0, concat_axis=0, tiled=True)  16.8 us
    pallas_call x1, Pallas kernels, local_part(): pl.pallas_call(functools.partial(local_kernel, heaps=heaps, reach=reach,...  15.6 us
    unnamed x50, local copies, waits for them, and re-layouts  13.2 us
    all_to_all x1, starting transfers between devices, shards(): lax.all_to_all(send, 'slab', split_axis=0, concat_axis=0, tiled=True)  12.3 us
    ppermute x1, waiting for transfers between devices, shards(): lax.ppermute(partial, 'slab', [(i, (i + 3 if i % 2 else i - 3) % slabs) f...  10.1 us
    pallas_call x1, Pallas kernels, project(): pl.pallas_call(functools.partial(project_kernel, heaps=heaps, reach=reach...  9.16 us
  transfers between devices with their start and end apart: 15, of which 7 were waited for; matrix products, arithmetic and copies ran while one was open for 4% of the time, Pallas kernels for 18%

profile of v3, /device:TPU:1, one launch (start us, length us, event | category | flops | bytes accessed | tf_op | source)
XLA Modules:
  0.0 147.2 jit_solution(10061097273767306169)
XLA Ops:
  0.7 0.6 pad_add_fusion.where_ref
  1.2 3.4 %frame.1 = (bf16[400,128]{1,0:T(8,128)(2,1)}, bf16[400,128]{1,0:T(8,128)(2,1)}, bf16[400,128]{1,0:T(8,128)(2,1)}, bf16[400,128]{1,0:T(8,128)(2,1)}) custom-call(s32[2]{0:T(128)} %pad_add_fusion.where_ref, s32[3,32]{1,0:T(4,128)} %box_ref.1, s32[1]{0:T(128)S(6)} %copy.21.count_ref, bf16[32,8,1728]{2,1,0:T(8,128)(2,1)} %share_ref.1, ...), custom_call_target="tpu_custom_call" | custom-call | flops 1000000000 | bytes 1000000 | tf_op jit(solution)/shard_map/frame/pallas_call | solution.py:422
  4.6 3.0 %collective-permute-start = (bf16[400,128]{1,0:T(8,128)(2,1)}, bf16[400,128]{1,0:T(8,128)(2,1)S(1)}, u32[]{:S(2)}, u32[]{:S(2)}) collective-permute-start(bf16[400,128]{1,0:T(8,128)(2,1)} %get-tuple-element.12), channel_id=1, source_target_pairs={{0,4},{4,8},{8,12},{12,16},{16,20},{20,24},{24,28},{28,32},{32,36}... | collective-permute-start | bytes 307208 | tf_op jit(solution)/shard_map/ppermute | solution.py:498
  7.7 1.6 %collective-permute-start.1 = (bf16[400,128]{1,0:T(8,128)(2,1)}, bf16[400,128]{1,0:T(8,128)(2,1)S(1)}, u32[]{:S(2)}, u32[]{:S(2)}) collective-permute-start(bf16[400,128]{1,0:T(8,128)(2,1)} %get-tuple-element.13), channel_id=1, source_target_pairs={{0,8},{4,12},{8,16},{12,20},{16,24},{20,28},{24,32},{28,36},{32,40... | collective-permute-start | bytes 307208 | tf_op jit(solution)/shard_map/ppermute | solution.py:498
  9.3 1.7 %collective-permute-start.2 = (bf16[400,128]{1,0:T(8,128)(2,1)}, bf16[400,128]{1,0:T(8,128)(2,1)S(1)}, u32[]{:S(2)}, u32[]{:S(2)}) collective-permute-start(bf16[400,128]{1,0:T(8,128)(2,1)} %get-tuple-element.14), channel_id=1, source_target_pairs={{0,12},{4,16},{8,20},{12,24},{16,28},{20,32},{24,36},{28,40},{32,4... | collective-permute-start | bytes 307208 | tf_op jit(solution)/shard_map/ppermute | solution.py:498
  11.0 0.9 constant_dynamic-update-slice_fusion.3
  11.9 0.0 collective-permute-done.after_ref
  11.9 0.0 copy-start.1
  11.9 1.6 %copy-done.1 = bf16[2,2,4,256,256]{4,3,2,1,0:T(8,128)(2,1)S(1)} copy-done((bf16[2,2,4,256,256]{4,3,2,1,0:T(8,128)(2,1)S(1)}, bf16[2,2,4,256,256]{4,3,2,1,0:T(8,128)(2,1)}, u32[]{:S(2)}) %copy-start.1) | copy-done | bytes 2097176
  13.5 2.1 %pack.1 = bf16[2,16,2,4,2,16,128]{6,5,4,3,2,1,0:T(8,128)(2,1)} custom-call(bf16[16,256,256]{2,1,0:T(8,128)(2,1)S(1)} %bitcast.28, bf16[400,128]{1,0:T(8,128)(2,1)S(1)} %collective-permute-done.after_ref), custom_call_target="tpu_custom_call" | custom-call | bytes 4194304 | tf_op jit(solution)/shard_map/pack/pallas_call | solution.py:333
  15.5 12.3 %all-to-all-start = ((bf16[64,8,16,128]{3,2,1,0:T(8,128)(2,1)}), bf16[64,8,16,128]{3,2,1,0:T(8,128)(2,1)}, u32[]{:S(2)}, u32[]{:S(2)}) async-start(bf16[64,8,16,128]{3,2,1,0:T(8,128)(2,1)} %bitcast.10), calls=%async_computation | async-start | bytes 4194304 | tf_op jit(solution)/shard_map/all_to_all | solution.py:517
  27.9 0.0 collective-permute-done.1
  27.9 0.0 collective-permute-done.2
  27.9 0.0 copy-start.14
  27.9 0.0 copy-start.16
  28.0 1.3 collective-permute-start.5
  29.2 2.5 %collective-permute-start.4 = (bf16[1600,128]{1,0:T(8,128)(2,1)S(1)}, bf16[1600,128]{1,0:T(8,128)(2,1)S(1)}, u32[]{:S(2)}, u32[]{:S(2)}) collective-permute-start(bf16[1600,128]{1,0:T(8,128)(2,1)S(1)} %constant_dynamic-update-slice_fusion.refs_0_), channel_id=1, source_target_pairs={{0,2},{1,3},{2,0},{3,1},{4,6},{5,7},{6,4},{7,5},{8,10},{9,11},{10,... | collective-permute-start | bytes 1228808 | tf_op jit(solution)/shard_map/ppermute | solution.py:498
  31.7 1.2 collective-permute-start.3
  32.8 7.0 %collective-permute-done.5.refs_3_ = bf16[1600,128]{1,0:T(8,128)(2,1)S(1)} collective-permute-done((bf16[1600,128]{1,0:T(8,128)(2,1)S(1)}, bf16[1600,128]{1,0:T(8,128)(2,1)S(1)}, u32[]{:S(2)}, u32[]{:S(2)}) %collective-permute-start.5) | collective-permute-done | bytes 409632 | tf_op jit(solution)/shard_map/ppermute | solution.py:498
  39.8 9.7 %collective-permute-done.4.refs_2_ = bf16[1600,128]{1,0:T(8,128)(2,1)S(1)} collective-permute-done((bf16[1600,128]{1,0:T(8,128)(2,1)S(1)}, bf16[1600,128]{1,0:T(8,128)(2,1)S(1)}, u32[]{:S(2)}, u32[]{:S(2)}) %collective-permute-start.4) | collective-permute-done | bytes 409632 | tf_op jit(solution)/shard_map/ppermute | solution.py:498
  49.5 0.0 collective-permute-done.3.refs_1_
  49.5 0.0 copy-done.2
  49.5 0.0 copy-start.6
  49.5 9.2 %project.1.refs_8_ = f32[4,8,128]{2,1,0:T(8,128)S(1)} custom-call(bf16[16,256,256]{2,1,0:T(8,128)(2,1)S(1)} %bitcast.29, bf16[1600,128]{1,0:T(8,128)(2,1)S(1)} %constant_dynamic-update-slice_fusion.refs_0_, bf16[1600,128]{1,0:T(8,128)(2,1)S(1)} %collective-permute-done.3.refs_1_, bf16[1600,128]{1,0:T(8,128)(2,1)S(1)} %collective-permute-done.4.refs_2_, ...), custom_call_target="tpu_custom_call" | custom-call | flops 32999999488 | bytes 5000000 | tf_op jit(solution)/shard_map/project/pallas_call | solution.py:184
  58.7 1.5 %collective-permute-start.9 = (f32[4,8,128]{2,1,0:T(8,128)S(1)}, f32[4,8,128]{2,1,0:T(8,128)S(1)}, u32[]{:S(2)}, u32[]{:S(2)}) collective-permute-start(f32[4,8,128]{2,1,0:T(8,128)S(1)} %project.1.refs_8_), channel_id=1, source_target_pairs={{0,4},{4,0},{8,12},{12,8},{16,20},{20,16},{24,28},{28,24},{32,36},... | collective-permute-start | bytes 49160 | tf_op jit(solution)/shard_map/ppermute | solution.py:526
  60.2 0.8 collective-permute-done.9
  61.0 1.5 %collective-permute-start.11 = (f32[2,4,8,128]{3,2,1,0:T(8,128)S(1)}, f32[2,4,8,128]{3,2,1,0:T(8,128)S(1)}, u32[]{:S(2)}, u32[]{:S(2)}) collective-permute-start(f32[2,4,8,128]{3,2,1,0:T(8,128)S(1)} %pad_maximum_fusion.refs_9_), channel_id=1, source_target_pairs={{0,8},{4,12},{8,16},{12,20},{16,24},{20,28},{24,32},{28,36},{32,40... | collective-permute-start | bytes 98312 | tf_op jit(solution)/shard_map/ppermute | solution.py:498
  62.5 3.7 %collective-permute-start.10 = (f32[2,4,8,128]{3,2,1,0:T(8,128)S(1)}, f32[2,4,8,128]{3,2,1,0:T(8,128)S(1)}, u32[]{:S(2)}, u32[]{:S(2)}) collective-permute-start(f32[2,4,8,128]{3,2,1,0:T(8,128)S(1)} %pad_maximum_fusion.refs_9_), channel_id=1, source_target_pairs={{0,248},{4,252},{8,0},{12,4},{16,8},{20,12},{24,16},{28,20},{32,24... | collective-permute-start | bytes 98312 | tf_op jit(solution)/shard_map/ppermute | solution.py:498
  66.2 0.0 collective-permute-start.12
  66.2 10.1 %collective-permute-done.12.refs_2_.refs_12_ = f32[4,8,128]{2,1,0:T(8,128)S(1)} collective-permute-done((f32[4,8,128]{2,1,0:T(8,128)S(1)}, f32[4,8,128]{2,1,0:T(8,128)S(1)}, u32[]{:S(2)}, u32[]{:S(2)}) %collective-permute-start.12) | collective-permute-done | bytes 16416 | tf_op jit(solution)/shard_map/ppermute | solution.py:531
  76.3 1.9 %collective-permute-done.11.refs_1_.refs_11_ = f32[2,4,8,128]{3,2,1,0:T(8,128)S(1)} collective-permute-done((f32[2,4,8,128]{3,2,1,0:T(8,128)S(1)}, f32[2,4,8,128]{3,2,1,0:T(8,128)S(1)}, u32[]{:S(2)}, u32[]{:S(2)}) %collective-permute-start.11) | collective-permute-done | bytes 32800 | tf_op jit(solution)/shard_map/ppermute | solution.py:498
  78.2 0.0 collective-permute-done.10.refs_0_.refs_10_
  78.2 1.0 all-to-all-done
  79.2 0.0 copy-done.16
  79.2 4.8 %along_z.1 = (bf16[256,2,16,128]{3,2,1,0:T(8,128)(2,1)S(1)}, f32[8,128]{1,0:T(8,128)S(1)}) custom-call(bf16[256,256]{1,0:T(8,128)(2,1)S(1)} %copy-done.16, bf16[256,256]{1,0:T(8,128)(2,1)S(1)} %copy-done.14, bf16[256,2,16,128]{3,2,1,0:T(8,128)(2,1)} %bitcast.11.in_ref, f32[2,4,8,128]{3,2,1,0:T(8,128)S(1)} %collective-permute-done.10.refs_0_.refs_10_, ...), custom_call_target="tpu_custom_call" | custom-call | flops 1073741824 | bytes 4194304 | tf_op jit(solution)/shard_map/along_z/pallas_call | solution.py:67
  84.1 0.6 copy-done.19
  84.7 1.3 copy-done.3
  86.0 0.0 copy-done.12
  86.0 6.5 %all-to-all-start.1 = ((bf16[64,8,16,128]{3,2,1,0:T(8,128)(2,1)}), bf16[64,8,16,128]{3,2,1,0:T(8,128)(2,1)}, u32[]{:S(2)}, u32[]{:S(2)}) async-start(bf16[64,8,16,128]{3,2,1,0:T(8,128)(2,1)} %bitcast.31), calls=%async_computation.1 | async-start | bytes 4194304 | tf_op jit(solution)/shard_map/all_to_all | solution.py:545
  92.6 1.3 collective-permute-start.8
  93.8 2.5 %collective-permute-start.7 = (bf16[512,128]{1,0:T(8,128)(2,1)S(1)}, bf16[512,128]{1,0:T(8,128)(2,1)S(1)}, u32[]{:S(2)}, u32[]{:S(2)}) collective-permute-start(bf16[512,128]{1,0:T(8,128)(2,1)S(1)} %bitcast.33), channel_id=1, source_target_pairs={{0,2},{1,3},{2,0},{3,1},{4,6},{5,7},{6,4},{7,5},{8,10},{9,11},{10,... | collective-permute-start | bytes 393224 | tf_op jit(solution)/shard_map/ppermute | solution.py:498
  96.3 1.1 collective-permute-start.6
  97.4 0.1 copy.13
  97.5 0.1 copy.14
  97.6 0.1 broadcast_multiply_fusion
  97.7 1.7 %multiply_bitcast_fusion = f32[4,8,4,4,8,4]{5,4,3,2,1,0:T(8,128)} fusion(f32[8,8]{0,1:T(8,128)S(1)} %copy.14, f32[4,4,4,4]{1,3,0,2:T(4,128)S(1)} %broadcast_multiply_fusion), kind=kLoop, calls=%fused_computation | loop fusion | flops 16384 | bytes 66816 | tf_op jit(solution)/shard_map/gh,pq,bc->gqbhpc/transpose | solution.py:536
  99.3 3.2 %reshape.27.mix_ref = f32[128,128]{1,0:T(8,128)S(1)} reshape(f32[4,8,4,4,8,4]{5,4,3,2,1,0:T(8,128)} %multiply_bitcast_fusion) | data formatting | bytes 131072 | tf_op jit(solution)/shard_map/reshape | solution.py:539
  102.5 0.0 collective-permute-done.8.refs_7_
  102.5 0.0 collective-permute-done.7.refs_6_
  102.6 0.0 collective-permute-done.6.refs_5_
  102.6 0.0 copy-start.5
  102.6 1.0 copy-done.5
  103.6 1.0 copy-done.7
  104.6 0.8 copy-done.9
  105.3 0.8 copy-done.11
  106.1 0.7 copy-done.13
  106.8 0.9 copy-done.15
  107.7 0.9 copy-done.17
  108.6 0.6 copy-done.18
  109.2 0.7 copy-done.20
  109.9 15.6 %local.1.local_ref = bf16[16,256,256]{2,1,0:T(8,128)(2,1)S(1)} custom-call(s32[2]{0:T(128)S(1)} %copy-done.18, f32[128,128]{1,0:T(8,128)S(1)} %reshape.27.mix_ref, bf16[256,256]{1,0:T(8,128)(2,1)S(1)} %copy-done.17, bf16[256,256]{1,0:T(8,128)(2,1)S(1)} %copy-done.15, bf16[16,256,256]{2,1,0:T(8,128)(2,1)S(1)} %bitcast.30, ...), custom_call_target="tpu_custom_call" | custom-call | flops 10000000000 | bytes 10000000 | tf_op jit(solution)/shard_map/local/pallas_call | solution.py:296
  125.5 1.4 copy-done
  126.9 16.8 %all-to-all-done.1 = bf16[64,8,16,128]{3,2,1,0:T(8,128)(2,1)} async-done(((bf16[64,8,16,128]{3,2,1,0:T(8,128)(2,1)}), bf16[64,8,16,128]{3,2,1,0:T(8,128)(2,1)}, u32[]{:S(2)}, u32[]{:S(2)}) %all-to-all-start.1) | async-done | bytes 2097184 | tf_op jit(solution)/shard_map/all_to_all | solution.py:545
  143.7 3.4 %join.1 = bf16[16,256,256]{2,1,0:T(8,128)(2,1)} custom-call(bf16[16,256,256]{2,1,0:T(8,128)(2,1)} %copy-done, bf16[2,16,2,4,2,16,128]{6,5,4,3,2,1,0:T(8,128)(2,1)} %bitcast.13.arrived_ref), custom_call_target="tpu_custom_call" | custom-call | flops 2097152 | bytes 6291456 | tf_op jit(solution)/shard_map/join/pallas_call | solution.py:475
  (33 shorter events, 0.1 us)
Async XLA Ops:
  4.6 7.2 %collective-permute-start = (bf16[400,128]{1,0:T(8,128)(2,1)}, bf16[400,128]{1,0:T(8,128)(2,1)S(1)}, u32[]{:S(2)}, u32[]{:S(2)}) collective-permute-start(bf16[400,128]{1,0:T(8,128)(2,1)} %get-tuple-element.12), channel_id=1, source_target_pairs={{0,4},{4,8},{8,12},{12,16},{16,20},{20,24},{24,28},{28,32},{32,36}... | collective-permute-start | bytes 307208 | tf_op jit(solution)/shard_map/ppermute | solution.py:498
  7.7 20.2 %collective-permute-start.1 = (bf16[400,128]{1,0:T(8,128)(2,1)}, bf16[400,128]{1,0:T(8,128)(2,1)S(1)}, u32[]{:S(2)}, u32[]{:S(2)}) collective-permute-start(bf16[400,128]{1,0:T(8,128)(2,1)} %get-tuple-element.13), channel_id=1, source_target_pairs={{0,8},{4,12},{8,16},{12,20},{16,24},{20,28},{24,32},{28,36},{32,40... | collective-permute-start | bytes 307208 | tf_op jit(solution)/shard_map/ppermute | solution.py:498
  9.3 18.6 %collective-permute-start.2 = (bf16[400,128]{1,0:T(8,128)(2,1)}, bf16[400,128]{1,0:T(8,128)(2,1)S(1)}, u32[]{:S(2)}, u32[]{:S(2)}) collective-permute-start(bf16[400,128]{1,0:T(8,128)(2,1)} %get-tuple-element.14), channel_id=1, source_target_pairs={{0,12},{4,16},{8,20},{12,24},{16,28},{20,32},{24,36},{28,40},{32,4... | collective-permute-start | bytes 307208 | tf_op jit(solution)/shard_map/ppermute | solution.py:498
  11.9 1.6 %copy-start.1 = (bf16[2,2,4,256,256]{4,3,2,1,0:T(8,128)(2,1)S(1)}, bf16[2,2,4,256,256]{4,3,2,1,0:T(8,128)(2,1)}, u32[]{:S(2)}) copy-start(bf16[2,2,4,256,256]{4,3,2,1,0:T(8,128)(2,1)} %param.9) | copy-start | bytes 6291460
  15.5 34.0 %copy-start.2 = (bf16[2,2,4,256,256]{4,3,2,1,0:T(8,128)(2,1)S(1)}, bf16[2,2,4,256,256]{4,3,2,1,0:T(8,128)(2,1)}, u32[]{:S(2)}) copy-start(bf16[2,2,4,256,256]{4,3,2,1,0:T(8,128)(2,1)} %param.9) | copy-start | bytes 6291460
  15.5 63.7 %all-to-all-start = ((bf16[64,8,16,128]{3,2,1,0:T(8,128)(2,1)}), bf16[64,8,16,128]{3,2,1,0:T(8,128)(2,1)}, u32[]{:S(2)}, u32[]{:S(2)}) async-start(bf16[64,8,16,128]{3,2,1,0:T(8,128)(2,1)} %bitcast.10), calls=%async_computation | async-start | bytes 4194304 | tf_op jit(solution)/shard_map/all_to_all | solution.py:517
  27.9 51.3 %copy-start.14 = (bf16[256,256]{1,0:T(8,128)(2,1)S(1)}, bf16[256,256]{1,0:T(8,128)(2,1)}, u32[]{:S(2)}) copy-start(bf16[256,256]{1,0:T(8,128)(2,1)} %constant.39.low_ref) | copy-start | bytes 393220
  27.9 51.3 %copy-start.16 = (bf16[256,256]{1,0:T(8,128)(2,1)S(1)}, bf16[256,256]{1,0:T(8,128)(2,1)}, u32[]{:S(2)}) copy-start(bf16[256,256]{1,0:T(8,128)(2,1)} %constant.36.high_ref) | copy-start | bytes 393220
  28.0 11.9 %collective-permute-start.5 = (bf16[1600,128]{1,0:T(8,128)(2,1)S(1)}, bf16[1600,128]{1,0:T(8,128)(2,1)S(1)}, u32[]{:S(2)}, u32[]{:S(2)}) collective-permute-start(bf16[1600,128]{1,0:T(8,128)(2,1)S(1)} %constant_dynamic-update-slice_fusion.refs_0_), channel_id=1, source_target_pairs={{0,1},{1,2},{2,3},{3,0},{4,5},{5,6},{6,7},{7,4},{8,9},{9,10},{10,1... | collective-permute-start | bytes 1228808 | tf_op jit(solution)/shard_map/ppermute | solution.py:498
  29.2 20.3 %collective-permute-start.4 = (bf16[1600,128]{1,0:T(8,128)(2,1)S(1)}, bf16[1600,128]{1,0:T(8,128)(2,1)S(1)}, u32[]{:S(2)}, u32[]{:S(2)}) collective-permute-start(bf16[1600,128]{1,0:T(8,128)(2,1)S(1)} %constant_dynamic-update-slice_fusion.refs_0_), channel_id=1, source_target_pairs={{0,2},{1,3},{2,0},{3,1},{4,6},{5,7},{6,4},{7,5},{8,10},{9,11},{10,... | collective-permute-start | bytes 1228808 | tf_op jit(solution)/shard_map/ppermute | solution.py:498
  31.7 17.8 %collective-permute-start.3 = (bf16[1600,128]{1,0:T(8,128)(2,1)S(1)}, bf16[1600,128]{1,0:T(8,128)(2,1)S(1)}, u32[]{:S(2)}, u32[]{:S(2)}) collective-permute-start(bf16[1600,128]{1,0:T(8,128)(2,1)S(1)} %constant_dynamic-update-slice_fusion.refs_0_), channel_id=1, source_target_pairs={{0,3},{1,0},{2,1},{3,2},{4,7},{5,4},{6,5},{7,6},{8,11},{9,8},{10,9... | collective-permute-start | bytes 1228808 | tf_op jit(solution)/shard_map/ppermute | solution.py:498
  49.5 9.2 %copy-start.4 = (bf16[1600,128]{1,0:T(8,128)(2,1)}, bf16[1600,128]{1,0:T(8,128)(2,1)S(1)}, u32[]{:S(2)}) copy-start(bf16[1600,128]{1,0:T(8,128)(2,1)S(1)} %collective-permute-done.4.refs_2_) | copy-start | bytes 1228804
  49.5 9.2 %copy-start.6 = (bf16[1600,128]{1,0:T(8,128)(2,1)}, bf16[1600,128]{1,0:T(8,128)(2,1)S(1)}, u32[]{:S(2)}) copy-start(bf16[1600,128]{1,0:T(8,128)(2,1)S(1)} %collective-permute-done.3.refs_1_) | copy-start | bytes 1228804
  58.7 2.3 %collective-permute-start.9 = (f32[4,8,128]{2,1,0:T(8,128)S(1)}, f32[4,8,128]{2,1,0:T(8,128)S(1)}, u32[]{:S(2)}, u32[]{:S(2)}) collective-permute-start(f32[4,8,128]{2,1,0:T(8,128)S(1)} %project.1.refs_8_), channel_id=1, source_target_pairs={{0,4},{4,0},{8,12},{12,8},{16,20},{20,16},{24,28},{28,24},{32,36},... | collective-permute-start | bytes 49160 | tf_op jit(solution)/shard_map/ppermute | solution.py:526
  61.0 17.1 %collective-permute-start.11 = (f32[2,4,8,128]{3,2,1,0:T(8,128)S(1)}, f32[2,4,8,128]{3,2,1,0:T(8,128)S(1)}, u32[]{:S(2)}, u32[]{:S(2)}) collective-permute-start(f32[2,4,8,128]{3,2,1,0:T(8,128)S(1)} %pad_maximum_fusion.refs_9_), channel_id=1, source_target_pairs={{0,8},{4,12},{8,16},{12,20},{16,24},{20,28},{24,32},{28,36},{32,40... | collective-permute-start | bytes 98312 | tf_op jit(solution)/shard_map/ppermute | solution.py:498
  62.5 15.7 %collective-permute-start.10 = (f32[2,4,8,128]{3,2,1,0:T(8,128)S(1)}, f32[2,4,8,128]{3,2,1,0:T(8,128)S(1)}, u32[]{:S(2)}, u32[]{:S(2)}) collective-permute-start(f32[2,4,8,128]{3,2,1,0:T(8,128)S(1)} %pad_maximum_fusion.refs_9_), channel_id=1, source_target_pairs={{0,248},{4,252},{8,0},{12,4},{16,8},{20,12},{24,16},{28,20},{32,24... | collective-permute-start | bytes 98312 | tf_op jit(solution)/shard_map/ppermute | solution.py:498
  66.2 10.1 %collective-permute-start.12 = (f32[4,8,128]{2,1,0:T(8,128)S(1)}, f32[4,8,128]{2,1,0:T(8,128)S(1)}, u32[]{:S(2)}, u32[]{:S(2)}) collective-permute-start(f32[4,8,128]{2,1,0:T(8,128)S(1)} %project.1.refs_8_), channel_id=1, source_target_pairs={{0,244},{4,16},{8,252},{12,24},{16,4},{20,32},{24,12},{28,40},{32,... | collective-permute-start | bytes 49160 | tf_op jit(solution)/shard_map/ppermute | solution.py:531
  76.3 9.7 %copy-start.12 = (f32[4,8,128]{2,1,0:T(8,128)}, f32[4,8,128]{2,1,0:T(8,128)S(1)}, u32[]{:S(2)}) copy-start(f32[4,8,128]{2,1,0:T(8,128)S(1)} %collective-permute-done.12.refs_2_.refs_12_) | copy-start | bytes 49156
  78.2 7.8 %copy-start.8 = (f32[2,4,8,128]{3,2,1,0:T(8,128)}, f32[2,4,8,128]{3,2,1,0:T(8,128)S(1)}, u32[]{:S(2)}) copy-start(f32[2,4,8,128]{3,2,1,0:T(8,128)S(1)} %collective-permute-done.11.refs_1_.refs_11_) | copy-start | bytes 98308
  78.2 7.8 %copy-start.10 = (f32[2,4,8,128]{3,2,1,0:T(8,128)}, f32[2,4,8,128]{3,2,1,0:T(8,128)S(1)}, u32[]{:S(2)}) copy-start(f32[2,4,8,128]{3,2,1,0:T(8,128)S(1)} %collective-permute-done.10.refs_0_.refs_10_) | copy-start | bytes 98308
  84.1 0.6 copy-start.19
  84.7 1.3 copy-start.3
  86.0 6.5 %copy-start.21 = (f32[4,64,256]{2,1,0:T(8,128)S(1)}, f32[4,64,256]{2,1,0:T(8,128)}, u32[]{:S(2)}) copy-start(f32[4,64,256]{2,1,0:T(8,128)} %param.10) | copy-start | bytes 786436
  86.0 11.5 %copy-start.22 = (f32[8,8]{1,0:T(8,128)S(1)}, f32[8,8]{1,0:T(8,128)}, u32[]{:S(2)}) copy-start(f32[8,8]{1,0:T(8,128)} %param.14) | copy-start | bytes 772
  86.0 57.7 %all-to-all-start.1 = ((bf16[64,8,16,128]{3,2,1,0:T(8,128)(2,1)}), bf16[64,8,16,128]{3,2,1,0:T(8,128)(2,1)}, u32[]{:S(2)}, u32[]{:S(2)}) async-start(bf16[64,8,16,128]{3,2,1,0:T(8,128)(2,1)} %bitcast.31), calls=%async_computation.1 | async-start | bytes 4194304 | tf_op jit(solution)/shard_map/all_to_all | solution.py:545
  92.6 10.0 %collective-permute-start.8 = (bf16[512,128]{1,0:T(8,128)(2,1)S(1)}, bf16[512,128]{1,0:T(8,128)(2,1)S(1)}, u32[]{:S(2)}, u32[]{:S(2)}) collective-permute-start(bf16[512,128]{1,0:T(8,128)(2,1)S(1)} %bitcast.32), channel_id=1, source_target_pairs={{0,1},{1,2},{2,3},{3,0},{4,5},{5,6},{6,7},{7,4},{8,9},{9,10},{10,1... | collective-permute-start | bytes 393224 | tf_op jit(solution)/shard_map/ppermute | solution.py:498
  93.8 8.7 %collective-permute-start.7 = (bf16[512,128]{1,0:T(8,128)(2,1)S(1)}, bf16[512,128]{1,0:T(8,128)(2,1)S(1)}, u32[]{:S(2)}, u32[]{:S(2)}) collective-permute-start(bf16[512,128]{1,0:T(8,128)(2,1)S(1)} %bitcast.33), channel_id=1, source_target_pairs={{0,2},{1,3},{2,0},{3,1},{4,6},{5,7},{6,4},{7,5},{8,10},{9,11},{10,... | collective-permute-start | bytes 393224 | tf_op jit(solution)/shard_map/ppermute | solution.py:498
  96.3 6.3 %collective-permute-start.6 = (bf16[512,128]{1,0:T(8,128)(2,1)S(1)}, bf16[512,128]{1,0:T(8,128)(2,1)S(1)}, u32[]{:S(2)}, u32[]{:S(2)}) collective-permute-start(bf16[512,128]{1,0:T(8,128)(2,1)S(1)} %bitcast.34), channel_id=1, source_target_pairs={{0,3},{1,0},{2,1},{3,2},{4,7},{5,4},{6,5},{7,6},{8,11},{9,8},{10,9... | collective-permute-start | bytes 393224 | tf_op jit(solution)/shard_map/ppermute | solution.py:498
  102.6 1.0 copy-start.5
  103.6 1.0 copy-start.7
  104.6 0.8 copy-start.9
  105.3 0.8 copy-start.11
  106.1 0.7 copy-start.13
  106.8 0.9 copy-start.15
  107.7 0.9 copy-start.17
  108.6 0.6 copy-start.18
  109.2 0.7 copy-start.20
  125.5 1.4 copy-start

commit v4 on v3

--- a/solution.py
+++ b/solution.py
@@ -13,6 +13,7 @@
 BOX = 12
 SLAB_PLANES = 4
 PAD = 16
+PITCH = 20
 LANES = 128
 HEAP = LANES // PAD
 F32 = jnp.float32
@@ -33,7 +34,7 @@
     table = row[(counter[:, None] - counter[None, :]) % length]
     high = jnp.asarray(table, F32).astype(BF16)
     low = (jnp.asarray(table, F32) - high.astype(F32)).astype(BF16)
-    return high, low
+    return jnp.stack([high, low])
 
 
 def whole(space=pltpu.VMEM):
@@ -46,23 +47,25 @@
     return lax.dot_general(a, b, dims, precision=precision, preferred_element_type=F32)
 
 
-def along_z_kernel(high_ref, low_ref, in_ref, *refs):
+def along_z_kernel(table_ref, in_ref, *refs):
     out_ref, token_ref, wide, result = refs[-4:]
     token_ref[...] = jnp.zeros_like(token_ref)
-    length, comps = in_ref.shape[:2]
+    length, comps, rows = in_ref.shape[:3]
     for c in range(comps):
-        wide[c] = in_ref[:, c].astype(F32).reshape(length * 16, LANES)
-        for i in range(8):
-            left = wide[c, pl.ds(2 * i, length, stride=16), :]
-            right = wide[c, pl.ds(2 * i + 1, length, stride=16), :]
+        for z in range(length):
+            wide[c, z * PITCH : z * PITCH + rows, :] = in_ref[z, c].astype(F32)
+        for i in range(rows // 2):
+            left = wide[c, pl.ds(2 * i, length, stride=PITCH), :]
+            right = wide[c, pl.ds(2 * i + 1, length, stride=PITCH), :]
             both = jnp.concatenate([left, right], axis=1).astype(BF16)
-            out = dot(high_ref[...], both) + dot(low_ref[...], both)
-            result[c, pl.ds(2 * i, length, stride=16), :] = out[:, :LANES]
-            result[c, pl.ds(2 * i + 1, length, stride=16), :] = out[:, LANES:]
-        out_ref[:, c] = result[c].reshape(length, 16, LANES).astype(BF16)
-
-
-def along_z(high, low, block, after):
+            out = dot(table_ref[0], both) + dot(table_ref[1], both)
+            result[c, pl.ds(2 * i, length, stride=PITCH), :] = out[:, :LANES]
+            result[c, pl.ds(2 * i + 1, length, stride=PITCH), :] = out[:, LANES:]
+        for z in range(length):
+            out_ref[z, c] = result[c, z * PITCH : z * PITCH + rows, :].astype(BF16)
+
+
+def along_z(table, block, after):
     length, comps = block.shape[:2]
     return pl.pallas_call(
         along_z_kernel,
@@ -70,15 +73,15 @@
             jax.ShapeDtypeStruct(block.shape, BF16),
             jax.ShapeDtypeStruct((8, LANES), F32),
         ),
-        in_specs=[whole()] * 3 + [whole(pl.ANY)] * len(after),
+        in_specs=[whole()] * 2 + [whole(pl.ANY)] * len(after),
         out_specs=(whole(), whole()),
-        scratch_shapes=[pltpu.VMEM((comps, length * 16, LANES), F32)] * 2,
+        scratch_shapes=[pltpu.VMEM((comps, length * PITCH, LANES), F32)] * 2,
         compiler_params=pltpu.CompilerParams(vmem_limit_bytes=VMEM_LIMIT),
         cost_estimate=pl.CostEstimate(
             flops=4 * length * block.size, bytes_accessed=4 * block.size, transcendentals=0
         ),
         name="along_z",
-    )(high, low, block, *after)
+    )(table, block, *after)
 
 
 def select_matrix(facts, length):
@@ -199,7 +202,7 @@
     )(wave, *cargo)
 
 
-def local_kernel(where_ref, mix_ref, high_ref, low_ref, wave_ref, *refs, heaps, reach, nproj):
+def local_kernel(mix_ref, table_ref, wave_ref, *refs, heaps, reach, nproj):
     cargo_refs, well_refs = refs[:heaps], refs[heaps : 2 * heaps]
     mine_ref, pair_ref, above_ref, below_ref, far_ref, _, out_ref = refs[2 * heaps : 2 * heaps + 7]
     total, spread, well, weights, facts, rows_vmem, rows_smem, sem = refs[2 * heaps + 7 :]
@@ -213,7 +216,7 @@
     copy = read_rows(cargo_refs, facts, (rows_vmem, rows_smem), sem, reach, stretch)
 
     for r in range(heaps):
-        place = lax.rem(where_ref[0] + r, heaps) * share
+        place = lax.rem(lax.axis_index("band") + r, heaps) * share
         for half in range(2):
             for z in range(SLAB_PLANES):
                 at = (half * SLAB_PLANES + z) * share
@@ -221,8 +224,8 @@
 
     def fill(i, carry):
         wave = wave_ref[i]
-        value = dot(wave, high_ref[...]) + dot(wave, low_ref[...])
-        value += dot(high_ref[...], wave) + dot(low_ref[...], wave)
+        value = dot(wave, table_ref[0]) + dot(wave, table_ref[1])
+        value += dot(table_ref[0], wave) + dot(table_ref[1], wave)
         wide = wave.astype(F32)
         for half in range(2):
             at = slice(half * LANES, (half + 1) * LANES)
@@ -234,7 +237,7 @@
     lax.fori_loop(0, planes, fill, 0)
     even = [far_ref, below_ref.at[0], below_ref.at[1], mine_ref, pair_ref.at[1], above_ref.at[0], above_ref.at[1]]
     odd = [below_ref.at[0], below_ref.at[1], pair_ref.at[0], mine_ref, above_ref.at[0], above_ref.at[1], far_ref]
-    is_even = lax.rem(where_ref[1], 2) == 0
+    is_even = lax.rem(lax.axis_index("slab"), 2) == 0
     for e in range(reach):
         full = None
         for d in range(reach):
@@ -288,7 +291,7 @@
     lax.fori_loop(0, planes, finish, 0)
 
 
-def local_part(where, mix, high, low, wave, cargo, wells, exchanged, after, nproj):
+def local_part(mix, table, wave, cargo, wells, exchanged, after, nproj):
     heaps = len(cargo)
     planes, length, _ = wave.shape
     parts = planes // SLAB_PLANES
@@ -296,7 +299,7 @@
     return pl.pallas_call(
         functools.partial(local_kernel, heaps=heaps, reach=reach, nproj=nproj),
         out_shape=jax.ShapeDtypeStruct(wave.shape, BF16),
-        in_specs=[whole(pltpu.SMEM)] + [whole()] * (4 + 2 * heaps + len(exchanged)) + [whole(pl.ANY)],
+        in_specs=[whole()] * (3 + 2 * heaps + len(exchanged)) + [whole(pl.ANY)],
         out_specs=whole(),
         scratch_shapes=[
             pltpu.VMEM((planes, 2, length + PAD, LANES), F32),
@@ -309,42 +312,7 @@
             flops=10_000_000_000, bytes_accessed=10_000_000, transcendentals=0
         ),
         name="local",
-    )(where, mix, high, low, wave, *cargo, *wells, *exchanged, after)
-
-
-def pack_kernel(in_ref, after_ref, out_ref):
-    bands, rows, columns, slab_planes, comps = out_ref.shape[:5]
-    for b in range(bands):
-        for c in range(comps):
-            for z in range(slab_planes):
-                plane = (b * comps + c) * slab_planes + z
-                for r in range(rows):
-                    for h in range(columns):
-                        at = (plane, slice(r * 16, (r + 1) * 16), slice(h * LANES, (h + 1) * LANES))
-                        out_ref[b, r, h, z, c] = in_ref[at]
-
-
-def pack(wave, bands, after):
-    planes, length, _ = wave.shape
-    comps = planes // SLAB_PLANES // bands
-    count = 4
-    row_blocks, halves = length // 16, length // LANES
-    shape = (bands, row_blocks, halves, SLAB_PLANES, comps, 16, LANES)
-    return pl.pallas_call(
-        pack_kernel,
-        out_shape=jax.ShapeDtypeStruct(shape, BF16),
-        grid=(count,),
-        in_specs=[
-            pl.BlockSpec((planes, length // count, length), lambda i: (0, i, 0)),
-            whole(pl.ANY),
-        ],
-        out_specs=pl.BlockSpec(
-            (bands, row_blocks // count) + shape[2:], lambda i: (0, i, 0, 0, 0, 0, 0)
-        ),
-        compiler_params=pltpu.CompilerParams(vmem_limit_bytes=VMEM_LIMIT),
-        cost_estimate=pl.CostEstimate(flops=0, bytes_accessed=4 * wave.size, transcendentals=0),
-        name="pack",
-    )(wave, after)
+    )(mix, table, wave, *cargo, *wells, *exchanged, after)
 
 
 def gather_rows(nproj):
@@ -357,11 +325,31 @@
     return jnp.asarray(table, BF16)
 
 
-def frame_kernel(where_ref, box_ref, count_ref, share_ref, order_ref, *refs):
-    out_refs, dense = refs[:-1], refs[-1]
-    heap = share_ref.shape[0]
-    nproj, cells = share_ref.shape[1:]
-    band, anchor = where_ref[0], where_ref[1] * SLAB_PLANES
+def frame_kernel(
+    box_ref, count_ref, projectors_ref, order_ref, wave_ref, send_ref, *refs
+):
+    out_refs, scratch = refs[:-10], refs[-10:]
+    dense, share_ref, order, done, field, packed, fetch_sem, in_sem, out_sem, done_sem = scratch
+    bands, row_blocks, columns, slab_planes, comps = packed.shape[:5]
+    heap, nproj, cells = share_ref.shape
+    band, anchor = lax.axis_index("band"), lax.axis_index("slab") * SLAB_PLANES
+    fetch = pltpu.make_async_copy(
+        projectors_ref.at[pl.ds(band * heap, heap)], share_ref, fetch_sem.at[0]
+    )
+    fetch.start()
+    fetch_order = pltpu.make_async_copy(order_ref, order, fetch_sem.at[1])
+    count = in_sem.shape[0]
+    step = row_blocks // count
+    loads, stores = [], []
+    for i in range(count):
+        lines = slice(i * step * 16, (i + 1) * step * 16)
+        at = slice(i * step, (i + 1) * step)
+        loads.append(pltpu.make_async_copy(wave_ref.at[:, lines], field.at[:, lines], in_sem.at[i]))
+        stores.append(pltpu.make_async_copy(packed.at[:, at], send_ref.at[:, at], out_sem.at[i]))
+        loads[i].start()
+    fetch_order.start()
+    fetch.wait()
+
     lane = lax.broadcasted_iota(jnp.int32, (nproj, LANES), 1)
     for a in range(heap):
         values = share_ref[a].astype(F32)
@@ -381,6 +369,19 @@
             at = (m // BOX, slice(m % BOX * nproj, (m % BOX + 1) * nproj))
             dense[at] = jnp.where(mine, source, dense[at] if a else 0.0)
 
+    for i in range(count):
+        loads[i].wait()
+        for r in range(i * step, (i + 1) * step):
+            for b in range(bands):
+                for c in range(comps):
+                    for z in range(slab_planes):
+                        plane = (b * comps + c) * slab_planes + z
+                        for h in range(columns):
+                            packed[b, r, h, z, c] = field[
+                                plane, r * 16 : (r + 1) * 16, h * LANES : (h + 1) * LANES
+                            ]
+        stores[i].start()
+
     lane = lax.broadcasted_iota(jnp.int32, (1, LANES), 1)
     offset = jnp.zeros((1, LANES), jnp.int32)
     row0 = jnp.zeros((1, LANES), jnp.int32)
@@ -400,6 +401,7 @@
     ).astype(BF16)
 
     rows = nproj * SLAB_PLANES * BOX
+    fetch_order.wait()
     for d in range(len(out_refs)):
         planes = []
         for z in range(SLAB_PLANES):
@@ -410,34 +412,69 @@
                     framed = jnp.where(offset == o, dense[f - o], framed)
             planes.append(framed)
         planes = jnp.concatenate(planes, axis=0).astype(BF16)
-        out_refs[d][0:rows, :] = dot(order_ref[...], planes).astype(BF16)
-        out_refs[d][rows : rows + PAD, :] = facts
-
-
-def frame(where, projectors, atom_box, atom_count):
+        done[d, 0:rows, :] = dot(order[...], planes).astype(BF16)
+        done[d, rows : rows + PAD, :] = facts
+        stores.append(
+            pltpu.make_async_copy(done.at[d], out_refs[d].at[0 : rows + PAD], done_sem.at[d])
+        )
+        stores[-1].start()
+    for store in stores:
+        store.wait()
+
+
+def frame(projectors, atom_box, atom_count, wave, bands):
     _, nproj, cells = projectors.shape
+    planes, length, _ = wave.shape
+    comps = planes // SLAB_PLANES // bands
     reach = (BOX + SLAB_PLANES) // SLAB_PLANES
     order = gather_rows(nproj)
-    shape = (nproj * SLAB_PLANES * BOX + PAD, LANES)
+    rows = nproj * SLAB_PLANES * BOX + PAD
+    shape = jax.ShapeDtypeStruct((rows, LANES), BF16)
+    send = (bands, length // 16, length // LANES, SLAB_PLANES, comps, 16, LANES)
+    count = 4
     return pl.pallas_call(
         frame_kernel,
-        out_shape=(jax.ShapeDtypeStruct(shape, BF16),) * reach,
-        grid_spec=pltpu.PrefetchScalarGridSpec(
-            num_scalar_prefetch=3,
-            grid=(1,),
-            in_specs=[
-                pl.BlockSpec((HEAP, nproj, cells), lambda i, where, box, count: (where[0], 0, 0)),
-                whole(),
-            ],
-            out_specs=(pl.BlockSpec(shape, lambda i, where, box, count: (0, 0)),) * reach,
-            scratch_shapes=[pltpu.VMEM((BOX, nproj * BOX, LANES), F32)],
-        ),
+        out_shape=(
+            jax.ShapeDtypeStruct(send, BF16),
+            jax.ShapeDtypeStruct((reach * rows, LANES), BF16),
+        )
+        + (shape,) * (reach - 1),
+        in_specs=[whole(pltpu.SMEM)] * 2 + [whole(pltpu.HBM)] * 3,
+        out_specs=(whole(pltpu.HBM),) * (1 + reach),
+        scratch_shapes=[
+            pltpu.VMEM((BOX, nproj * BOX, LANES), F32),
+            pltpu.VMEM((HEAP, nproj, cells), BF16),
+            pltpu.VMEM(order.shape, BF16),
+            pltpu.VMEM((reach, rows, LANES), BF16),
+            pltpu.VMEM(wave.shape, BF16),
+            pltpu.VMEM(send, BF16),
+            pltpu.SemaphoreType.DMA((2,)),
+            pltpu.SemaphoreType.DMA((count,)),
+            pltpu.SemaphoreType.DMA((count,)),
+            pltpu.SemaphoreType.DMA((reach,)),
+        ],
         compiler_params=pltpu.CompilerParams(vmem_limit_bytes=VMEM_MOST),
         cost_estimate=pl.CostEstimate(
-            flops=1_000_000_000, bytes_accessed=1_000_000, transcendentals=0
+            flops=1_000_000_000, bytes_accessed=9_000_000, transcendentals=0
         ),
         name="frame",
-    )(where, atom_box, atom_count, projectors, order)
+    )(atom_box, atom_count, projectors, order, wave)
+
+
+def gate_kernel(*refs):
+    pass
+
+
+def gate(block, after):
+    return pl.pallas_call(
+        gate_kernel,
+        out_shape=jax.ShapeDtypeStruct(block.shape, block.dtype),
+        in_specs=[whole(pltpu.HBM)] + [whole(pl.ANY)] * len(after),
+        out_specs=whole(pltpu.HBM),
+        input_output_aliases={0: 0},
+        compiler_params=pltpu.CompilerParams(vmem_limit_bytes=VMEM_MOST),
+        name="gate",
+    )(block, *after)
 
 
 def join_kernel(local_ref, arrived_ref, out_ref, near, here, there, near_sem, in_sem, out_sem):
@@ -505,18 +542,19 @@
     slabs = lax.axis_size("slab")
     heaps = lax.axis_size("band")
     nproj = projectors.shape[1]
-    high, low = kinetic_table(length)
+    table = kinetic_table(length)
     wave = wavefunctions.reshape(planes, length, length)
 
-    where = jnp.stack([lax.axis_index("band"), lax.axis_index("slab")]).astype(jnp.int32)
-    framed = frame(where, projectors, atom_box, atom_count)
-    reach = len(framed)
-    arrived = [framed[0]] + [ahead(framed[d], d) for d in range(1, reach)]
-
-    send = pack(wave, bands, arrived[1]).reshape(slabs, slab_planes * comps, 16, LANES)
+    send, cargo, *framed = frame(projectors, atom_box, atom_count, wave, bands)
+    reach = len(framed) + 1
+    arrived = [ahead(framed[d - 1], d) for d in range(1, reach)]
+
+    send = gate(send, arrived[:1]).reshape(slabs, slab_planes * comps, 16, LANES)
     columns = lax.all_to_all(send, "slab", split_axis=0, concat_axis=0, tiled=True)
 
-    cargo = jnp.concatenate(arrived, axis=0)
+    rows = arrived[0].shape[0]
+    for d in range(1, reach):
+        cargo = lax.dynamic_update_slice_in_dim(cargo, arrived[d - 1], d * rows, 0)
     cargo = [cargo] + [ahead(cargo, -r, "band") for r in range(1, heaps)]
     well = potential.astype(BF16).reshape(slab_planes, length // heaps, 2, LANES)
     well = well.transpose(2, 0, 1, 3).reshape(-1, LANES)
@@ -524,7 +562,7 @@
 
     partial = project(wave, cargo, reach, nproj)
     other = lax.ppermute(partial, "slab", [(i, i ^ 1) for i in range(slabs)])
-    even = where[1] % 2 == 0
+    even = lax.axis_index("slab") % 2 == 0
     pair = jnp.stack([jnp.where(even, partial, other), jnp.where(even, other, partial)])
     above = ahead(pair, -2)
     below = ahead(pair, 2)
@@ -539,8 +577,8 @@
     ).reshape(heaps * nproj * parts, heaps * nproj * parts)
 
     exchanged = [partial, pair, above, below, far]
-    columns, token = along_z(high, low, columns.reshape(length, comps, 16, LANES), exchanged[2:])
-    local = local_part(where, mix, high, low, wave, cargo, wells, exchanged, token, nproj)
+    columns, token = along_z(table, columns.reshape(length, comps, 16, LANES), exchanged[2:])
+    local = local_part(mix, table, wave, cargo, wells, exchanged, token, nproj)
     columns = columns.reshape(slabs, slab_planes * comps, 16, LANES)
     back = lax.all_to_all(columns, "slab", split_axis=0, concat_axis=0, tiled=True)
     back = back.reshape(bands, length // 16, length // LANES, slab_planes, comps, 16, LANES)

time: 148 us -> 142 us (0.959)
  local copies, waits for them, and re-layouts: 16.5 us -> 12.7 us
  Pallas kernels: 38.4 us -> 35.4 us
    unnamed x50 -> x21, local copies, waits for them, and re-layouts: 13.2 us -> 7.49 us
    all_to_all x1, waiting for transfers between devices: 16.8 us -> 22.1 us  [shards(): lax.all_to_all(columns, 'slab', split_axis=0, concat_axis=0, tiled=True)]
    ppermute x1, waiting for transfers between devices: 10.1 us -> 5.54 us  [shards(): lax.ppermute(partial, 'slab', [(i, (i + 3 if i % 2 else i - 3) % slabs) f...]
    pallas_call x1, Pallas kernels: 4.81 us -> 1.54 us  [along_z(): pl.pallas_call(along_z_kernel, out_shape=(jax.ShapeDtypeStruct(block.shap...]
    dynamic_update_slice x0 -> x3, local copies, waits for them, and re-layouts: none -> 1.96 us  [shards(): cargo = lax.dynamic_update_slice_in_dim(cargo, arrived[d - 1], d * rows, 0)]
  transfers between devices with their start and end apart: 15 -> 15, of which waited for: 7 -> 7; matrix products, arithmetic and copies ran while one was open for 4% -> 5% of each run, Pallas kernels for 18% -> 19%
where the time goes in v4:
time: 142 us; the launch traced here: 141 us
  waiting for transfers between devices  48.5 us (34%)
  starting transfers between devices  42.2 us (30%)
  Pallas kernels  35.4 us (25%)
  local copies, waits for them, and re-layouts  12.7 us (9%)
  other arithmetic  1.77 us (1%)
    all_to_all x1, waiting for transfers between devices, shards(): lax.all_to_all(columns, 'slab', split_axis=0, concat_axis=0, tiled=True)  22.1 us
    ppermute x11, starting transfers between devices, ahead(): lax.ppermute(block, axis, [(i, (i + distance) % size) for i in range(size)])  21.4 us
    ppermute x11, waiting for transfers between devices, ahead(): lax.ppermute(block, axis, [(i, (i + distance) % size) for i in range(size)])  18.9 us
    pallas_call x1, Pallas kernels, local_part(): pl.pallas_call(functools.partial(local_kernel, heaps=heaps, reach=reach,...  16 us
    all_to_all x1, starting transfers between devices, shards(): lax.all_to_all(send, 'slab', split_axis=0, concat_axis=0, tiled=True)  12.9 us
    pallas_call x1, Pallas kernels, project(): pl.pallas_call(functools.partial(project_kernel, heaps=heaps, reach=reach...  10.2 us
    unnamed x21, local copies, waits for them, and re-layouts  7.49 us
    all_to_all x1, starting transfers between devices, shards(): lax.all_to_all(columns, 'slab', split_axis=0, concat_axis=0, tiled=True)  6.57 us
  transfers between devices with their start and end apart: 15, of which 7 were waited for; matrix products, arithmetic and copies ran while one was open for 5% of the time, Pallas kernels for 19%

profile of v4, /device:TPU:1, one launch (start us, length us, event | category | flops | bytes accessed | tf_op | source)
XLA Modules:
  0.0 141.5 jit_solution(8899668097058294265)
XLA Ops:
  0.7 4.3 %frame.1 = (bf16[2,16,2,4,2,16,128]{6,5,4,3,2,1,0:T(8,128)(2,1)}, bf16[1600,128]{1,0:T(8,128)(2,1)}, bf16[400,128]{1,0:T(8,128)(2,1)}, bf16[400,128]{1,0:T(8,128)(2,1)}, bf16[400,128]{1,0:T(8,128)(2,1)}) custom-call(s32[3,32]{1,0:T(4,128)} %box_ref.1, s32[1]{0:T(128)S(6)} %copy.23.count_ref, bf16[32,8,1728]{2,1,0:T(8,128)(2,1)} %projectors_ref.1, ...), custom_call_target="tpu_custom_call" | custom-call | flops 1000000000 | bytes 9000000 | tf_op jit(solution)/shard_map/frame/pallas_call | solution.py:435
  4.9 3.1 %collective-permute-start = (bf16[400,128]{1,0:T(8,128)(2,1)}, bf16[400,128]{1,0:T(8,128)(2,1)S(1)}, u32[]{:S(2)}, u32[]{:S(2)}) collective-permute-start(bf16[400,128]{1,0:T(8,128)(2,1)} %get-tuple-element.13), channel_id=1, source_target_pairs={{0,4},{4,8},{8,12},{12,16},{16,20},{20,24},{24,28},{28,32},{32,36}... | collective-permute-start | bytes 307208 | tf_op jit(solution)/shard_map/ppermute | solution.py:535
  8.0 1.6 %collective-permute-start.1 = (bf16[400,128]{1,0:T(8,128)(2,1)}, bf16[400,128]{1,0:T(8,128)(2,1)S(1)}, u32[]{:S(2)}, u32[]{:S(2)}) collective-permute-start(bf16[400,128]{1,0:T(8,128)(2,1)} %get-tuple-element.14), channel_id=1, source_target_pairs={{0,8},{4,12},{8,16},{12,20},{16,24},{20,28},{24,32},{28,36},{32,40... | collective-permute-start | bytes 307208 | tf_op jit(solution)/shard_map/ppermute | solution.py:535
  9.7 1.7 %collective-permute-start.2 = (bf16[400,128]{1,0:T(8,128)(2,1)}, bf16[400,128]{1,0:T(8,128)(2,1)S(1)}, u32[]{:S(2)}, u32[]{:S(2)}) collective-permute-start(bf16[400,128]{1,0:T(8,128)(2,1)} %get-tuple-element.15), channel_id=1, source_target_pairs={{0,12},{4,16},{8,20},{12,24},{16,28},{20,32},{24,36},{28,40},{32,4... | collective-permute-start | bytes 307208 | tf_op jit(solution)/shard_map/ppermute | solution.py:535
  11.4 0.0 collective-permute-done.refs_1_
  11.4 0.0 copy-start.6
  11.4 0.6 copy-done.6
  12.0 0.0 copy-start.7
  12.0 12.9 %all-to-all-start = ((bf16[64,8,16,128]{3,2,1,0:T(8,128)(2,1)}), bf16[64,8,16,128]{3,2,1,0:T(8,128)(2,1)S(1)}, u32[]{:S(2)}, u32[]{:S(2)}) async-start(bf16[64,8,16,128]{3,2,1,0:T(8,128)(2,1)} %bitcast.35), calls=%async_computation | async-start | bytes 4194304 | tf_op jit(solution)/shard_map/all_to_all | solution.py:553
  24.9 0.0 copy-done.7
  24.9 0.6 constant_dynamic-update-slice_fusion.2
  25.6 0.0 collective-permute-done.1
  25.6 0.7 constant_dynamic-update-slice_fusion.1
  26.2 0.0 collective-permute-done.2
  26.2 0.7 constant_dynamic-update-slice_fusion.refs_0_
  26.9 1.2 collective-permute-start.5
  28.1 2.5 %collective-permute-start.4 = (bf16[1600,128]{1,0:T(8,128)(2,1)}, bf16[1600,128]{1,0:T(8,128)(2,1)S(1)}, u32[]{:S(2)}, u32[]{:S(2)}) collective-permute-start(bf16[1600,128]{1,0:T(8,128)(2,1)} %constant_dynamic-update-slice_fusion.refs_0_), channel_id=1, source_target_pairs={{0,2},{1,3},{2,0},{3,1},{4,6},{5,7},{6,4},{7,5},{8,10},{9,11},{10,... | collective-permute-start | bytes 1228808 | tf_op jit(solution)/shard_map/ppermute | solution.py:535
  30.6 1.2 collective-permute-start.3
  31.7 7.2 %collective-permute-done.5.refs_3_ = bf16[1600,128]{1,0:T(8,128)(2,1)S(1)} collective-permute-done((bf16[1600,128]{1,0:T(8,128)(2,1)}, bf16[1600,128]{1,0:T(8,128)(2,1)S(1)}, u32[]{:S(2)}, u32[]{:S(2)}) %collective-permute-start.5) | collective-permute-done | bytes 409632 | tf_op jit(solution)/shard_map/ppermute | solution.py:535
  38.9 9.8 %collective-permute-done.4.refs_2_ = bf16[1600,128]{1,0:T(8,128)(2,1)S(1)} collective-permute-done((bf16[1600,128]{1,0:T(8,128)(2,1)}, bf16[1600,128]{1,0:T(8,128)(2,1)S(1)}, u32[]{:S(2)}, u32[]{:S(2)}) %collective-permute-start.4) | collective-permute-done | bytes 409632 | tf_op jit(solution)/shard_map/ppermute | solution.py:535
  48.7 0.0 collective-permute-done.3.refs_1_
  48.7 0.0 copy-start.2
  48.7 1.6 %copy-done.2 = bf16[2,2,4,256,256]{4,3,2,1,0:T(8,128)(2,1)S(1)} copy-done((bf16[2,2,4,256,256]{4,3,2,1,0:T(8,128)(2,1)S(1)}, bf16[2,2,4,256,256]{4,3,2,1,0:T(8,128)(2,1)}, u32[]{:S(2)}) %copy-start.2) | copy-done | bytes 2097176
  50.3 10.2 %project.1.refs_8_ = f32[4,8,128]{2,1,0:T(8,128)S(1)} custom-call(bf16[16,256,256]{2,1,0:T(8,128)(2,1)S(1)} %bitcast.33, bf16[1600,128]{1,0:T(8,128)(2,1)} %constant_dynamic-update-slice_fusion.refs_0_, bf16[1600,128]{1,0:T(8,128)(2,1)S(1)} %collective-permute-done.3.refs_1_, bf16[1600,128]{1,0:T(8,128)(2,1)S(1)} %collective-permute-done.4.refs_2_, ...), custom_call_target="tpu_custom_call" | custom-call | flops 32999999488 | bytes 5000000 | tf_op jit(solution)/shard_map/project/pallas_call | solution.py:187
  60.5 1.4 collective-permute-start.9
  61.8 0.8 collective-permute-done.9
  62.7 1.5 %collective-permute-start.11 = (f32[2,4,8,128]{3,2,1,0:T(8,128)S(1)}, f32[2,4,8,128]{3,2,1,0:T(8,128)S(1)}, u32[]{:S(2)}, u32[]{:S(2)}) collective-permute-start(f32[2,4,8,128]{3,2,1,0:T(8,128)S(1)} %pad_maximum_fusion.refs_9_), channel_id=1, source_target_pairs={{0,8},{4,12},{8,16},{12,20},{16,24},{20,28},{24,32},{28,36},{32,40... | collective-permute-start | bytes 98312 | tf_op jit(solution)/shard_map/ppermute | solution.py:535
  64.2 3.7 %collective-permute-start.10 = (f32[2,4,8,128]{3,2,1,0:T(8,128)S(1)}, f32[2,4,8,128]{3,2,1,0:T(8,128)S(1)}, u32[]{:S(2)}, u32[]{:S(2)}) collective-permute-start(f32[2,4,8,128]{3,2,1,0:T(8,128)S(1)} %pad_maximum_fusion.refs_9_), channel_id=1, source_target_pairs={{0,248},{4,252},{8,0},{12,4},{16,8},{20,12},{24,16},{28,20},{32,24... | collective-permute-start | bytes 98312 | tf_op jit(solution)/shard_map/ppermute | solution.py:535
  67.9 0.0 collective-permute-start.12
  67.9 5.5 %collective-permute-done.12.refs_2_.refs_12_ = f32[4,8,128]{2,1,0:T(8,128)S(1)} collective-permute-done((f32[4,8,128]{2,1,0:T(8,128)S(1)}, f32[4,8,128]{2,1,0:T(8,128)S(1)}, u32[]{:S(2)}, u32[]{:S(2)}) %collective-permute-start.12) | collective-permute-done | bytes 16416 | tf_op jit(solution)/shard_map/ppermute | solution.py:569
  73.4 1.9 %collective-permute-done.11.refs_1_.refs_11_ = f32[2,4,8,128]{3,2,1,0:T(8,128)S(1)} collective-permute-done((f32[2,4,8,128]{3,2,1,0:T(8,128)S(1)}, f32[2,4,8,128]{3,2,1,0:T(8,128)S(1)}, u32[]{:S(2)}, u32[]{:S(2)}) %collective-permute-start.11) | collective-permute-done | bytes 32800 | tf_op jit(solution)/shard_map/ppermute | solution.py:535
  75.3 0.0 collective-permute-done.10.refs_0_.refs_10_
  75.3 1.0 all-to-all-done
  76.4 0.0 copy-start.4
  76.4 0.9 copy-done.4
  77.3 1.5 %along_z.1 = (bf16[256,2,16,128]{3,2,1,0:T(8,128)(2,1)S(1)}, f32[8,128]{1,0:T(8,128)S(1)}) custom-call(bf16[2,256,256]{2,1,0:T(8,128)(2,1)S(1)} %copy-done.4, bf16[256,2,16,128]{3,2,1,0:T(8,128)(2,1)S(1)} %bitcast.26, f32[2,4,8,128]{3,2,1,0:T(8,128)S(1)} %collective-permute-done.10.refs_0_.refs_10_, ...), custom_call_target="tpu_custom_call" | custom-call | flops 1073741824 | bytes 4194304 | tf_op jit(solution)/shard_map/along_z/pallas_call | solution.py:70
  78.9 0.0 copy-start.1
  78.9 1.3 copy-done.1
  80.2 0.0 copy-start.8
  80.2 0.0 copy-start.9
  80.2 6.6 %all-to-all-start.1 = ((bf16[64,8,16,128]{3,2,1,0:T(8,128)(2,1)}), bf16[64,8,16,128]{3,2,1,0:T(8,128)(2,1)}, u32[]{:S(2)}, u32[]{:S(2)}) async-start(bf16[64,8,16,128]{3,2,1,0:T(8,128)(2,1)} %bitcast.27), calls=%async_computation.1 | async-start | bytes 4194304 | tf_op jit(solution)/shard_map/all_to_all | solution.py:583
  86.8 0.0 copy-done.8
  86.8 1.3 collective-permute-start.8
  88.1 2.5 %collective-permute-start.7 = (bf16[512,128]{1,0:T(8,128)(2,1)S(1)}, bf16[512,128]{1,0:T(8,128)(2,1)S(1)}, u32[]{:S(2)}, u32[]{:S(2)}) collective-permute-start(bf16[512,128]{1,0:T(8,128)(2,1)S(1)} %bitcast.29), channel_id=1, source_target_pairs={{0,2},{1,3},{2,0},{3,1},{4,6},{5,7},{6,4},{7,5},{8,10},{9,11},{10,... | collective-permute-start | bytes 393224 | tf_op jit(solution)/shard_map/ppermute | solution.py:535
  90.6 1.1 collective-permute-start.6
  91.7 0.0 copy-done.9
  91.7 0.1 copy.14
  91.8 0.1 copy.15
  91.9 0.1 broadcast_multiply_fusion
  91.9 0.0 copy-start.5
  92.0 1.7 %multiply_bitcast_fusion = f32[4,8,4,4,8,4]{5,4,3,2,1,0:T(8,128)} fusion(f32[8,8]{0,1:T(8,128)S(1)} %copy.15, f32[4,4,4,4]{1,3,0,2:T(4,128)S(1)} %broadcast_multiply_fusion), kind=kLoop, calls=%fused_computation | loop fusion | flops 16384 | bytes 66816 | tf_op jit(solution)/shard_map/gh,pq,bc->gqbhpc/transpose | solution.py:574
  93.6 3.2 %reshape.27.mix_ref = f32[128,128]{1,0:T(8,128)S(1)} reshape(f32[4,8,4,4,8,4]{5,4,3,2,1,0:T(8,128)} %multiply_bitcast_fusion) | data formatting | bytes 131072 | tf_op jit(solution)/shard_map/reshape | solution.py:577
  96.8 0.0 collective-permute-done.8.refs_7_
  96.8 0.0 collective-permute-done.7.refs_6_
  96.8 0.0 collective-permute-done.6.refs_5_
  96.8 0.0 copy-done.5
  96.8 0.0 copy-start.3
  96.9 1.6 %copy-done.3 = bf16[2,2,4,256,256]{4,3,2,1,0:T(8,128)(2,1)S(1)} copy-done((bf16[2,2,4,256,256]{4,3,2,1,0:T(8,128)(2,1)S(1)}, bf16[2,2,4,256,256]{4,3,2,1,0:T(8,128)(2,1)}, u32[]{:S(2)}) %copy-start.3) | copy-done | bytes 2097176
  98.4 16.0 %local.1.local_ref = bf16[16,256,256]{2,1,0:T(8,128)(2,1)S(1)} custom-call(f32[128,128]{1,0:T(8,128)S(1)} %reshape.27.mix_ref, bf16[2,256,256]{2,1,0:T(8,128)(2,1)S(1)} %copy-done.5, bf16[16,256,256]{2,1,0:T(8,128)(2,1)S(1)} %bitcast.34, bf16[1600,128]{1,0:T(8,128)(2,1)} %constant_dynamic-update-slice_fusion.refs_0_, ...), custom_call_target="tpu_custom_call" | custom-call | flops 10000000000 | bytes 10000000 | tf_op jit(solution)/shard_map/local/pallas_call | solution.py:299
  114.4 0.0 copy-start
  114.4 1.4 copy-done
  115.8 22.1 %all-to-all-done.1 = bf16[64,8,16,128]{3,2,1,0:T(8,128)(2,1)} async-done(((bf16[64,8,16,128]{3,2,1,0:T(8,128)(2,1)}), bf16[64,8,16,128]{3,2,1,0:T(8,128)(2,1)}, u32[]{:S(2)}, u32[]{:S(2)}) %all-to-all-start.1) | async-done | bytes 2097184 | tf_op jit(solution)/shard_map/all_to_all | solution.py:583
  137.9 3.4 %join.1 = bf16[16,256,256]{2,1,0:T(8,128)(2,1)} custom-call(bf16[16,256,256]{2,1,0:T(8,128)(2,1)} %copy-done, bf16[2,16,2,4,2,16,128]{6,5,4,3,2,1,0:T(8,128)(2,1)} %bitcast.11.arrived_ref), custom_call_target="tpu_custom_call" | custom-call | flops 2097152 | bytes 6291456 | tf_op jit(solution)/shard_map/join/pallas_call | solution.py:512
  (6 shorter events, 0.0 us)
Async XLA Ops:
  4.9 6.5 %collective-permute-start = (bf16[400,128]{1,0:T(8,128)(2,1)}, bf16[400,128]{1,0:T(8,128)(2,1)S(1)}, u32[]{:S(2)}, u32[]{:S(2)}) collective-permute-start(bf16[400,128]{1,0:T(8,128)(2,1)} %get-tuple-element.13), channel_id=1, source_target_pairs={{0,4},{4,8},{8,12},{12,16},{16,20},{20,24},{24,28},{28,32},{32,36}... | collective-permute-start | bytes 307208 | tf_op jit(solution)/shard_map/ppermute | solution.py:535
  8.0 17.5 %collective-permute-start.1 = (bf16[400,128]{1,0:T(8,128)(2,1)}, bf16[400,128]{1,0:T(8,128)(2,1)S(1)}, u32[]{:S(2)}, u32[]{:S(2)}) collective-permute-start(bf16[400,128]{1,0:T(8,128)(2,1)} %get-tuple-element.14), channel_id=1, source_target_pairs={{0,8},{4,12},{8,16},{12,20},{16,24},{20,28},{24,32},{28,36},{32,40... | collective-permute-start | bytes 307208 | tf_op jit(solution)/shard_map/ppermute | solution.py:535
  9.7 16.6 %collective-permute-start.2 = (bf16[400,128]{1,0:T(8,128)(2,1)}, bf16[400,128]{1,0:T(8,128)(2,1)S(1)}, u32[]{:S(2)}, u32[]{:S(2)}) collective-permute-start(bf16[400,128]{1,0:T(8,128)(2,1)} %get-tuple-element.15), channel_id=1, source_target_pairs={{0,12},{4,16},{8,20},{12,24},{16,28},{20,32},{24,36},{28,40},{32,4... | collective-permute-start | bytes 307208 | tf_op jit(solution)/shard_map/ppermute | solution.py:535
  11.4 0.6 copy-start.6
  12.0 12.9 %copy-start.7 = (bf16[400,128]{1,0:T(8,128)(2,1)S(1)}, bf16[400,128]{1,0:T(8,128)(2,1)}, u32[]{:S(2)}) copy-start(bf16[400,128]{1,0:T(8,128)(2,1)} %copy-done.6) | copy-start | bytes 307204
  12.0 64.4 %all-to-all-start = ((bf16[64,8,16,128]{3,2,1,0:T(8,128)(2,1)}), bf16[64,8,16,128]{3,2,1,0:T(8,128)(2,1)S(1)}, u32[]{:S(2)}, u32[]{:S(2)}) async-start(bf16[64,8,16,128]{3,2,1,0:T(8,128)(2,1)} %bitcast.35), calls=%async_computation | async-start | bytes 4194304 | tf_op jit(solution)/shard_map/all_to_all | solution.py:553
  26.9 12.0 %collective-permute-start.5 = (bf16[1600,128]{1,0:T(8,128)(2,1)}, bf16[1600,128]{1,0:T(8,128)(2,1)S(1)}, u32[]{:S(2)}, u32[]{:S(2)}) collective-permute-start(bf16[1600,128]{1,0:T(8,128)(2,1)} %constant_dynamic-update-slice_fusion.refs_0_), channel_id=1, source_target_pairs={{0,1},{1,2},{2,3},{3,0},{4,5},{5,6},{6,7},{7,4},{8,9},{9,10},{10,1... | collective-permute-start | bytes 1228808 | tf_op jit(solution)/shard_map/ppermute | solution.py:535
  28.1 20.6 %collective-permute-start.4 = (bf16[1600,128]{1,0:T(8,128)(2,1)}, bf16[1600,128]{1,0:T(8,128)(2,1)S(1)}, u32[]{:S(2)}, u32[]{:S(2)}) collective-permute-start(bf16[1600,128]{1,0:T(8,128)(2,1)} %constant_dynamic-update-slice_fusion.refs_0_), channel_id=1, source_target_pairs={{0,2},{1,3},{2,0},{3,1},{4,6},{5,7},{6,4},{7,5},{8,10},{9,11},{10,... | collective-permute-start | bytes 1228808 | tf_op jit(solution)/shard_map/ppermute | solution.py:535
  30.6 18.1 %collective-permute-start.3 = (bf16[1600,128]{1,0:T(8,128)(2,1)}, bf16[1600,128]{1,0:T(8,128)(2,1)S(1)}, u32[]{:S(2)}, u32[]{:S(2)}) collective-permute-start(bf16[1600,128]{1,0:T(8,128)(2,1)} %constant_dynamic-update-slice_fusion.refs_0_), channel_id=1, source_target_pairs={{0,3},{1,0},{2,1},{3,2},{4,7},{5,4},{6,5},{7,6},{8,11},{9,8},{10,9... | collective-permute-start | bytes 1228808 | tf_op jit(solution)/shard_map/ppermute | solution.py:535
  48.7 1.6 %copy-start.2 = (bf16[2,2,4,256,256]{4,3,2,1,0:T(8,128)(2,1)S(1)}, bf16[2,2,4,256,256]{4,3,2,1,0:T(8,128)(2,1)}, u32[]{:S(2)}) copy-start(bf16[2,2,4,256,256]{4,3,2,1,0:T(8,128)(2,1)} %param.9) | copy-start | bytes 6291460
  60.5 2.2 %collective-permute-start.9 = (f32[4,8,128]{2,1,0:T(8,128)S(1)}, f32[4,8,128]{2,1,0:T(8,128)S(1)}, u32[]{:S(2)}, u32[]{:S(2)}) collective-permute-start(f32[4,8,128]{2,1,0:T(8,128)S(1)} %project.1.refs_8_), channel_id=1, source_target_pairs={{0,4},{4,0},{8,12},{12,8},{16,20},{20,16},{24,28},{28,24},{32,36},... | collective-permute-start | bytes 49160 | tf_op jit(solution)/shard_map/ppermute | solution.py:564
  62.7 12.7 %collective-permute-start.11 = (f32[2,4,8,128]{3,2,1,0:T(8,128)S(1)}, f32[2,4,8,128]{3,2,1,0:T(8,128)S(1)}, u32[]{:S(2)}, u32[]{:S(2)}) collective-permute-start(f32[2,4,8,128]{3,2,1,0:T(8,128)S(1)} %pad_maximum_fusion.refs_9_), channel_id=1, source_target_pairs={{0,8},{4,12},{8,16},{12,20},{16,24},{20,28},{24,32},{28,36},{32,40... | collective-permute-start | bytes 98312 | tf_op jit(solution)/shard_map/ppermute | solution.py:535
  64.2 11.2 %collective-permute-start.10 = (f32[2,4,8,128]{3,2,1,0:T(8,128)S(1)}, f32[2,4,8,128]{3,2,1,0:T(8,128)S(1)}, u32[]{:S(2)}, u32[]{:S(2)}) collective-permute-start(f32[2,4,8,128]{3,2,1,0:T(8,128)S(1)} %pad_maximum_fusion.refs_9_), channel_id=1, source_target_pairs={{0,248},{4,252},{8,0},{12,4},{16,8},{20,12},{24,16},{28,20},{32,24... | collective-permute-start | bytes 98312 | tf_op jit(solution)/shard_map/ppermute | solution.py:535
  67.9 5.5 %collective-permute-start.12 = (f32[4,8,128]{2,1,0:T(8,128)S(1)}, f32[4,8,128]{2,1,0:T(8,128)S(1)}, u32[]{:S(2)}, u32[]{:S(2)}) collective-permute-start(f32[4,8,128]{2,1,0:T(8,128)S(1)} %project.1.refs_8_), channel_id=1, source_target_pairs={{0,244},{4,16},{8,252},{12,24},{16,4},{20,32},{24,12},{28,40},{32,... | collective-permute-start | bytes 49160 | tf_op jit(solution)/shard_map/ppermute | solution.py:569
  76.4 1.0 copy-start.4
  78.9 1.3 copy-start.1
  80.2 6.6 %copy-start.8 = (f32[4,64,256]{2,1,0:T(8,128)S(1)}, f32[4,64,256]{2,1,0:T(8,128)}, u32[]{:S(2)}) copy-start(f32[4,64,256]{2,1,0:T(8,128)} %param.10) | copy-start | bytes 786436
  80.2 11.5 %copy-start.9 = (f32[8,8]{1,0:T(8,128)S(1)}, f32[8,8]{1,0:T(8,128)}, u32[]{:S(2)}) copy-start(f32[8,8]{1,0:T(8,128)} %param.14) | copy-start | bytes 772
  80.2 57.7 %all-to-all-start.1 = ((bf16[64,8,16,128]{3,2,1,0:T(8,128)(2,1)}), bf16[64,8,16,128]{3,2,1,0:T(8,128)(2,1)}, u32[]{:S(2)}, u32[]{:S(2)}) async-start(bf16[64,8,16,128]{3,2,1,0:T(8,128)(2,1)} %bitcast.27), calls=%async_computation.1 | async-start | bytes 4194304 | tf_op jit(solution)/shard_map/all_to_all | solution.py:583
  86.8 10.0 %collective-permute-start.8 = (bf16[512,128]{1,0:T(8,128)(2,1)S(1)}, bf16[512,128]{1,0:T(8,128)(2,1)S(1)}, u32[]{:S(2)}, u32[]{:S(2)}) collective-permute-start(bf16[512,128]{1,0:T(8,128)(2,1)S(1)} %bitcast.28), channel_id=1, source_target_pairs={{0,1},{1,2},{2,3},{3,0},{4,5},{5,6},{6,7},{7,4},{8,9},{9,10},{10,1... | collective-permute-start | bytes 393224 | tf_op jit(solution)/shard_map/ppermute | solution.py:535
  88.1 8.7 %collective-permute-start.7 = (bf16[512,128]{1,0:T(8,128)(2,1)S(1)}, bf16[512,128]{1,0:T(8,128)(2,1)S(1)}, u32[]{:S(2)}, u32[]{:S(2)}) collective-permute-start(bf16[512,128]{1,0:T(8,128)(2,1)S(1)} %bitcast.29), channel_id=1, source_target_pairs={{0,2},{1,3},{2,0},{3,1},{4,6},{5,7},{6,4},{7,5},{8,10},{9,11},{10,... | collective-permute-start | bytes 393224 | tf_op jit(solution)/shard_map/ppermute | solution.py:535
  90.6 6.3 %collective-permute-start.6 = (bf16[512,128]{1,0:T(8,128)(2,1)S(1)}, bf16[512,128]{1,0:T(8,128)(2,1)S(1)}, u32[]{:S(2)}, u32[]{:S(2)}) collective-permute-start(bf16[512,128]{1,0:T(8,128)(2,1)S(1)} %bitcast.30), channel_id=1, source_target_pairs={{0,3},{1,0},{2,1},{3,2},{4,7},{5,4},{6,5},{7,6},{8,11},{9,8},{10,9... | collective-permute-start | bytes 393224 | tf_op jit(solution)/shard_map/ppermute | solution.py:535
  91.9 4.9 %copy-start.5 = (bf16[2,256,256]{2,1,0:T(8,128)(2,1)S(1)}, bf16[2,256,256]{2,1,0:T(8,128)(2,1)}, u32[]{:S(2)}) copy-start(bf16[2,256,256]{2,1,0:T(8,128)(2,1)} %constant.45.table_ref) | copy-start | bytes 786436
  96.8 1.6 %copy-start.3 = (bf16[2,2,4,256,256]{4,3,2,1,0:T(8,128)(2,1)S(1)}, bf16[2,2,4,256,256]{4,3,2,1,0:T(8,128)(2,1)}, u32[]{:S(2)}) copy-start(bf16[2,2,4,256,256]{4,3,2,1,0:T(8,128)(2,1)} %param.9) | copy-start | bytes 6291460
  114.4 1.4 copy-start

commit v5 on v4

--- a/solution.py
+++ b/solution.py
@@ -75,7 +75,7 @@
         ),
         in_specs=[whole()] * 2 + [whole(pl.ANY)] * len(after),
         out_specs=(whole(), whole()),
-        scratch_shapes=[pltpu.VMEM((comps, length * PITCH, LANES), F32)] * 2,
+        scratch_shapes=[pltpu.VMEM((comps, (length + 1) * PITCH, LANES), F32)] * 2,
         compiler_params=pltpu.CompilerParams(vmem_limit_bytes=VMEM_LIMIT),
         cost_estimate=pl.CostEstimate(
             flops=4 * length * block.size, bytes_accessed=4 * block.size, transcendentals=0
@@ -508,7 +508,7 @@
 
 
 def join(local, arrived):
-    count = 8
+    count = 4
     return pl.pallas_call(
         join_kernel,
         out_shape=jax.ShapeDtypeStruct(local.shape, BF16),

time: 142 us -> 142 us (level)
  no operation moved by 1% of the time
where the time goes in v5:
time: 142 us; the launch traced here: 141 us
  waiting for transfers between devices  48.4 us (34%)
  starting transfers between devices  42.2 us (30%)
  Pallas kernels  35.2 us (25%)
  local copies, waits for them, and re-layouts  12.7 us (9%)
  other arithmetic  1.77 us (1%)
    all_to_all x1, waiting for transfers between devices, shards(): lax.all_to_all(columns, 'slab', split_axis=0, concat_axis=0, tiled=True)  22.1 us
    ppermute x11, starting transfers between devices, ahead(): lax.ppermute(block, axis, [(i, (i + distance) % size) for i in range(size)])  21.4 us
    ppermute x11, waiting for transfers between devices, ahead(): lax.ppermute(block, axis, [(i, (i + distance) % size) for i in range(size)])  18.9 us
    pallas_call x1, Pallas kernels, local_part(): pl.pallas_call(functools.partial(local_kernel, heaps=heaps, reach=reach,...  16 us
    all_to_all x1, starting transfers between devices, shards(): lax.all_to_all(send, 'slab', split_axis=0, concat_axis=0, tiled=True)  12.9 us
    pallas_call x1, Pallas kernels, project(): pl.pallas_call(functools.partial(project_kernel, heaps=heaps, reach=reach...  10.2 us
    unnamed x21, local copies, waits for them, and re-layouts  7.49 us
    all_to_all x1, starting transfers between devices, shards(): lax.all_to_all(columns, 'slab', split_axis=0, concat_axis=0, tiled=True)  6.57 us
  transfers between devices with their start and end apart: 15, of which 7 were waited for; matrix products, arithmetic and copies ran while one was open for 5% of the time, Pallas kernels for 19%

profile of v5, /device:TPU:1, one launch (start us, length us, event | category | flops | bytes accessed | tf_op | source)
XLA Modules:
  0.0 141.3 jit_solution(4021757166355910794)
XLA Ops:
  0.7 4.3 %frame.1 = (bf16[2,16,2,4,2,16,128]{6,5,4,3,2,1,0:T(8,128)(2,1)}, bf16[1600,128]{1,0:T(8,128)(2,1)}, bf16[400,128]{1,0:T(8,128)(2,1)}, bf16[400,128]{1,0:T(8,128)(2,1)}, bf16[400,128]{1,0:T(8,128)(2,1)}) custom-call(s32[3,32]{1,0:T(4,128)} %box_ref.1, s32[1]{0:T(128)S(6)} %copy.23.count_ref, bf16[32,8,1728]{2,1,0:T(8,128)(2,1)} %projectors_ref.1, ...), custom_call_target="tpu_custom_call" | custom-call | flops 1000000000 | bytes 9000000 | tf_op jit(solution)/shard_map/frame/pallas_call | solution.py:435
  4.9 3.1 %collective-permute-start = (bf16[400,128]{1,0:T(8,128)(2,1)}, bf16[400,128]{1,0:T(8,128)(2,1)S(1)}, u32[]{:S(2)}, u32[]{:S(2)}) collective-permute-start(bf16[400,128]{1,0:T(8,128)(2,1)} %get-tuple-element.13), channel_id=1, source_target_pairs={{0,4},{4,8},{8,12},{12,16},{16,20},{20,24},{24,28},{28,32},{32,36}... | collective-permute-start | bytes 307208 | tf_op jit(solution)/shard_map/ppermute | solution.py:535
  8.0 1.6 %collective-permute-start.1 = (bf16[400,128]{1,0:T(8,128)(2,1)}, bf16[400,128]{1,0:T(8,128)(2,1)S(1)}, u32[]{:S(2)}, u32[]{:S(2)}) collective-permute-start(bf16[400,128]{1,0:T(8,128)(2,1)} %get-tuple-element.14), channel_id=1, source_target_pairs={{0,8},{4,12},{8,16},{12,20},{16,24},{20,28},{24,32},{28,36},{32,40... | collective-permute-start | bytes 307208 | tf_op jit(solution)/shard_map/ppermute | solution.py:535
  9.7 1.7 %collective-permute-start.2 = (bf16[400,128]{1,0:T(8,128)(2,1)}, bf16[400,128]{1,0:T(8,128)(2,1)S(1)}, u32[]{:S(2)}, u32[]{:S(2)}) collective-permute-start(bf16[400,128]{1,0:T(8,128)(2,1)} %get-tuple-element.15), channel_id=1, source_target_pairs={{0,12},{4,16},{8,20},{12,24},{16,28},{20,32},{24,36},{28,40},{32,4... | collective-permute-start | bytes 307208 | tf_op jit(solution)/shard_map/ppermute | solution.py:535
  11.4 0.0 collective-permute-done.refs_1_
  11.4 0.0 copy-start.6
  11.4 0.6 copy-done.6
  12.0 0.0 copy-start.7
  12.0 12.9 %all-to-all-start = ((bf16[64,8,16,128]{3,2,1,0:T(8,128)(2,1)}), bf16[64,8,16,128]{3,2,1,0:T(8,128)(2,1)S(1)}, u32[]{:S(2)}, u32[]{:S(2)}) async-start(bf16[64,8,16,128]{3,2,1,0:T(8,128)(2,1)} %bitcast.35), calls=%async_computation | async-start | bytes 4194304 | tf_op jit(solution)/shard_map/all_to_all | solution.py:553
  24.9 0.0 copy-done.7
  24.9 0.6 constant_dynamic-update-slice_fusion.2
  25.6 0.0 collective-permute-done.1
  25.6 0.7 constant_dynamic-update-slice_fusion.1
  26.2 0.0 collective-permute-done.2
  26.2 0.7 constant_dynamic-update-slice_fusion.refs_0_
  26.9 1.2 collective-permute-start.5
  28.1 2.5 %collective-permute-start.4 = (bf16[1600,128]{1,0:T(8,128)(2,1)}, bf16[1600,128]{1,0:T(8,128)(2,1)S(1)}, u32[]{:S(2)}, u32[]{:S(2)}) collective-permute-start(bf16[1600,128]{1,0:T(8,128)(2,1)} %constant_dynamic-update-slice_fusion.refs_0_), channel_id=1, source_target_pairs={{0,2},{1,3},{2,0},{3,1},{4,6},{5,7},{6,4},{7,5},{8,10},{9,11},{10,... | collective-permute-start | bytes 1228808 | tf_op jit(solution)/shard_map/ppermute | solution.py:535
  30.6 1.2 collective-permute-start.3
  31.7 7.2 %collective-permute-done.5.refs_3_ = bf16[1600,128]{1,0:T(8,128)(2,1)S(1)} collective-permute-done((bf16[1600,128]{1,0:T(8,128)(2,1)}, bf16[1600,128]{1,0:T(8,128)(2,1)S(1)}, u32[]{:S(2)}, u32[]{:S(2)}) %collective-permute-start.5) | collective-permute-done | bytes 409632 | tf_op jit(solution)/shard_map/ppermute | solution.py:535
  38.9 9.8 %collective-permute-done.4.refs_2_ = bf16[1600,128]{1,0:T(8,128)(2,1)S(1)} collective-permute-done((bf16[1600,128]{1,0:T(8,128)(2,1)}, bf16[1600,128]{1,0:T(8,128)(2,1)S(1)}, u32[]{:S(2)}, u32[]{:S(2)}) %collective-permute-start.4) | collective-permute-done | bytes 409632 | tf_op jit(solution)/shard_map/ppermute | solution.py:535
  48.7 0.0 collective-permute-done.3.refs_1_
  48.7 0.0 copy-start.2
  48.7 1.6 %copy-done.2 = bf16[2,2,4,256,256]{4,3,2,1,0:T(8,128)(2,1)S(1)} copy-done((bf16[2,2,4,256,256]{4,3,2,1,0:T(8,128)(2,1)S(1)}, bf16[2,2,4,256,256]{4,3,2,1,0:T(8,128)(2,1)}, u32[]{:S(2)}) %copy-start.2) | copy-done | bytes 2097176
  50.3 10.2 %project.1.refs_8_ = f32[4,8,128]{2,1,0:T(8,128)S(1)} custom-call(bf16[16,256,256]{2,1,0:T(8,128)(2,1)S(1)} %bitcast.33, bf16[1600,128]{1,0:T(8,128)(2,1)} %constant_dynamic-update-slice_fusion.refs_0_, bf16[1600,128]{1,0:T(8,128)(2,1)S(1)} %collective-permute-done.3.refs_1_, bf16[1600,128]{1,0:T(8,128)(2,1)S(1)} %collective-permute-done.4.refs_2_, ...), custom_call_target="tpu_custom_call" | custom-call | flops 32999999488 | bytes 5000000 | tf_op jit(solution)/shard_map/project/pallas_call | solution.py:187
  60.5 1.4 collective-permute-start.9
  61.9 0.8 collective-permute-done.9
  62.7 1.4 collective-permute-start.11
  64.1 3.8 %collective-permute-start.10 = (f32[2,4,8,128]{3,2,1,0:T(8,128)S(1)}, f32[2,4,8,128]{3,2,1,0:T(8,128)S(1)}, u32[]{:S(2)}, u32[]{:S(2)}) collective-permute-start(f32[2,4,8,128]{3,2,1,0:T(8,128)S(1)} %pad_maximum_fusion.refs_9_), channel_id=1, source_target_pairs={{0,248},{4,252},{8,0},{12,4},{16,8},{20,12},{24,16},{28,20},{32,24... | collective-permute-start | bytes 98312 | tf_op jit(solution)/shard_map/ppermute | solution.py:535
  67.9 0.0 collective-permute-start.12
  67.9 5.5 %collective-permute-done.12.refs_2_.refs_12_ = f32[4,8,128]{2,1,0:T(8,128)S(1)} collective-permute-done((f32[4,8,128]{2,1,0:T(8,128)S(1)}, f32[4,8,128]{2,1,0:T(8,128)S(1)}, u32[]{:S(2)}, u32[]{:S(2)}) %collective-permute-start.12) | collective-permute-done | bytes 16416 | tf_op jit(solution)/shard_map/ppermute | solution.py:569
  73.4 1.9 %collective-permute-done.11.refs_1_.refs_11_ = f32[2,4,8,128]{3,2,1,0:T(8,128)S(1)} collective-permute-done((f32[2,4,8,128]{3,2,1,0:T(8,128)S(1)}, f32[2,4,8,128]{3,2,1,0:T(8,128)S(1)}, u32[]{:S(2)}, u32[]{:S(2)}) %collective-permute-start.11) | collective-permute-done | bytes 32800 | tf_op jit(solution)/shard_map/ppermute | solution.py:535
  75.3 0.0 collective-permute-done.10.refs_0_.refs_10_
  75.3 1.0 all-to-all-done
  76.4 0.0 copy-start.4
  76.4 0.9 copy-done.4
  77.3 1.5 %along_z.1 = (bf16[256,2,16,128]{3,2,1,0:T(8,128)(2,1)S(1)}, f32[8,128]{1,0:T(8,128)S(1)}) custom-call(bf16[2,256,256]{2,1,0:T(8,128)(2,1)S(1)} %copy-done.4, bf16[256,2,16,128]{3,2,1,0:T(8,128)(2,1)S(1)} %bitcast.26, f32[2,4,8,128]{3,2,1,0:T(8,128)S(1)} %collective-permute-done.10.refs_0_.refs_10_, ...), custom_call_target="tpu_custom_call" | custom-call | flops 1073741824 | bytes 4194304 | tf_op jit(solution)/shard_map/along_z/pallas_call | solution.py:70
  78.9 0.0 copy-start.1
  78.9 1.3 copy-done.1
  80.2 0.0 copy-start.8
  80.2 0.0 copy-start.9
  80.2 6.6 %all-to-all-start.1 = ((bf16[64,8,16,128]{3,2,1,0:T(8,128)(2,1)}), bf16[64,8,16,128]{3,2,1,0:T(8,128)(2,1)}, u32[]{:S(2)}, u32[]{:S(2)}) async-start(bf16[64,8,16,128]{3,2,1,0:T(8,128)(2,1)} %bitcast.27), calls=%async_computation.1 | async-start | bytes 4194304 | tf_op jit(solution)/shard_map/all_to_all | solution.py:583
  86.8 0.0 copy-done.8
  86.8 1.3 collective-permute-start.8
  88.1 2.5 %collective-permute-start.7 = (bf16[512,128]{1,0:T(8,128)(2,1)S(1)}, bf16[512,128]{1,0:T(8,128)(2,1)S(1)}, u32[]{:S(2)}, u32[]{:S(2)}) collective-permute-start(bf16[512,128]{1,0:T(8,128)(2,1)S(1)} %bitcast.29), channel_id=1, source_target_pairs={{0,2},{1,3},{2,0},{3,1},{4,6},{5,7},{6,4},{7,5},{8,10},{9,11},{10,... | collective-permute-start | bytes 393224 | tf_op jit(solution)/shard_map/ppermute | solution.py:535
  90.6 1.1 collective-permute-start.6
  91.7 0.0 copy-done.9
  91.7 0.1 copy.14
  91.8 0.1 copy.15
  91.9 0.1 broadcast_multiply_fusion
  92.0 0.0 copy-start.5
  92.0 1.7 %multiply_bitcast_fusion = f32[4,8,4,4,8,4]{5,4,3,2,1,0:T(8,128)} fusion(f32[8,8]{0,1:T(8,128)S(1)} %copy.15, f32[4,4,4,4]{1,3,0,2:T(4,128)S(1)} %broadcast_multiply_fusion), kind=kLoop, calls=%fused_computation | loop fusion | flops 16384 | bytes 66816 | tf_op jit(solution)/shard_map/gh,pq,bc->gqbhpc/transpose | solution.py:574
  93.6 3.2 %reshape.27.mix_ref = f32[128,128]{1,0:T(8,128)S(1)} reshape(f32[4,8,4,4,8,4]{5,4,3,2,1,0:T(8,128)} %multiply_bitcast_fusion) | data formatting | bytes 131072 | tf_op jit(solution)/shard_map/reshape | solution.py:577
  96.8 0.0 collective-permute-done.8.refs_7_
  96.8 0.0 collective-permute-done.7.refs_6_
  96.8 0.0 collective-permute-done.6.refs_5_
  96.8 0.0 copy-done.5
  96.8 0.0 copy-start.3
  96.9 1.6 %copy-done.3 = bf16[2,2,4,256,256]{4,3,2,1,0:T(8,128)(2,1)S(1)} copy-done((bf16[2,2,4,256,256]{4,3,2,1,0:T(8,128)(2,1)S(1)}, bf16[2,2,4,256,256]{4,3,2,1,0:T(8,128)(2,1)}, u32[]{:S(2)}) %copy-start.3) | copy-done | bytes 2097176
  98.4 16.0 %local.1.local_ref = bf16[16,256,256]{2,1,0:T(8,128)(2,1)S(1)} custom-call(f32[128,128]{1,0:T(8,128)S(1)} %reshape.27.mix_ref, bf16[2,256,256]{2,1,0:T(8,128)(2,1)S(1)} %copy-done.5, bf16[16,256,256]{2,1,0:T(8,128)(2,1)S(1)} %bitcast.34, bf16[1600,128]{1,0:T(8,128)(2,1)} %constant_dynamic-update-slice_fusion.refs_0_, ...), custom_call_target="tpu_custom_call" | custom-call | flops 10000000000 | bytes 10000000 | tf_op jit(solution)/shard_map/local/pallas_call | solution.py:299
  114.5 0.0 copy-start
  114.5 1.4 copy-done
  115.8 22.1 %all-to-all-done.1 = bf16[64,8,16,128]{3,2,1,0:T(8,128)(2,1)} async-done(((bf16[64,8,16,128]{3,2,1,0:T(8,128)(2,1)}), bf16[64,8,16,128]{3,2,1,0:T(8,128)(2,1)}, u32[]{:S(2)}, u32[]{:S(2)}) %all-to-all-start.1) | async-done | bytes 2097184 | tf_op jit(solution)/shard_map/all_to_all | solution.py:583
  137.9 3.2 %join.1 = bf16[16,256,256]{2,1,0:T(8,128)(2,1)} custom-call(bf16[16,256,256]{2,1,0:T(8,128)(2,1)} %copy-done, bf16[2,16,2,4,2,16,128]{6,5,4,3,2,1,0:T(8,128)(2,1)} %bitcast.11.arrived_ref), custom_call_target="tpu_custom_call" | custom-call | flops 2097152 | bytes 6291456 | tf_op jit(solution)/shard_map/join/pallas_call | solution.py:512
  (6 shorter events, 0.0 us)
Async XLA Ops:
  4.9 6.5 %collective-permute-start = (bf16[400,128]{1,0:T(8,128)(2,1)}, bf16[400,128]{1,0:T(8,128)(2,1)S(1)}, u32[]{:S(2)}, u32[]{:S(2)}) collective-permute-start(bf16[400,128]{1,0:T(8,128)(2,1)} %get-tuple-element.13), channel_id=1, source_target_pairs={{0,4},{4,8},{8,12},{12,16},{16,20},{20,24},{24,28},{28,32},{32,36}... | collective-permute-start | bytes 307208 | tf_op jit(solution)/shard_map/ppermute | solution.py:535
  8.0 17.5 %collective-permute-start.1 = (bf16[400,128]{1,0:T(8,128)(2,1)}, bf16[400,128]{1,0:T(8,128)(2,1)S(1)}, u32[]{:S(2)}, u32[]{:S(2)}) collective-permute-start(bf16[400,128]{1,0:T(8,128)(2,1)} %get-tuple-element.14), channel_id=1, source_target_pairs={{0,8},{4,12},{8,16},{12,20},{16,24},{20,28},{24,32},{28,36},{32,40... | collective-permute-start | bytes 307208 | tf_op jit(solution)/shard_map/ppermute | solution.py:535
  9.7 16.6 %collective-permute-start.2 = (bf16[400,128]{1,0:T(8,128)(2,1)}, bf16[400,128]{1,0:T(8,128)(2,1)S(1)}, u32[]{:S(2)}, u32[]{:S(2)}) collective-permute-start(bf16[400,128]{1,0:T(8,128)(2,1)} %get-tuple-element.15), channel_id=1, source_target_pairs={{0,12},{4,16},{8,20},{12,24},{16,28},{20,32},{24,36},{28,40},{32,4... | collective-permute-start | bytes 307208 | tf_op jit(solution)/shard_map/ppermute | solution.py:535
  11.4 0.6 copy-start.6
  12.0 12.9 %copy-start.7 = (bf16[400,128]{1,0:T(8,128)(2,1)S(1)}, bf16[400,128]{1,0:T(8,128)(2,1)}, u32[]{:S(2)}) copy-start(bf16[400,128]{1,0:T(8,128)(2,1)} %copy-done.6) | copy-start | bytes 307204
  12.0 64.4 %all-to-all-start = ((bf16[64,8,16,128]{3,2,1,0:T(8,128)(2,1)}), bf16[64,8,16,128]{3,2,1,0:T(8,128)(2,1)S(1)}, u32[]{:S(2)}, u32[]{:S(2)}) async-start(bf16[64,8,16,128]{3,2,1,0:T(8,128)(2,1)} %bitcast.35), calls=%async_computation | async-start | bytes 4194304 | tf_op jit(solution)/shard_map/all_to_all | solution.py:553
  26.9 12.0 %collective-permute-start.5 = (bf16[1600,128]{1,0:T(8,128)(2,1)}, bf16[1600,128]{1,0:T(8,128)(2,1)S(1)}, u32[]{:S(2)}, u32[]{:S(2)}) collective-permute-start(bf16[1600,128]{1,0:T(8,128)(2,1)} %constant_dynamic-update-slice_fusion.refs_0_), channel_id=1, source_target_pairs={{0,1},{1,2},{2,3},{3,0},{4,5},{5,6},{6,7},{7,4},{8,9},{9,10},{10,1... | collective-permute-start | bytes 1228808 | tf_op jit(solution)/shard_map/ppermute | solution.py:535
  28.1 20.6 %collective-permute-start.4 = (bf16[1600,128]{1,0:T(8,128)(2,1)}, bf16[1600,128]{1,0:T(8,128)(2,1)S(1)}, u32[]{:S(2)}, u32[]{:S(2)}) collective-permute-start(bf16[1600,128]{1,0:T(8,128)(2,1)} %constant_dynamic-update-slice_fusion.refs_0_), channel_id=1, source_target_pairs={{0,2},{1,3},{2,0},{3,1},{4,6},{5,7},{6,4},{7,5},{8,10},{9,11},{10,... | collective-permute-start | bytes 1228808 | tf_op jit(solution)/shard_map/ppermute | solution.py:535
  30.6 18.1 %collective-permute-start.3 = (bf16[1600,128]{1,0:T(8,128)(2,1)}, bf16[1600,128]{1,0:T(8,128)(2,1)S(1)}, u32[]{:S(2)}, u32[]{:S(2)}) collective-permute-start(bf16[1600,128]{1,0:T(8,128)(2,1)} %constant_dynamic-update-slice_fusion.refs_0_), channel_id=1, source_target_pairs={{0,3},{1,0},{2,1},{3,2},{4,7},{5,4},{6,5},{7,6},{8,11},{9,8},{10,9... | collective-permute-start | bytes 1228808 | tf_op jit(solution)/shard_map/ppermute | solution.py:535
  48.7 1.6 %copy-start.2 = (bf16[2,2,4,256,256]{4,3,2,1,0:T(8,128)(2,1)S(1)}, bf16[2,2,4,256,256]{4,3,2,1,0:T(8,128)(2,1)}, u32[]{:S(2)}) copy-start(bf16[2,2,4,256,256]{4,3,2,1,0:T(8,128)(2,1)} %param.9) | copy-start | bytes 6291460
  60.5 2.2 %collective-permute-start.9 = (f32[4,8,128]{2,1,0:T(8,128)S(1)}, f32[4,8,128]{2,1,0:T(8,128)S(1)}, u32[]{:S(2)}, u32[]{:S(2)}) collective-permute-start(f32[4,8,128]{2,1,0:T(8,128)S(1)} %project.1.refs_8_), channel_id=1, source_target_pairs={{0,4},{4,0},{8,12},{12,8},{16,20},{20,16},{24,28},{28,24},{32,36},... | collective-permute-start | bytes 49160 | tf_op jit(solution)/shard_map/ppermute | solution.py:564
  62.7 12.6 %collective-permute-start.11 = (f32[2,4,8,128]{3,2,1,0:T(8,128)S(1)}, f32[2,4,8,128]{3,2,1,0:T(8,128)S(1)}, u32[]{:S(2)}, u32[]{:S(2)}) collective-permute-start(f32[2,4,8,128]{3,2,1,0:T(8,128)S(1)} %pad_maximum_fusion.refs_9_), channel_id=1, source_target_pairs={{0,8},{4,12},{8,16},{12,20},{16,24},{20,28},{24,32},{28,36},{32,40... | collective-permute-start | bytes 98312 | tf_op jit(solution)/shard_map/ppermute | solution.py:535
  64.1 11.2 %collective-permute-start.10 = (f32[2,4,8,128]{3,2,1,0:T(8,128)S(1)}, f32[2,4,8,128]{3,2,1,0:T(8,128)S(1)}, u32[]{:S(2)}, u32[]{:S(2)}) collective-permute-start(f32[2,4,8,128]{3,2,1,0:T(8,128)S(1)} %pad_maximum_fusion.refs_9_), channel_id=1, source_target_pairs={{0,248},{4,252},{8,0},{12,4},{16,8},{20,12},{24,16},{28,20},{32,24... | collective-permute-start | bytes 98312 | tf_op jit(solution)/shard_map/ppermute | solution.py:535
  67.9 5.5 %collective-permute-start.12 = (f32[4,8,128]{2,1,0:T(8,128)S(1)}, f32[4,8,128]{2,1,0:T(8,128)S(1)}, u32[]{:S(2)}, u32[]{:S(2)}) collective-permute-start(f32[4,8,128]{2,1,0:T(8,128)S(1)} %project.1.refs_8_), channel_id=1, source_target_pairs={{0,244},{4,16},{8,252},{12,24},{16,4},{20,32},{24,12},{28,40},{32,... | collective-permute-start | bytes 49160 | tf_op jit(solution)/shard_map/ppermute | solution.py:569
  76.4 1.0 copy-start.4
  78.9 1.3 copy-start.1
  80.2 6.6 %copy-start.8 = (f32[4,64,256]{2,1,0:T(8,128)S(1)}, f32[4,64,256]{2,1,0:T(8,128)}, u32[]{:S(2)}) copy-start(f32[4,64,256]{2,1,0:T(8,128)} %param.10) | copy-start | bytes 786436
  80.2 11.5 %copy-start.9 = (f32[8,8]{1,0:T(8,128)S(1)}, f32[8,8]{1,0:T(8,128)}, u32[]{:S(2)}) copy-start(f32[8,8]{1,0:T(8,128)} %param.14) | copy-start | bytes 772
  80.2 57.7 %all-to-all-start.1 = ((bf16[64,8,16,128]{3,2,1,0:T(8,128)(2,1)}), bf16[64,8,16,128]{3,2,1,0:T(8,128)(2,1)}, u32[]{:S(2)}, u32[]{:S(2)}) async-start(bf16[64,8,16,128]{3,2,1,0:T(8,128)(2,1)} %bitcast.27), calls=%async_computation.1 | async-start | bytes 4194304 | tf_op jit(solution)/shard_map/all_to_all | solution.py:583
  86.8 10.0 %collective-permute-start.8 = (bf16[512,128]{1,0:T(8,128)(2,1)S(1)}, bf16[512,128]{1,0:T(8,128)(2,1)S(1)}, u32[]{:S(2)}, u32[]{:S(2)}) collective-permute-start(bf16[512,128]{1,0:T(8,128)(2,1)S(1)} %bitcast.28), channel_id=1, source_target_pairs={{0,1},{1,2},{2,3},{3,0},{4,5},{5,6},{6,7},{7,4},{8,9},{9,10},{10,1... | collective-permute-start | bytes 393224 | tf_op jit(solution)/shard_map/ppermute | solution.py:535
  88.1 8.7 %collective-permute-start.7 = (bf16[512,128]{1,0:T(8,128)(2,1)S(1)}, bf16[512,128]{1,0:T(8,128)(2,1)S(1)}, u32[]{:S(2)}, u32[]{:S(2)}) collective-permute-start(bf16[512,128]{1,0:T(8,128)(2,1)S(1)} %bitcast.29), channel_id=1, source_target_pairs={{0,2},{1,3},{2,0},{3,1},{4,6},{5,7},{6,4},{7,5},{8,10},{9,11},{10,... | collective-permute-start | bytes 393224 | tf_op jit(solution)/shard_map/ppermute | solution.py:535
  90.6 6.3 %collective-permute-start.6 = (bf16[512,128]{1,0:T(8,128)(2,1)S(1)}, bf16[512,128]{1,0:T(8,128)(2,1)S(1)}, u32[]{:S(2)}, u32[]{:S(2)}) collective-permute-start(bf16[512,128]{1,0:T(8,128)(2,1)S(1)} %bitcast.30), channel_id=1, source_target_pairs={{0,3},{1,0},{2,1},{3,2},{4,7},{5,4},{6,5},{7,6},{8,11},{9,8},{10,9... | collective-permute-start | bytes 393224 | tf_op jit(solution)/shard_map/ppermute | solution.py:535
  92.0 4.9 %copy-start.5 = (bf16[2,256,256]{2,1,0:T(8,128)(2,1)S(1)}, bf16[2,256,256]{2,1,0:T(8,128)(2,1)}, u32[]{:S(2)}) copy-start(bf16[2,256,256]{2,1,0:T(8,128)(2,1)} %constant.45.table_ref) | copy-start | bytes 786436
  96.8 1.6 %copy-start.3 = (bf16[2,2,4,256,256]{4,3,2,1,0:T(8,128)(2,1)S(1)}, bf16[2,2,4,256,256]{4,3,2,1,0:T(8,128)(2,1)}, u32[]{:S(2)}) copy-start(bf16[2,2,4,256,256]{4,3,2,1,0:T(8,128)(2,1)} %param.9) | copy-start | bytes 6291460
  114.5 1.4 copy-start

commit v6 on v5

--- a/solution.py
+++ b/solution.py
@@ -47,10 +47,25 @@
     return lax.dot_general(a, b, dims, precision=precision, preferred_element_type=F32)
 
 
-def along_z_kernel(table_ref, in_ref, *refs):
+def circulant(length):
+    column = lax.broadcasted_iota(jnp.int32, (8, length), 1)
+    near = jnp.minimum(column, length - column)
+    scale = 1.0 / (3.0 * (length // 2) ** 2)
+    sine = jnp.sin(near.astype(F32) * (np.pi / length))
+    sign = jnp.where(near % 2 == 0, 0.5 * scale, -0.5 * scale)
+    row = sign / jnp.where(near == 0, 1.0, sine * sine)
+    row = jnp.where(near == 0, scale * (length * length + 2) / 12.0, row)
+    full = jnp.broadcast_to(row[0:1], (length, length))
+    full = pltpu.roll(full, 0, 1, stride=1, stride_axis=0)
+    high = full.astype(BF16)
+    return high, (full - high.astype(F32)).astype(BF16)
+
+
+def along_z_kernel(in_ref, *refs):
     out_ref, token_ref, wide, result = refs[-4:]
     token_ref[...] = jnp.zeros_like(token_ref)
     length, comps, rows = in_ref.shape[:3]
+    high, low = circulant(length)
     for c in range(comps):
         for z in range(length):
             wide[c, z * PITCH : z * PITCH + rows, :] = in_ref[z, c].astype(F32)
@@ -58,14 +73,14 @@
             left = wide[c, pl.ds(2 * i, length, stride=PITCH), :]
             right = wide[c, pl.ds(2 * i + 1, length, stride=PITCH), :]
             both = jnp.concatenate([left, right], axis=1).astype(BF16)
-            out = dot(table_ref[0], both) + dot(table_ref[1], both)
+            out = dot(high, both) + dot(low, both)
             result[c, pl.ds(2 * i, length, stride=PITCH), :] = out[:, :LANES]
             result[c, pl.ds(2 * i + 1, length, stride=PITCH), :] = out[:, LANES:]
         for z in range(length):
             out_ref[z, c] = result[c, z * PITCH : z * PITCH + rows, :].astype(BF16)
 
 
-def along_z(table, block, after):
+def along_z(block, after):
     length, comps = block.shape[:2]
     return pl.pallas_call(
         along_z_kernel,
@@ -73,7 +88,7 @@
             jax.ShapeDtypeStruct(block.shape, BF16),
             jax.ShapeDtypeStruct((8, LANES), F32),
         ),
-        in_specs=[whole()] * 2 + [whole(pl.ANY)] * len(after),
+        in_specs=[whole()] + [whole(pl.ANY)] * len(after),
         out_specs=(whole(), whole()),
         scratch_shapes=[pltpu.VMEM((comps, (length + 1) * PITCH, LANES), F32)] * 2,
         compiler_params=pltpu.CompilerParams(vmem_limit_bytes=VMEM_LIMIT),
@@ -81,7 +96,7 @@
             flops=4 * length * block.size, bytes_accessed=4 * block.size, transcendentals=0
         ),
         name="along_z",
-    )(table, block, *after)
+    )(block, *after)
 
 
 def select_matrix(facts, length):
@@ -577,7 +592,7 @@
     ).reshape(heaps * nproj * parts, heaps * nproj * parts)
 
     exchanged = [partial, pair, above, below, far]
-    columns, token = along_z(table, columns.reshape(length, comps, 16, LANES), exchanged[2:])
+    columns, token = along_z(columns.reshape(length, comps, 16, LANES), exchanged[2:])
     local = local_part(mix, table, wave, cargo, wells, exchanged, token, nproj)
     columns = columns.reshape(slabs, slab_planes * comps, 16, LANES)
     back = lax.all_to_all(columns, "slab", split_axis=0, concat_axis=0, tiled=True)

time: 142 us -> 141 us (level)
    unnamed x21 -> x19, local copies, waits for them, and re-layouts: 7.49 us -> 6.55 us
where the time goes in v6:
time: 141 us; the launch traced here: 140 us
  waiting for transfers between devices  48.5 us (34%)
  starting transfers between devices  42.2 us (30%)
  Pallas kernels  35.2 us (25%)
  local copies, waits for them, and re-layouts  11.8 us (8%)
  other arithmetic  1.77 us (1%)
    all_to_all x1, waiting for transfers between devices, shards(): lax.all_to_all(columns, 'slab', split_axis=0, concat_axis=0, tiled=True)  22.1 us
    ppermute x11, starting transfers between devices, ahead(): lax.ppermute(block, axis, [(i, (i + distance) % size) for i in range(size)])  21.3 us
    ppermute x11, waiting for transfers between devices, ahead(): lax.ppermute(block, axis, [(i, (i + distance) % size) for i in range(size)])  18.9 us
    pallas_call x1, Pallas kernels, local_part(): pl.pallas_call(functools.partial(local_kernel, heaps=heaps, reach=reach,...  16 us
    all_to_all x1, starting transfers between devices, shards(): lax.all_to_all(send, 'slab', split_axis=0, concat_axis=0, tiled=True)  12.9 us
    pallas_call x1, Pallas kernels, project(): pl.pallas_call(functools.partial(project_kernel, heaps=heaps, reach=reach...  10.2 us
    all_to_all x1, starting transfers between devices, shards(): lax.all_to_all(columns, 'slab', split_axis=0, concat_axis=0, tiled=True)  6.57 us
    unnamed x19, local copies, waits for them, and re-layouts  6.55 us
  transfers between devices with their start and end apart: 15, of which 7 were waited for; matrix products, arithmetic and copies ran while one was open for 5% of the time, Pallas kernels for 19%

profile of v6, /device:TPU:1, one launch (start us, length us, event | category | flops | bytes accessed | tf_op | source)
XLA Modules:
  0.0 140.4 jit_solution(13501148353776485155)
XLA Ops:
  0.7 4.3 %frame.1 = (bf16[2,16,2,4,2,16,128]{6,5,4,3,2,1,0:T(8,128)(2,1)}, bf16[1600,128]{1,0:T(8,128)(2,1)}, bf16[400,128]{1,0:T(8,128)(2,1)}, bf16[400,128]{1,0:T(8,128)(2,1)}, bf16[400,128]{1,0:T(8,128)(2,1)}) custom-call(s32[3,32]{1,0:T(4,128)} %box_ref.1, s32[1]{0:T(128)S(6)} %copy.23.count_ref, bf16[32,8,1728]{2,1,0:T(8,128)(2,1)} %projectors_ref.1, ...), custom_call_target="tpu_custom_call" | custom-call | flops 1000000000 | bytes 9000000 | tf_op jit(solution)/shard_map/frame/pallas_call | solution.py:450
  4.9 3.1 %collective-permute-start = (bf16[400,128]{1,0:T(8,128)(2,1)}, bf16[400,128]{1,0:T(8,128)(2,1)S(1)}, u32[]{:S(2)}, u32[]{:S(2)}) collective-permute-start(bf16[400,128]{1,0:T(8,128)(2,1)} %get-tuple-element.13), channel_id=1, source_target_pairs={{0,4},{4,8},{8,12},{12,16},{16,20},{20,24},{24,28},{28,32},{32,36}... | collective-permute-start | bytes 307208 | tf_op jit(solution)/shard_map/ppermute | solution.py:550
  8.0 1.6 %collective-permute-start.1 = (bf16[400,128]{1,0:T(8,128)(2,1)}, bf16[400,128]{1,0:T(8,128)(2,1)S(1)}, u32[]{:S(2)}, u32[]{:S(2)}) collective-permute-start(bf16[400,128]{1,0:T(8,128)(2,1)} %get-tuple-element.14), channel_id=1, source_target_pairs={{0,8},{4,12},{8,16},{12,20},{16,24},{20,28},{24,32},{28,36},{32,40... | collective-permute-start | bytes 307208 | tf_op jit(solution)/shard_map/ppermute | solution.py:550
  9.7 1.7 %collective-permute-start.2 = (bf16[400,128]{1,0:T(8,128)(2,1)}, bf16[400,128]{1,0:T(8,128)(2,1)S(1)}, u32[]{:S(2)}, u32[]{:S(2)}) collective-permute-start(bf16[400,128]{1,0:T(8,128)(2,1)} %get-tuple-element.15), channel_id=1, source_target_pairs={{0,12},{4,16},{8,20},{12,24},{16,28},{20,32},{24,36},{28,40},{32,4... | collective-permute-start | bytes 307208 | tf_op jit(solution)/shard_map/ppermute | solution.py:550
  11.4 0.0 collective-permute-done.refs_1_
  11.4 0.0 copy-start.5
  11.4 0.6 copy-done.5
  12.0 0.0 copy-start.6
  12.0 12.9 %all-to-all-start = ((bf16[64,8,16,128]{3,2,1,0:T(8,128)(2,1)}), bf16[64,8,16,128]{3,2,1,0:T(8,128)(2,1)S(1)}, u32[]{:S(2)}, u32[]{:S(2)}) async-start(bf16[64,8,16,128]{3,2,1,0:T(8,128)(2,1)} %bitcast.35), calls=%async_computation | async-start | bytes 4194304 | tf_op jit(solution)/shard_map/all_to_all | solution.py:568
  24.9 0.0 copy-done.6
  24.9 0.6 constant_dynamic-update-slice_fusion.2
  25.6 0.0 collective-permute-done.1
  25.6 0.6 constant_dynamic-update-slice_fusion.1
  26.2 0.0 collective-permute-done.2
  26.2 0.6 constant_dynamic-update-slice_fusion.refs_0_
  26.9 1.2 collective-permute-start.5
  28.1 2.5 %collective-permute-start.4 = (bf16[1600,128]{1,0:T(8,128)(2,1)}, bf16[1600,128]{1,0:T(8,128)(2,1)S(1)}, u32[]{:S(2)}, u32[]{:S(2)}) collective-permute-start(bf16[1600,128]{1,0:T(8,128)(2,1)} %constant_dynamic-update-slice_fusion.refs_0_), channel_id=1, source_target_pairs={{0,2},{1,3},{2,0},{3,1},{4,6},{5,7},{6,4},{7,5},{8,10},{9,11},{10,... | collective-permute-start | bytes 1228808 | tf_op jit(solution)/shard_map/ppermute | solution.py:550
  30.5 1.2 collective-permute-start.3
  31.7 7.2 %collective-permute-done.5.refs_3_ = bf16[1600,128]{1,0:T(8,128)(2,1)S(1)} collective-permute-done((bf16[1600,128]{1,0:T(8,128)(2,1)}, bf16[1600,128]{1,0:T(8,128)(2,1)S(1)}, u32[]{:S(2)}, u32[]{:S(2)}) %collective-permute-start.5) | collective-permute-done | bytes 409632 | tf_op jit(solution)/shard_map/ppermute | solution.py:550
  38.9 9.8 %collective-permute-done.4.refs_2_ = bf16[1600,128]{1,0:T(8,128)(2,1)S(1)} collective-permute-done((bf16[1600,128]{1,0:T(8,128)(2,1)}, bf16[1600,128]{1,0:T(8,128)(2,1)S(1)}, u32[]{:S(2)}, u32[]{:S(2)}) %collective-permute-start.4) | collective-permute-done | bytes 409632 | tf_op jit(solution)/shard_map/ppermute | solution.py:550
  48.7 0.0 collective-permute-done.3.refs_1_
  48.7 0.0 copy-start.2
  48.7 1.6 %copy-done.2 = bf16[2,2,4,256,256]{4,3,2,1,0:T(8,128)(2,1)S(1)} copy-done((bf16[2,2,4,256,256]{4,3,2,1,0:T(8,128)(2,1)S(1)}, bf16[2,2,4,256,256]{4,3,2,1,0:T(8,128)(2,1)}, u32[]{:S(2)}) %copy-start.2) | copy-done | bytes 2097176
  50.3 10.2 %project.1.refs_8_ = f32[4,8,128]{2,1,0:T(8,128)S(1)} custom-call(bf16[16,256,256]{2,1,0:T(8,128)(2,1)S(1)} %bitcast.33, bf16[1600,128]{1,0:T(8,128)(2,1)} %constant_dynamic-update-slice_fusion.refs_0_, bf16[1600,128]{1,0:T(8,128)(2,1)S(1)} %collective-permute-done.3.refs_1_, bf16[1600,128]{1,0:T(8,128)(2,1)S(1)} %collective-permute-done.4.refs_2_, ...), custom_call_target="tpu_custom_call" | custom-call | flops 32999999488 | bytes 5000000 | tf_op jit(solution)/shard_map/project/pallas_call | solution.py:202
  60.4 1.4 collective-permute-start.9
  61.8 0.8 collective-permute-done.9
  62.7 1.4 %collective-permute-start.11 = (f32[2,4,8,128]{3,2,1,0:T(8,128)S(1)}, f32[2,4,8,128]{3,2,1,0:T(8,128)S(1)}, u32[]{:S(2)}, u32[]{:S(2)}) collective-permute-start(f32[2,4,8,128]{3,2,1,0:T(8,128)S(1)} %pad_maximum_fusion.refs_9_), channel_id=1, source_target_pairs={{0,8},{4,12},{8,16},{12,20},{16,24},{20,28},{24,32},{28,36},{32,40... | collective-permute-start | bytes 98312 | tf_op jit(solution)/shard_map/ppermute | solution.py:550
  64.1 3.7 %collective-permute-start.10 = (f32[2,4,8,128]{3,2,1,0:T(8,128)S(1)}, f32[2,4,8,128]{3,2,1,0:T(8,128)S(1)}, u32[]{:S(2)}, u32[]{:S(2)}) collective-permute-start(f32[2,4,8,128]{3,2,1,0:T(8,128)S(1)} %pad_maximum_fusion.refs_9_), channel_id=1, source_target_pairs={{0,248},{4,252},{8,0},{12,4},{16,8},{20,12},{24,16},{28,20},{32,24... | collective-permute-start | bytes 98312 | tf_op jit(solution)/shard_map/ppermute | solution.py:550
  67.8 0.0 collective-permute-start.12
  67.8 5.6 %collective-permute-done.12.refs_2_.refs_12_ = f32[4,8,128]{2,1,0:T(8,128)S(1)} collective-permute-done((f32[4,8,128]{2,1,0:T(8,128)S(1)}, f32[4,8,128]{2,1,0:T(8,128)S(1)}, u32[]{:S(2)}, u32[]{:S(2)}) %collective-permute-start.12) | collective-permute-done | bytes 16416 | tf_op jit(solution)/shard_map/ppermute | solution.py:584
  73.4 1.9 %collective-permute-done.11.refs_1_.refs_11_ = f32[2,4,8,128]{3,2,1,0:T(8,128)S(1)} collective-permute-done((f32[2,4,8,128]{3,2,1,0:T(8,128)S(1)}, f32[2,4,8,128]{3,2,1,0:T(8,128)S(1)}, u32[]{:S(2)}, u32[]{:S(2)}) %collective-permute-start.11) | collective-permute-done | bytes 32800 | tf_op jit(solution)/shard_map/ppermute | solution.py:550
  75.4 0.0 collective-permute-done.10.refs_0_.refs_10_
  75.4 1.0 all-to-all-done
  76.4 1.6 %along_z.1 = (bf16[256,2,16,128]{3,2,1,0:T(8,128)(2,1)S(1)}, f32[8,128]{1,0:T(8,128)S(1)}) custom-call(bf16[256,2,16,128]{3,2,1,0:T(8,128)(2,1)S(1)} %bitcast.26, f32[2,4,8,128]{3,2,1,0:T(8,128)S(1)} %collective-permute-done.10.refs_0_.refs_10_, f32[2,4,8,128]{3,2,1,0:T(8,128)S(1)} %collective-permute-done.11.refs_1_.refs_11_, ...), custom_call_target="tpu_custom_call" | custom-call | flops 1073741824 | bytes 4194304 | tf_op jit(solution)/shard_map/along_z/pallas_call | solution.py:85
  78.0 0.0 copy-start.1
  78.0 1.3 copy-done.1
  79.3 0.0 copy-start.7
  79.3 0.0 copy-start.8
  79.3 6.6 %all-to-all-start.1 = ((bf16[64,8,16,128]{3,2,1,0:T(8,128)(2,1)}), bf16[64,8,16,128]{3,2,1,0:T(8,128)(2,1)}, u32[]{:S(2)}, u32[]{:S(2)}) async-start(bf16[64,8,16,128]{3,2,1,0:T(8,128)(2,1)} %bitcast.27), calls=%async_computation.1 | async-start | bytes 4194304 | tf_op jit(solution)/shard_map/all_to_all | solution.py:598
  85.9 0.0 copy-done.7
  85.9 1.3 collective-permute-start.8
  87.2 2.4 %collective-permute-start.7 = (bf16[512,128]{1,0:T(8,128)(2,1)S(1)}, bf16[512,128]{1,0:T(8,128)(2,1)S(1)}, u32[]{:S(2)}, u32[]{:S(2)}) collective-permute-start(bf16[512,128]{1,0:T(8,128)(2,1)S(1)} %bitcast.29), channel_id=1, source_target_pairs={{0,2},{1,3},{2,0},{3,1},{4,6},{5,7},{6,4},{7,5},{8,10},{9,11},{10,... | collective-permute-start | bytes 393224 | tf_op jit(solution)/shard_map/ppermute | solution.py:550
  89.6 1.2 collective-permute-start.6
  90.8 0.0 copy-done.8
  90.8 0.1 copy.14
  90.9 0.1 copy.15
  91.0 0.1 broadcast_multiply_fusion
  91.0 0.0 copy-start.4
  91.0 1.7 %multiply_bitcast_fusion = f32[4,8,4,4,8,4]{5,4,3,2,1,0:T(8,128)} fusion(f32[8,8]{0,1:T(8,128)S(1)} %copy.15, f32[4,4,4,4]{1,3,0,2:T(4,128)S(1)} %broadcast_multiply_fusion), kind=kLoop, calls=%fused_computation | loop fusion | flops 16384 | bytes 66816 | tf_op jit(solution)/shard_map/gh,pq,bc->gqbhpc/transpose | solution.py:589
  92.7 3.2 %reshape.27.mix_ref = f32[128,128]{1,0:T(8,128)S(1)} reshape(f32[4,8,4,4,8,4]{5,4,3,2,1,0:T(8,128)} %multiply_bitcast_fusion) | data formatting | bytes 131072 | tf_op jit(solution)/shard_map/reshape | solution.py:592
  95.9 0.0 collective-permute-done.8.refs_7_
  95.9 0.0 collective-permute-done.7.refs_6_
  95.9 0.0 collective-permute-done.6.refs_5_
  95.9 0.0 copy-done.4
  95.9 0.0 copy-start.3
  95.9 1.6 %copy-done.3 = bf16[2,2,4,256,256]{4,3,2,1,0:T(8,128)(2,1)S(1)} copy-done((bf16[2,2,4,256,256]{4,3,2,1,0:T(8,128)(2,1)S(1)}, bf16[2,2,4,256,256]{4,3,2,1,0:T(8,128)(2,1)}, u32[]{:S(2)}) %copy-start.3) | copy-done | bytes 2097176
  97.5 16.0 %local.1.local_ref = bf16[16,256,256]{2,1,0:T(8,128)(2,1)S(1)} custom-call(f32[128,128]{1,0:T(8,128)S(1)} %reshape.27.mix_ref, bf16[2,256,256]{2,1,0:T(8,128)(2,1)S(1)} %copy-done.4, bf16[16,256,256]{2,1,0:T(8,128)(2,1)S(1)} %bitcast.34, bf16[1600,128]{1,0:T(8,128)(2,1)} %constant_dynamic-update-slice_fusion.refs_0_, ...), custom_call_target="tpu_custom_call" | custom-call | flops 10000000000 | bytes 10000000 | tf_op jit(solution)/shard_map/local/pallas_call | solution.py:314
  113.6 0.0 copy-start
  113.6 1.3 copy-done
  114.9 22.1 %all-to-all-done.1 = bf16[64,8,16,128]{3,2,1,0:T(8,128)(2,1)} async-done(((bf16[64,8,16,128]{3,2,1,0:T(8,128)(2,1)}), bf16[64,8,16,128]{3,2,1,0:T(8,128)(2,1)}, u32[]{:S(2)}, u32[]{:S(2)}) %all-to-all-start.1) | async-done | bytes 2097184 | tf_op jit(solution)/shard_map/all_to_all | solution.py:598
  137.0 3.2 %join.1 = bf16[16,256,256]{2,1,0:T(8,128)(2,1)} custom-call(bf16[16,256,256]{2,1,0:T(8,128)(2,1)} %copy-done, bf16[2,16,2,4,2,16,128]{6,5,4,3,2,1,0:T(8,128)(2,1)} %bitcast.11.arrived_ref), custom_call_target="tpu_custom_call" | custom-call | flops 2097152 | bytes 6291456 | tf_op jit(solution)/shard_map/join/pallas_call | solution.py:527
  (6 shorter events, 0.0 us)
Async XLA Ops:
  4.9 6.5 %collective-permute-start = (bf16[400,128]{1,0:T(8,128)(2,1)}, bf16[400,128]{1,0:T(8,128)(2,1)S(1)}, u32[]{:S(2)}, u32[]{:S(2)}) collective-permute-start(bf16[400,128]{1,0:T(8,128)(2,1)} %get-tuple-element.13), channel_id=1, source_target_pairs={{0,4},{4,8},{8,12},{12,16},{16,20},{20,24},{24,28},{28,32},{32,36}... | collective-permute-start | bytes 307208 | tf_op jit(solution)/shard_map/ppermute | solution.py:550
  8.0 17.6 %collective-permute-start.1 = (bf16[400,128]{1,0:T(8,128)(2,1)}, bf16[400,128]{1,0:T(8,128)(2,1)S(1)}, u32[]{:S(2)}, u32[]{:S(2)}) collective-permute-start(bf16[400,128]{1,0:T(8,128)(2,1)} %get-tuple-element.14), channel_id=1, source_target_pairs={{0,8},{4,12},{8,16},{12,20},{16,24},{20,28},{24,32},{28,36},{32,40... | collective-permute-start | bytes 307208 | tf_op jit(solution)/shard_map/ppermute | solution.py:550
  9.7 16.6 %collective-permute-start.2 = (bf16[400,128]{1,0:T(8,128)(2,1)}, bf16[400,128]{1,0:T(8,128)(2,1)S(1)}, u32[]{:S(2)}, u32[]{:S(2)}) collective-permute-start(bf16[400,128]{1,0:T(8,128)(2,1)} %get-tuple-element.15), channel_id=1, source_target_pairs={{0,12},{4,16},{8,20},{12,24},{16,28},{20,32},{24,36},{28,40},{32,4... | collective-permute-start | bytes 307208 | tf_op jit(solution)/shard_map/ppermute | solution.py:550
  11.4 0.6 copy-start.5
  12.0 12.9 %copy-start.6 = (bf16[400,128]{1,0:T(8,128)(2,1)S(1)}, bf16[400,128]{1,0:T(8,128)(2,1)}, u32[]{:S(2)}) copy-start(bf16[400,128]{1,0:T(8,128)(2,1)} %copy-done.5) | copy-start | bytes 307204
  12.0 64.4 %all-to-all-start = ((bf16[64,8,16,128]{3,2,1,0:T(8,128)(2,1)}), bf16[64,8,16,128]{3,2,1,0:T(8,128)(2,1)S(1)}, u32[]{:S(2)}, u32[]{:S(2)}) async-start(bf16[64,8,16,128]{3,2,1,0:T(8,128)(2,1)} %bitcast.35), calls=%async_computation | async-start | bytes 4194304 | tf_op jit(solution)/shard_map/all_to_all | solution.py:568
  26.9 12.0 %collective-permute-start.5 = (bf16[1600,128]{1,0:T(8,128)(2,1)}, bf16[1600,128]{1,0:T(8,128)(2,1)S(1)}, u32[]{:S(2)}, u32[]{:S(2)}) collective-permute-start(bf16[1600,128]{1,0:T(8,128)(2,1)} %constant_dynamic-update-slice_fusion.refs_0_), channel_id=1, source_target_pairs={{0,1},{1,2},{2,3},{3,0},{4,5},{5,6},{6,7},{7,4},{8,9},{9,10},{10,1... | collective-permute-start | bytes 1228808 | tf_op jit(solution)/shard_map/ppermute | solution.py:550
  28.1 20.6 %collective-permute-start.4 = (bf16[1600,128]{1,0:T(8,128)(2,1)}, bf16[1600,128]{1,0:T(8,128)(2,1)S(1)}, u32[]{:S(2)}, u32[]{:S(2)}) collective-permute-start(bf16[1600,128]{1,0:T(8,128)(2,1)} %constant_dynamic-update-slice_fusion.refs_0_), channel_id=1, source_target_pairs={{0,2},{1,3},{2,0},{3,1},{4,6},{5,7},{6,4},{7,5},{8,10},{9,11},{10,... | collective-permute-start | bytes 1228808 | tf_op jit(solution)/shard_map/ppermute | solution.py:550
  30.5 18.1 %collective-permute-start.3 = (bf16[1600,128]{1,0:T(8,128)(2,1)}, bf16[1600,128]{1,0:T(8,128)(2,1)S(1)}, u32[]{:S(2)}, u32[]{:S(2)}) collective-permute-start(bf16[1600,128]{1,0:T(8,128)(2,1)} %constant_dynamic-update-slice_fusion.refs_0_), channel_id=1, source_target_pairs={{0,3},{1,0},{2,1},{3,2},{4,7},{5,4},{6,5},{7,6},{8,11},{9,8},{10,9... | collective-permute-start | bytes 1228808 | tf_op jit(solution)/shard_map/ppermute | solution.py:550
  48.7 1.6 %copy-start.2 = (bf16[2,2,4,256,256]{4,3,2,1,0:T(8,128)(2,1)S(1)}, bf16[2,2,4,256,256]{4,3,2,1,0:T(8,128)(2,1)}, u32[]{:S(2)}) copy-start(bf16[2,2,4,256,256]{4,3,2,1,0:T(8,128)(2,1)} %param.9) | copy-start | bytes 6291460
  60.4 2.2 %collective-permute-start.9 = (f32[4,8,128]{2,1,0:T(8,128)S(1)}, f32[4,8,128]{2,1,0:T(8,128)S(1)}, u32[]{:S(2)}, u32[]{:S(2)}) collective-permute-start(f32[4,8,128]{2,1,0:T(8,128)S(1)} %project.1.refs_8_), channel_id=1, source_target_pairs={{0,4},{4,0},{8,12},{12,8},{16,20},{20,16},{24,28},{28,24},{32,36},... | collective-permute-start | bytes 49160 | tf_op jit(solution)/shard_map/ppermute | solution.py:579
  62.7 12.7 %collective-permute-start.11 = (f32[2,4,8,128]{3,2,1,0:T(8,128)S(1)}, f32[2,4,8,128]{3,2,1,0:T(8,128)S(1)}, u32[]{:S(2)}, u32[]{:S(2)}) collective-permute-start(f32[2,4,8,128]{3,2,1,0:T(8,128)S(1)} %pad_maximum_fusion.refs_9_), channel_id=1, source_target_pairs={{0,8},{4,12},{8,16},{12,20},{16,24},{20,28},{24,32},{28,36},{32,40... | collective-permute-start | bytes 98312 | tf_op jit(solution)/shard_map/ppermute | solution.py:550
  64.1 11.2 %collective-permute-start.10 = (f32[2,4,8,128]{3,2,1,0:T(8,128)S(1)}, f32[2,4,8,128]{3,2,1,0:T(8,128)S(1)}, u32[]{:S(2)}, u32[]{:S(2)}) collective-permute-start(f32[2,4,8,128]{3,2,1,0:T(8,128)S(1)} %pad_maximum_fusion.refs_9_), channel_id=1, source_target_pairs={{0,248},{4,252},{8,0},{12,4},{16,8},{20,12},{24,16},{28,20},{32,24... | collective-permute-start | bytes 98312 | tf_op jit(solution)/shard_map/ppermute | solution.py:550
  67.8 5.6 %collective-permute-start.12 = (f32[4,8,128]{2,1,0:T(8,128)S(1)}, f32[4,8,128]{2,1,0:T(8,128)S(1)}, u32[]{:S(2)}, u32[]{:S(2)}) collective-permute-start(f32[4,8,128]{2,1,0:T(8,128)S(1)} %project.1.refs_8_), channel_id=1, source_target_pairs={{0,244},{4,16},{8,252},{12,24},{16,4},{20,32},{24,12},{28,40},{32,... | collective-permute-start | bytes 49160 | tf_op jit(solution)/shard_map/ppermute | solution.py:584
  78.0 1.3 copy-start.1
  79.3 6.6 %copy-start.7 = (f32[4,64,256]{2,1,0:T(8,128)S(1)}, f32[4,64,256]{2,1,0:T(8,128)}, u32[]{:S(2)}) copy-start(f32[4,64,256]{2,1,0:T(8,128)} %param.10) | copy-start | bytes 786436
  79.3 11.5 %copy-start.8 = (f32[8,8]{1,0:T(8,128)S(1)}, f32[8,8]{1,0:T(8,128)}, u32[]{:S(2)}) copy-start(f32[8,8]{1,0:T(8,128)} %param.14) | copy-start | bytes 772
  79.3 57.7 %all-to-all-start.1 = ((bf16[64,8,16,128]{3,2,1,0:T(8,128)(2,1)}), bf16[64,8,16,128]{3,2,1,0:T(8,128)(2,1)}, u32[]{:S(2)}, u32[]{:S(2)}) async-start(bf16[64,8,16,128]{3,2,1,0:T(8,128)(2,1)} %bitcast.27), calls=%async_computation.1 | async-start | bytes 4194304 | tf_op jit(solution)/shard_map/all_to_all | solution.py:598
  85.9 10.0 %collective-permute-start.8 = (bf16[512,128]{1,0:T(8,128)(2,1)S(1)}, bf16[512,128]{1,0:T(8,128)(2,1)S(1)}, u32[]{:S(2)}, u32[]{:S(2)}) collective-permute-start(bf16[512,128]{1,0:T(8,128)(2,1)S(1)} %bitcast.28), channel_id=1, source_target_pairs={{0,1},{1,2},{2,3},{3,0},{4,5},{5,6},{6,7},{7,4},{8,9},{9,10},{10,1... | collective-permute-start | bytes 393224 | tf_op jit(solution)/shard_map/ppermute | solution.py:550
  87.2 8.7 %collective-permute-start.7 = (bf16[512,128]{1,0:T(8,128)(2,1)S(1)}, bf16[512,128]{1,0:T(8,128)(2,1)S(1)}, u32[]{:S(2)}, u32[]{:S(2)}) collective-permute-start(bf16[512,128]{1,0:T(8,128)(2,1)S(1)} %bitcast.29), channel_id=1, source_target_pairs={{0,2},{1,3},{2,0},{3,1},{4,6},{5,7},{6,4},{7,5},{8,10},{9,11},{10,... | collective-permute-start | bytes 393224 | tf_op jit(solution)/shard_map/ppermute | solution.py:550
  89.6 6.3 %collective-permute-start.6 = (bf16[512,128]{1,0:T(8,128)(2,1)S(1)}, bf16[512,128]{1,0:T(8,128)(2,1)S(1)}, u32[]{:S(2)}, u32[]{:S(2)}) collective-permute-start(bf16[512,128]{1,0:T(8,128)(2,1)S(1)} %bitcast.30), channel_id=1, source_target_pairs={{0,3},{1,0},{2,1},{3,2},{4,7},{5,4},{6,5},{7,6},{8,11},{9,8},{10,9... | collective-permute-start | bytes 393224 | tf_op jit(solution)/shard_map/ppermute | solution.py:550
  91.0 4.9 %copy-start.4 = (bf16[2,256,256]{2,1,0:T(8,128)(2,1)S(1)}, bf16[2,256,256]{2,1,0:T(8,128)(2,1)}, u32[]{:S(2)}) copy-start(bf16[2,256,256]{2,1,0:T(8,128)(2,1)} %constant.45.table_ref) | copy-start | bytes 786436
  95.9 1.6 %copy-start.3 = (bf16[2,2,4,256,256]{4,3,2,1,0:T(8,128)(2,1)S(1)}, bf16[2,2,4,256,256]{4,3,2,1,0:T(8,128)(2,1)}, u32[]{:S(2)}) copy-start(bf16[2,2,4,256,256]{4,3,2,1,0:T(8,128)(2,1)} %param.9) | copy-start | bytes 6291460
  113.6 1.4 copy-start
